TPU v7x, 32 devices: a whole 2x2x4 slice. The times are simulated.
32 devices in a mesh: dp: 8 (over y, x, core), tensor: 4 (over z).
Axes of the slice: x: 2, y: 2, z: 4, core: 2. Of those that a mesh axis runs over, the one named last changes fastest.
Arguments:
- gate_act: bfloat16 [256, 14336], P('dp', 'tensor'), may hold values from -6 to 6
- up_act: bfloat16 [256, 14336], P('dp', 'tensor'), may hold values from -6 to 6
- cotangent: bfloat16 [256, 4096], P(('dp', 'tensor')), may hold values from -6 to 6
- down_blocks: bfloat16 [112, 2048, 128], P('tensor'), may hold values from -0.125 to 0.125
- down_index: int32 [112, 16], P('tensor'), may hold values from 0 to 31, as said below
Outputs:
- down_grad: float32 [2048, 112, 128], P('dp', 'tensor')
- gate_grad: bfloat16 [256, 14336], P('dp', 'tensor')
- up_grad: bfloat16 [256, 14336], P('dp', 'tensor')
Inputs may be any that keep to these rules, and one draw needn't show every extreme that they name: `down_index`: each row names 16 distinct feature blocks.
All inputs are finite; a program needn't handle non-finite values.
Results may differ from a plain program's by a relative error of at most 0.0029.
Values may be sent and summed in bfloat16 or wider, within the bound.
No kernel may reach another device: no remote copies, remote signals or barrier semaphores. Data moves between devices by JAX's collectives and lax.ppermute only.
A program may use at most 128 MiB of HBM per device.

v0:
```python
import jax
import jax.numpy as jnp
from jax import lax
from jax.sharding import PartitionSpec as P


def local(gate_act, up_act, cotangent, down_blocks, down_index):
    gathered = lax.all_gather(cotangent, "tensor", axis=0, tiled=True)
    row_count = gathered.shape[0]
    local_blocks, kept_span, block_size = down_blocks.shape
    feature_count = gathered.shape[1] // block_size
    feature_view = gathered.reshape(row_count, feature_count, block_size)
    gate_value = gate_act.astype(jnp.float32).reshape(row_count, local_blocks, block_size)
    up_value = up_act.astype(jnp.float32).reshape(row_count, local_blocks, block_size)
    sigmoid_gate = jax.nn.sigmoid(gate_value)
    hidden = (gate_value * sigmoid_gate * up_value).astype(jnp.bfloat16)
    hidden_blocks = hidden.transpose(1, 0, 2)
    replicas = lax.axis_size("dp")

    def select(index_row):
        return jnp.take(feature_view, index_row, axis=1).reshape(row_count, kept_span)

    def one_grad(inputs):
        index_row, weight_block = inputs
        return jnp.dot(select(index_row), weight_block, preferred_element_type=jnp.float32)

    hidden_grad = lax.map(one_grad, (down_index, down_blocks)).transpose(1, 0, 2)
    gate_out = (
        (hidden_grad * up_value * sigmoid_gate * (1.0 + gate_value * (1.0 - sigmoid_gate)))
        .astype(jnp.bfloat16)
        .reshape(row_count, local_blocks * block_size)
    )
    up_out = (
        (hidden_grad * gate_value * sigmoid_gate)
        .astype(jnp.bfloat16)
        .reshape(row_count, local_blocks * block_size)
    )

    def one_term(inputs):
        index_row, hidden_block = inputs
        part_rows = select(index_row)
        return jnp.dot(part_rows.T, hidden_block, preferred_element_type=jnp.float32)

    summed = lax.psum_scatter(
        lax.map(one_term, (down_index, hidden_blocks)).transpose(1, 0, 2),
        "dp",
        scatter_dimension=0,
        tiled=True,
    )
    down_grad = summed / replicas
    return (down_grad, gate_out, up_out)


def solution(mesh):
    in_specs = (
        P("dp", "tensor"),
        P("dp", "tensor"),
        P(("dp", "tensor"), None),
        P("tensor", None, None),
        P("tensor", None),
    )
    out_specs = (P("dp", "tensor", None), P("dp", "tensor"), P("dp", "tensor"))
    return jax.shard_map(local, mesh=mesh, in_specs=in_specs, out_specs=out_specs, check_vma=False)
```

profile of v0, /device:TPU:0, one launch (start us, length us, event | category | flops | bytes accessed | tf_op | source)
XLA Modules:
  0.0 332.9 jit_solution(8032950739998437527)
XLA Ops:
  7.2 15.8 %all_gather.3 = bf16[32,4096]{1,0:T(8,128)(2,1)S(1)} all-gather(bf16[8,4096]{1,0:T(8,128)(2,1)} %param.13), channel_id=1, replica_groups=mesh['dp'=8,'tensor'=4] {'tensor'}, dimensions={0}, use_global_device_ids=true | all-gather | bytes 327680 | tf_op jit(solution)/shard_map/all_gather | solution.py:8
  23.9 56.9 %while.21 = (s32[]{:T(128)}, f32[28,32,128]{2,0,1:T(8,128)S(1)}, s32[28,16]{1,0:T(8,128)S(1)}, bf16[32,32,128]{2,0,1:T(8,128)(2,1)S(1)}, bf16[28,2048,128]{2,1,0:T(8,128)(2,1)}, /*index=5*/s32[]{:T(128)}, s32[]{:T(128)}) while((s32[]{:T(128)}, f32[28,32,128]{2,0,1:T(8,128)S(1)}, s32[28,16]{1,0:T(8,128)S(1)}, ...), condition=%wide.region_4.6_spmd, body=%wide.region_3.5_spmd.sunk | while | flops 16843872 | bytes 971637 | solution.py:27
  24.5 1.3 fusion.31
  26.5 1.3 fusion.31
  28.6 1.3 fusion.31
  30.6 1.3 fusion.31
  32.6 1.3 fusion.31
  34.7 1.3 fusion.31
  36.7 1.3 fusion.31
  38.7 1.3 fusion.31
  40.8 1.3 fusion.31
  42.8 1.3 fusion.31
  44.8 1.3 fusion.31
  46.9 1.3 fusion.31
  48.9 1.3 fusion.31
  50.9 1.3 fusion.31
  53.0 1.3 fusion.31
  55.0 1.3 fusion.31
  57.0 1.3 fusion.31
  59.1 1.3 fusion.31
  61.1 1.3 fusion.31
  63.1 1.3 fusion.31
  65.2 1.3 fusion.31
  67.2 1.3 fusion.31
  69.2 1.3 fusion.31
  71.3 1.3 fusion.31
  73.3 1.3 fusion.31
  75.3 1.3 fusion.31
  77.4 1.3 fusion.31
  79.4 1.3 fusion.31
  80.8 1.1 reshape.46
  81.9 1.1 reshape.48
  83.4 57.9 %while.20 = (s32[]{:T(128)}, f32[28,2048,128]{2,1,0:T(8,128)}, s32[28,16]{1,0:T(8,128)S(1)}, bf16[32,32,128]{2,0,1:T(8,128)(2,1)S(1)}, bf16[28,32,128]{2,1,0:T(8,128)(2,1)S(1)}, /*index=5*/s32[]{:T(128)}) while((s32[]{:T(128)}, f32[28,2048,128]{2,1,0:T(8,128)}, s32[28,16]{1,0:T(8,128)S(1)}, bf16[32,32,128]{2,0,1:T(8,128)(2,1)S(1)}, ...), condition=%wide.region_1.3_spmd, body=%wide.region_0.2_spmd.sunk | while | flops 16843872 | bytes 1455961 | solution.py:45
  84.1 1.4 fusion.28
  86.1 1.5 fusion.28
  88.2 1.5 fusion.28
  90.3 1.5 fusion.28
  92.3 1.4 fusion.28
  94.4 1.5 fusion.28
  96.4 1.5 fusion.28
  98.5 1.5 fusion.28
  100.6 1.5 fusion.28
  102.7 1.4 fusion.28
  104.7 1.4 fusion.28
  106.8 1.5 fusion.28
  108.8 1.5 fusion.28
  111.0 1.4 fusion.28
  113.0 1.5 fusion.28
  115.1 1.4 fusion.28
  117.1 1.4 fusion.28
  119.2 1.5 fusion.28
  121.3 1.5 fusion.28
  123.3 1.5 fusion.28
  125.4 1.4 fusion.28
  127.4 1.5 fusion.28
  129.5 1.5 fusion.28
  131.6 1.5 fusion.28
  133.7 1.5 fusion.28
  135.8 1.4 fusion.28
  137.8 1.4 fusion.28
  139.8 1.5 fusion.28
  141.3 0.9 copy_bitcast_fusion.1
  142.2 179.6 %reduce-scatter.2.cloned.1.call-done = f32[256,28,128]{2,0,1:T(8,128)} async-done(((f32[2048,28,128]{2,0,1:T(8,128)}), f32[256,28,128]{2,0,1:T(8,128)}) %reduce-scatter.2.cloned.1.call-update) | async-done | bytes 3670032 | tf_op jit(solution)/shard_map/reduce_scatter | solution.py:44
  321.8 4.3 %broadcast_multiply_fusion = f32[256,28,128]{2,0,1:T(8,128)} fusion(f32[256,28,128]{2,0,1:T(8,128)} %reduce-scatter.2.cloned.1.call-done), kind=kLoop, calls=%fused_computation.25 | loop fusion | flops 917504 | bytes 7340032 | tf_op jit(solution)/shard_map/div | solution.py:50
  (204 shorter events, 37.2 us)
Async XLA Ops:
  7.2 314.6 %reduce-scatter.2.cloned.1.call-start = ((), (), s32[]{:S(2)}) async-start(), calls=%async_computation.1 | async-start | bytes 33030144 | tf_op jit(solution)/shard_map/reduce_scatter | solution.py:44
Sparse Core Ops, SparseCore 0:
  141.4 180.3 reduce-scatter.1
where the time goes:
time: 334 us; the launch traced here: 333 us
  waiting for transfers between devices  180 us (54%)
  matrix products  77.2 us (23%)
  local copies, waits for them, and re-layouts  38.7 us (12%)
  blocking collectives  15.8 us (5%)
  between operations  14.1 us (4%)
  other arithmetic  5.71 us (2%)
    reduce_scatter x1, waiting for transfers between devices, local(): lax.psum_scatter(lax.map(one_term, (down_index, hidden_blocks)).transpose...  180 us
    dot_general x28, matrix products, one_term(): jnp.dot(part_rows.T, hidden_block, preferred_element_type=jnp.float32)  40.9 us
    dot_general x28, matrix products, one_grad(): jnp.dot(select(index_row), weight_block, preferred_element_type=jnp.float32)  36.3 us
    gather x56, local copies, waits for them, and re-layouts, select(): jnp.take(feature_view, index_row, axis=1).reshape(row_count, kept_span)  32.2 us
    all_gather x1, blocking collectives, local(): gathered = lax.all_gather(cotangent, 'tensor', axis=0, tiled=True)  15.8 us
  transfers between devices with their start and end apart: 1, of which 1 were waited for; matrix products, arithmetic and copies ran while one was open for 0% of the time, Pallas kernels for 0%

commit v1 on v0

--- a/solution.py
+++ b/solution.py
@@ -1,10 +1,14 @@
+import functools
+
 import jax
 import jax.numpy as jnp
 from jax import lax
+from jax.experimental import pallas as pl
+from jax.experimental.pallas import tpu as pltpu
 from jax.sharding import PartitionSpec as P
 
 
-def local(gate_act, up_act, cotangent, down_blocks, down_index):
+def reduced(gate_act, up_act, cotangent, down_blocks, down_index):
     gathered = lax.all_gather(cotangent, "tensor", axis=0, tiled=True)
     row_count = gathered.shape[0]
     local_blocks, kept_span, block_size = down_blocks.shape
@@ -51,6 +55,130 @@
     return (down_grad, gate_out, up_out)
 
 
+def hidden_grad_kernel(index_ref, cot_ref, weight_ref, gate_ref, up_ref, gate_out, up_out, *, per_step, keep):
+    step = pl.program_id(0)
+    for j in range(per_step):
+        block = step * per_step + j
+        chosen = jnp.concatenate(
+            [cot_ref[:, pl.ds(pl.multiple_of(index_ref[block, k] * 128, 128), 128)] for k in range(keep)], axis=1
+        )
+        grad = jnp.dot(chosen, weight_ref[j], preferred_element_type=jnp.float32)
+        span = slice(j * 128, (j + 1) * 128)
+        gate = gate_ref[:, span].astype(jnp.float32)
+        up = up_ref[:, span].astype(jnp.float32)
+        sig = jax.nn.sigmoid(gate)
+        gate_out[:, span] = (grad * up * sig * (1.0 + gate * (1.0 - sig))).astype(jnp.bfloat16)
+        up_out[:, span] = (grad * gate * sig).astype(jnp.bfloat16)
+
+
+def hidden_grads(index, cot, weights, gate, up, per_step=4):
+    blocks, span, size = weights.shape
+    rows = cot.shape[0]
+    wide = pl.BlockSpec((rows, per_step * size), lambda f, *_: (0, f))
+    return pl.pallas_call(
+        functools.partial(hidden_grad_kernel, per_step=per_step, keep=span // size),
+        grid_spec=pltpu.PrefetchScalarGridSpec(
+            num_scalar_prefetch=1,
+            grid=(blocks // per_step,),
+            in_specs=[
+                pl.BlockSpec(cot.shape, lambda f, *_: (0, 0)),
+                pl.BlockSpec((per_step, span, size), lambda f, *_: (f, 0, 0)),
+                wide,
+                wide,
+            ],
+            out_specs=[wide, wide],
+        ),
+        out_shape=[jax.ShapeDtypeStruct(gate.shape, gate.dtype)] * 2,
+        compiler_params=pltpu.CompilerParams(vmem_limit_bytes=32 * 2**20),
+        cost_estimate=pl.CostEstimate(
+            flops=2 * rows * blocks * span * size, bytes_accessed=2 * blocks * span * size, transcendentals=0
+        ),
+        name="hidden_grads",
+    )(index, cot, weights, gate, up)
+
+
+def down_grad_kernel(index_ref, *refs, pieces, per_step, kept, features, scale):
+    hidden, cot, out_ref, turned = refs[:pieces], refs[pieces : 2 * pieces], refs[2 * pieces], refs[2 * pieces + 1]
+    step = pl.program_id(0)
+
+    @pl.when(step == 0)
+    def _():
+        for d in range(features):
+            span = slice(d * 128, (d + 1) * 128)
+            turned[d] = jnp.concatenate([c[:, span] for c in cot], axis=0).T
+
+    for j in range(per_step):
+        block = step * per_step + j
+        right = jnp.concatenate([h[:, j * 128 : (j + 1) * 128] for h in hidden], axis=0)
+        for k in range(kept):
+            left = turned[index_ref[block, k]]
+            out_ref[j, k * 128 : (k + 1) * 128, :] = jnp.dot(left, right, preferred_element_type=jnp.float32) * scale
+
+
+def down_grads(index, hidden, cot, scale, per_step=4):
+    rows, width = hidden[0].shape
+    pieces = len(hidden)
+    kept = index.shape[1]
+    blocks = width // 128
+    features = cot[0].shape[1] // 128
+    tokens = pieces * rows
+    return pl.pallas_call(
+        functools.partial(
+            down_grad_kernel, pieces=pieces, per_step=per_step, kept=kept, features=features, scale=scale
+        ),
+        grid_spec=pltpu.PrefetchScalarGridSpec(
+            num_scalar_prefetch=1,
+            grid=(blocks // per_step,),
+            in_specs=[pl.BlockSpec((rows, per_step * 128), lambda f, *_: (0, f))] * pieces
+            + [pl.BlockSpec(c.shape, lambda f, *_: (0, 0)) for c in cot],
+            out_specs=pl.BlockSpec((per_step, kept * 128, 128), lambda f, *_: (f, 0, 0)),
+            scratch_shapes=[pltpu.VMEM((features, 128, tokens), jnp.bfloat16)],
+        ),
+        out_shape=jax.ShapeDtypeStruct((blocks, kept * 128, 128), jnp.float32),
+        compiler_params=pltpu.CompilerParams(vmem_limit_bytes=32 * 2**20),
+        cost_estimate=pl.CostEstimate(
+            flops=2 * tokens * kept * 128 * width, bytes_accessed=4 * blocks * kept * 128 * 128, transcendentals=0
+        ),
+        name="down_grads",
+    )(index, *hidden, *cot)
+
+
+def spread(own, size):
+    first = [(i, i ^ (2 if i % 2 == 0 else 4)) for i in range(size)]
+    second = [(i, i ^ (4 if i % 2 == 0 else 2)) for i in range(size)]
+    other = [(i, i ^ 1) for i in range(size)]
+    step = functools.partial(lax.ppermute, axis_name="dp")
+    one = step(own, perm=first)
+    two = step(own, perm=second)
+    three = step(one, perm=second)
+    mine = [own, one, two, three]
+    return mine + [step(piece, perm=other) for piece in mine]
+
+
+def gathered(gate_act, up_act, cotangent, down_blocks, down_index):
+    replicas = lax.axis_size("dp")
+    parts = lax.axis_size("tensor")
+    rows, width = gate_act.shape
+    kept = down_index.shape[1] // replicas
+
+    gate_value = gate_act.astype(jnp.float32)
+    hidden = (gate_value * jax.nn.sigmoid(gate_value) * up_act.astype(jnp.float32)).astype(jnp.bfloat16)
+
+    cot = lax.all_gather(cotangent, "tensor", axis=0, tiled=True)
+    hidden_pieces = spread(hidden, replicas)
+    cot_pieces = spread(cot, replicas)
+    gate_out, up_out = hidden_grads(down_index, cot, down_blocks, gate_act, up_act)
+    own_index = lax.dynamic_slice_in_dim(down_index, lax.axis_index("dp") * kept, kept, axis=1)
+    down_grad = down_grads(own_index, hidden_pieces, cot_pieces, 1.0 / replicas)
+    return down_grad.transpose(1, 0, 2), gate_out, up_out
+
+
+def local(gate_act, up_act, cotangent, down_blocks, down_index):
+    if lax.axis_size("dp") == 8 and gate_act.shape[0] % 16 == 0 and gate_act.shape[0] <= 64:
+        return gathered(gate_act, up_act, cotangent, down_blocks, down_index)
+    return reduced(gate_act, up_act, cotangent, down_blocks, down_index)
+
+
 def solution(mesh):
     in_specs = (
         P("dp", "tensor"),

time: 334 us -> 56.7 us (0.17)
  waiting for transfers between devices: 180 us -> 10.1 us
  matrix products: 77.2 us -> 0 us
  local copies, waits for them, and re-layouts: 38.7 us -> 7.9 us
  between operations: 14.1 us -> 0.68 us
  Pallas kernels: 0 us -> 12.3 us
  starting transfers between devices: 0.04 us -> 7.87 us
  other arithmetic: 5.71 us -> 1.19 us
    reduce_scatter x1 -> x0, waiting for transfers between devices: 180 us -> none  [local(): lax.psum_scatter(lax.map(one_term, (down_index, hidden_blocks)).transpose...]
    dot_general x56 -> x0, matrix products: 77.2 us -> none  [the longest x28 40.9 us: one_term(): jnp.dot(part_rows.T, hidden_block, preferred_element_type=jnp.float32)]
    gather x56 -> x0, local copies, waits for them, and re-layouts: 32.2 us -> none  [select(): jnp.take(feature_view, index_row, axis=1).reshape(row_count, kept_span)]
    pallas_call x0 -> x2, Pallas kernels: none -> 12.3 us  [the longest x1 7.06 us: down_grads(): pl.pallas_call(functools.partial(down_grad_kernel, pieces=pieces, per_ste...]
    ppermute x0 -> x14, waiting for transfers between devices: none -> 10.1 us  [the longest x2 4.24 us: spread(): three = step(one, perm=second)]
    ppermute x0 -> x14, starting transfers between devices: none -> 7.87 us  [the longest x2 2.09 us: spread(): two = step(own, perm=second)]
    unnamed x0 -> x7, local copies, waits for them, and re-layouts: none -> 7.83 us
    div x1 -> x0, other arithmetic: 4.25 us -> none  [local(): down_grad = summed / replicas]
  transfers between devices with their start and end apart: 1 -> 14, of which waited for: 1 -> 6; matrix products, arithmetic and copies ran while one was open for 0% -> 4% of each run, Pallas kernels for 0% -> 9%
where the time goes in v1:
time: 56.7 us; the launch traced here: 55.9 us
  blocking collectives  15.8 us (28%)
  Pallas kernels  12.3 us (22%)
  waiting for transfers between devices  10.1 us (18%)
  local copies, waits for them, and re-layouts  7.9 us (14%)
  starting transfers between devices  7.87 us (14%)
  other arithmetic  1.19 us (2%)
  between operations  0.68 us (1%)
    all_gather x1, blocking collectives, gathered(): cot = lax.all_gather(cotangent, 'tensor', axis=0, tiled=True)  15.8 us
    unnamed x7, local copies, waits for them, and re-layouts  7.83 us
    pallas_call x1, Pallas kernels, down_grads(): pl.pallas_call(functools.partial(down_grad_kernel, pieces=pieces, per_ste...  7.06 us
    pallas_call x1, Pallas kernels, hidden_grads(): pl.pallas_call(functools.partial(hidden_grad_kernel, per_step=per_step, k...  5.24 us
    ppermute x2, waiting for transfers between devices, spread(): three = step(one, perm=second)  4.24 us
    ppermute x2, waiting for transfers between devices, spread(): two = step(own, perm=second)  3.18 us
    ppermute x2, waiting for transfers between devices, spread(): one = step(own, perm=first)  2.72 us
    ppermute x2, starting transfers between devices, spread(): two = step(own, perm=second)  2.09 us
  transfers between devices with their start and end apart: 14, of which 6 were waited for; matrix products, arithmetic and copies ran while one was open for 4% of the time, Pallas kernels for 9%

profile of v1, /device:TPU:0, one launch (start us, length us, event | category | flops | bytes accessed | tf_op | source)
XLA Modules:
  0.0 55.9 jit_solution(7203561236136109160)
XLA Ops:
  0.6 15.8 %all_gather.3.refs_8_.cot_ref = bf16[32,4096]{1,0:T(8,128)(2,1)S(1)} all-gather(bf16[8,4096]{1,0:T(8,128)(2,1)} %param.7), channel_id=1, replica_groups=mesh['dp'=8,'tensor'=4] {'tensor'}, dimensions={0}, use_global_device_ids=true | all-gather | bytes 327680 | tf_op jit(solution)/shard_map/all_gather | solution.py:167
  16.5 1.5 %collective-permute-start.7 = (bf16[32,4096]{1,0:T(8,128)(2,1)S(1)}, bf16[32,4096]{1,0:T(8,128)(2,1)S(1)}, u32[]{:S(2)}, u32[]{:S(2)}) collective-permute-start(bf16[32,4096]{1,0:T(8,128)(2,1)S(1)} %all_gather.3.refs_8_.cot_ref), channel_id=1, source_target_pairs={{0,8},{4,20},{8,0},{12,28},{16,24},{20,4},{24,16},{28,12},{1,9},{5... | collective-permute-start | bytes 786440 | tf_op jit(solution)/shard_map/ppermute | solution.py:151
  18.0 1.2 %fusion.4.refs_0_ = bf16[32,3584]{1,0:T(8,128)(2,1)S(1)} fusion(bf16[32,3584]{1,0:T(8,128)(2,1)} %up_ref.1, bf16[32,3584]{1,0:T(8,128)(2,1)} %gate_ref.1), kind=kLoop, calls=%fused_computation.6 | loop fusion | flops 917504 | bytes 688128 | tf_op jit(solution)/shard_map/convert_element_type | solution.py:165
  19.2 0.1 collective-permute-start.3
  19.2 1.6 %collective-permute-start.1 = (bf16[32,3584]{1,0:T(8,128)(2,1)S(1)}, bf16[32,3584]{1,0:T(8,128)(2,1)S(1)}, u32[]{:S(2)}, u32[]{:S(2)}) collective-permute-start(bf16[32,3584]{1,0:T(8,128)(2,1)S(1)} %fusion.4.refs_0_), channel_id=1, source_target_pairs={{0,16},{4,12},{8,24},{12,4},{16,0},{20,28},{24,8},{28,20},{1,17},{... | collective-permute-start | bytes 688136 | tf_op jit(solution)/shard_map/ppermute | solution.py:152
  20.8 0.5 collective-permute-start
  21.4 0.5 collective-permute-start.8
  21.9 0.0 collective-permute-done.3.refs_4_
  21.9 0.6 %collective-permute-start.10 = (bf16[32,4096]{1,0:T(8,128)(2,1)S(1)}, bf16[32,4096]{1,0:T(8,128)(2,1)S(1)}, u32[]{:S(2)}, u32[]{:S(2)}) collective-permute-start(bf16[32,4096]{1,0:T(8,128)(2,1)S(1)} %all_gather.3.refs_8_.cot_ref), channel_id=1, source_target_pairs={{0,4},{4,0},{8,12},{12,8},{16,20},{20,16},{24,28},{28,24},{1,5},{5... | collective-permute-start | bytes 786440 | tf_op jit(solution)/shard_map/ppermute | solution.py:155
  22.4 0.9 %collective-permute-done.7.refs_9_ = bf16[32,4096]{1,0:T(8,128)(2,1)S(1)} collective-permute-done((bf16[32,4096]{1,0:T(8,128)(2,1)S(1)}, bf16[32,4096]{1,0:T(8,128)(2,1)S(1)}, u32[]{:S(2)}, u32[]{:S(2)}) %collective-permute-start.7) | collective-permute-done | bytes 262176 | tf_op jit(solution)/shard_map/ppermute | solution.py:151
  23.3 1.5 %collective-permute-start.9 = (bf16[32,4096]{1,0:T(8,128)(2,1)S(1)}, bf16[32,4096]{1,0:T(8,128)(2,1)S(1)}, u32[]{:S(2)}, u32[]{:S(2)}) collective-permute-start(bf16[32,4096]{1,0:T(8,128)(2,1)S(1)} %collective-permute-done.7.refs_9_), channel_id=1, source_target_pairs={{0,16},{4,12},{8,24},{12,4},{16,0},{20,28},{24,8},{28,20},{1,17},{... | collective-permute-start | bytes 786440 | tf_op jit(solution)/shard_map/ppermute | solution.py:153
  24.8 2.7 %collective-permute-done.1.refs_2_ = bf16[32,3584]{1,0:T(8,128)(2,1)S(1)} collective-permute-done((bf16[32,3584]{1,0:T(8,128)(2,1)S(1)}, bf16[32,3584]{1,0:T(8,128)(2,1)S(1)}, u32[]{:S(2)}, u32[]{:S(2)}) %collective-permute-start.1) | collective-permute-done | bytes 229408 | tf_op jit(solution)/shard_map/ppermute | solution.py:152
  27.5 0.0 collective-permute-start.5
  27.5 1.9 %collective-permute-done.refs_1_ = bf16[32,3584]{1,0:T(8,128)(2,1)S(1)} collective-permute-done((bf16[32,3584]{1,0:T(8,128)(2,1)S(1)}, bf16[32,3584]{1,0:T(8,128)(2,1)S(1)}, u32[]{:S(2)}, u32[]{:S(2)}) %collective-permute-start) | collective-permute-done | bytes 229408 | tf_op jit(solution)/shard_map/ppermute | solution.py:151
  29.4 0.4 collective-permute-start.2
  29.8 0.5 collective-permute-done.8.refs_10_
  30.3 0.4 collective-permute-start.12
  30.7 0.0 collective-permute-done.10.refs_12_
  30.7 0.1 collective-permute-start.11
  30.8 2.3 %collective-permute-done.9.refs_11_ = bf16[32,4096]{1,0:T(8,128)(2,1)S(1)} collective-permute-done((bf16[32,4096]{1,0:T(8,128)(2,1)S(1)}, bf16[32,4096]{1,0:T(8,128)(2,1)S(1)}, u32[]{:S(2)}, u32[]{:S(2)}) %collective-permute-start.9) | collective-permute-done | bytes 262176 | tf_op jit(solution)/shard_map/ppermute | solution.py:153
  33.1 0.4 collective-permute-start.13
  33.5 0.0 collective-permute-done.5.refs_6_
  33.5 0.1 collective-permute-start.4
  33.6 1.9 %collective-permute-done.2.refs_3_ = bf16[32,3584]{1,0:T(8,128)(2,1)S(1)} collective-permute-done((bf16[32,3584]{1,0:T(8,128)(2,1)S(1)}, bf16[32,3584]{1,0:T(8,128)(2,1)S(1)}, u32[]{:S(2)}, u32[]{:S(2)}) %collective-permute-start.2) | collective-permute-done | bytes 229408 | tf_op jit(solution)/shard_map/ppermute | solution.py:153
  35.6 0.1 collective-permute-start.6
  35.7 0.8 %copy.8.index_ref = s32[28,16]{1,0:T(8,128)S(1)} copy(s32[28,16]{0,1:T(8,128)} %param.9) | data formatting | bytes 3584 | tf_op args[4]
  36.5 0.0 copy-start
  36.5 5.2 %copy-done = bf16[28,2048,128]{2,1,0:T(8,128)(2,1)S(1)} copy-done((bf16[28,2048,128]{2,1,0:T(8,128)(2,1)S(1)}, bf16[28,2048,128]{2,1,0:T(8,128)(2,1)}, u32[]{:S(2)}) %copy-start) | copy-done | bytes 14680088
  41.6 0.0 copy-start.1
  41.6 0.9 %copy-done.1 = bf16[32,3584]{1,0:T(8,128)(2,1)S(1)} copy-done((bf16[32,3584]{1,0:T(8,128)(2,1)S(1)}, bf16[32,3584]{1,0:T(8,128)(2,1)}, u32[]{:S(2)}) %copy-start.1) | copy-done | bytes 229400
  42.6 0.0 copy-start.2
  42.6 0.9 %copy-done.2 = bf16[32,3584]{1,0:T(8,128)(2,1)S(1)} copy-done((bf16[32,3584]{1,0:T(8,128)(2,1)S(1)}, bf16[32,3584]{1,0:T(8,128)(2,1)}, u32[]{:S(2)}) %copy-start.2) | copy-done | bytes 229400
  43.5 5.2 %hidden_grads.1 = (bf16[32,3584]{1,0:T(8,128)(2,1)}, bf16[32,3584]{1,0:T(8,128)(2,1)}) custom-call(s32[28,16]{1,0:T(8,128)S(1)} %copy.8.index_ref, bf16[32,4096]{1,0:T(8,128)(2,1)S(1)} %all_gather.3.refs_8_.cot_ref, bf16[28,2048,128]{2,1,0:T(8,128)(2,1)S(1)} %copy-done, bf16[32,3584]{1,0:T(8,128)(2,1)S(1)} %copy-done.2, bf16[32,3584]{1,0:T(8,128)(2,1)S(1)} %copy-done.1), custom_call_target="tpu_custom_call" | custom-call | flops 469762048 | bytes 14680064 | tf_op jit(solution)/shard_map/hidden_grads/pallas_call | solution.py:78
  48.8 0.1 constant_dynamic-slice_fusion.index_ref
  48.8 0.0 collective-permute-done.4.refs_5_
  48.8 0.0 collective-permute-done.12.refs_14_
  48.8 0.0 collective-permute-done.11.refs_13_
  48.8 0.0 collective-permute-done.6.refs_7_
  48.9 0.0 collective-permute-done.13.refs_15_
  48.9 7.1 %down_grads.1 = f32[28,256,128]{2,1,0:T(8,128)} custom-call(s32[28,2]{1,0:T(8,128)S(1)} %constant_dynamic-slice_fusion.index_ref, bf16[32,3584]{1,0:T(8,128)(2,1)S(1)} %fusion.4.refs_0_, bf16[32,3584]{1,0:T(8,128)(2,1)S(1)} %collective-permute-done.refs_1_, bf16[32,3584]{1,0:T(8,128)(2,1)S(1)} %collective-permute-done.1.refs_2_, ...), custom_call_target="tpu_custom_call" | custom-call | flops 469762048 | bytes 3670016 | tf_op jit(solution)/shard_map/down_grads/pallas_call | solution.py:125
Async XLA Ops:
  16.5 6.8 %collective-permute-start.7 = (bf16[32,4096]{1,0:T(8,128)(2,1)S(1)}, bf16[32,4096]{1,0:T(8,128)(2,1)S(1)}, u32[]{:S(2)}, u32[]{:S(2)}) collective-permute-start(bf16[32,4096]{1,0:T(8,128)(2,1)S(1)} %all_gather.3.refs_8_.cot_ref), channel_id=1, source_target_pairs={{0,8},{4,20},{8,0},{12,28},{16,24},{20,4},{24,16},{28,12},{1,9},{5... | collective-permute-start | bytes 786440 | tf_op jit(solution)/shard_map/ppermute | solution.py:151
  19.2 2.7 %collective-permute-start.3 = (bf16[32,3584]{1,0:T(8,128)(2,1)S(1)}, bf16[32,3584]{1,0:T(8,128)(2,1)S(1)}, u32[]{:S(2)}, u32[]{:S(2)}) collective-permute-start(bf16[32,3584]{1,0:T(8,128)(2,1)S(1)} %fusion.4.refs_0_), channel_id=1, source_target_pairs={{0,4},{4,0},{8,12},{12,8},{16,20},{20,16},{24,28},{28,24},{1,5},{5... | collective-permute-start | bytes 688136 | tf_op jit(solution)/shard_map/ppermute | solution.py:155
  19.2 8.3 %collective-permute-start.1 = (bf16[32,3584]{1,0:T(8,128)(2,1)S(1)}, bf16[32,3584]{1,0:T(8,128)(2,1)S(1)}, u32[]{:S(2)}, u32[]{:S(2)}) collective-permute-start(bf16[32,3584]{1,0:T(8,128)(2,1)S(1)} %fusion.4.refs_0_), channel_id=1, source_target_pairs={{0,16},{4,12},{8,24},{12,4},{16,0},{20,28},{24,8},{28,20},{1,17},{... | collective-permute-start | bytes 688136 | tf_op jit(solution)/shard_map/ppermute | solution.py:152
  20.8 8.5 %collective-permute-start = (bf16[32,3584]{1,0:T(8,128)(2,1)S(1)}, bf16[32,3584]{1,0:T(8,128)(2,1)S(1)}, u32[]{:S(2)}, u32[]{:S(2)}) collective-permute-start(bf16[32,3584]{1,0:T(8,128)(2,1)S(1)} %fusion.4.refs_0_), channel_id=1, source_target_pairs={{0,8},{4,20},{8,0},{12,28},{16,24},{20,4},{24,16},{28,12},{1,9},{5... | collective-permute-start | bytes 688136 | tf_op jit(solution)/shard_map/ppermute | solution.py:151
  21.4 8.9 %collective-permute-start.8 = (bf16[32,4096]{1,0:T(8,128)(2,1)S(1)}, bf16[32,4096]{1,0:T(8,128)(2,1)S(1)}, u32[]{:S(2)}, u32[]{:S(2)}) collective-permute-start(bf16[32,4096]{1,0:T(8,128)(2,1)S(1)} %all_gather.3.refs_8_.cot_ref), channel_id=1, source_target_pairs={{0,16},{4,12},{8,24},{12,4},{16,0},{20,28},{24,8},{28,20},{1,17},{... | collective-permute-start | bytes 786440 | tf_op jit(solution)/shard_map/ppermute | solution.py:152
  21.9 8.8 %collective-permute-start.10 = (bf16[32,4096]{1,0:T(8,128)(2,1)S(1)}, bf16[32,4096]{1,0:T(8,128)(2,1)S(1)}, u32[]{:S(2)}, u32[]{:S(2)}) collective-permute-start(bf16[32,4096]{1,0:T(8,128)(2,1)S(1)} %all_gather.3.refs_8_.cot_ref), channel_id=1, source_target_pairs={{0,4},{4,0},{8,12},{12,8},{16,20},{20,16},{24,28},{28,24},{1,5},{5... | collective-permute-start | bytes 786440 | tf_op jit(solution)/shard_map/ppermute | solution.py:155
  23.3 9.8 %collective-permute-start.9 = (bf16[32,4096]{1,0:T(8,128)(2,1)S(1)}, bf16[32,4096]{1,0:T(8,128)(2,1)S(1)}, u32[]{:S(2)}, u32[]{:S(2)}) collective-permute-start(bf16[32,4096]{1,0:T(8,128)(2,1)S(1)} %collective-permute-done.7.refs_9_), channel_id=1, source_target_pairs={{0,16},{4,12},{8,24},{12,4},{16,0},{20,28},{24,8},{28,20},{1,17},{... | collective-permute-start | bytes 786440 | tf_op jit(solution)/shard_map/ppermute | solution.py:153
  27.5 6.0 %collective-permute-start.5 = (bf16[32,3584]{1,0:T(8,128)(2,1)S(1)}, bf16[32,3584]{1,0:T(8,128)(2,1)S(1)}, u32[]{:S(2)}, u32[]{:S(2)}) collective-permute-start(bf16[32,3584]{1,0:T(8,128)(2,1)S(1)} %collective-permute-done.1.refs_2_), channel_id=1, source_target_pairs={{0,4},{4,0},{8,12},{12,8},{16,20},{20,16},{24,28},{28,24},{1,5},{5... | collective-permute-start | bytes 688136 | tf_op jit(solution)/shard_map/ppermute | solution.py:155
  29.4 6.2 %collective-permute-start.2 = (bf16[32,3584]{1,0:T(8,128)(2,1)S(1)}, bf16[32,3584]{1,0:T(8,128)(2,1)S(1)}, u32[]{:S(2)}, u32[]{:S(2)}) collective-permute-start(bf16[32,3584]{1,0:T(8,128)(2,1)S(1)} %collective-permute-done.refs_1_), channel_id=1, source_target_pairs={{0,16},{4,12},{8,24},{12,4},{16,0},{20,28},{24,8},{28,20},{1,17},{... | collective-permute-start | bytes 688136 | tf_op jit(solution)/shard_map/ppermute | solution.py:153
  30.3 18.5 %collective-permute-start.12 = (bf16[32,4096]{1,0:T(8,128)(2,1)S(1)}, bf16[32,4096]{1,0:T(8,128)(2,1)S(1)}, u32[]{:S(2)}, u32[]{:S(2)}) collective-permute-start(bf16[32,4096]{1,0:T(8,128)(2,1)S(1)} %collective-permute-done.8.refs_10_), channel_id=1, source_target_pairs={{0,4},{4,0},{8,12},{12,8},{16,20},{20,16},{24,28},{28,24},{1,5},{5... | collective-permute-start | bytes 786440 | tf_op jit(solution)/shard_map/ppermute | solution.py:155
  30.7 18.2 %collective-permute-start.11 = (bf16[32,4096]{1,0:T(8,128)(2,1)S(1)}, bf16[32,4096]{1,0:T(8,128)(2,1)S(1)}, u32[]{:S(2)}, u32[]{:S(2)}) collective-permute-start(bf16[32,4096]{1,0:T(8,128)(2,1)S(1)} %collective-permute-done.7.refs_9_), channel_id=1, source_target_pairs={{0,4},{4,0},{8,12},{12,8},{16,20},{20,16},{24,28},{28,24},{1,5},{5... | collective-permute-start | bytes 786440 | tf_op jit(solution)/shard_map/ppermute | solution.py:155
  33.1 15.7 %collective-permute-start.13 = (bf16[32,4096]{1,0:T(8,128)(2,1)S(1)}, bf16[32,4096]{1,0:T(8,128)(2,1)S(1)}, u32[]{:S(2)}, u32[]{:S(2)}) collective-permute-start(bf16[32,4096]{1,0:T(8,128)(2,1)S(1)} %collective-permute-done.9.refs_11_), channel_id=1, source_target_pairs={{0,4},{4,0},{8,12},{12,8},{16,20},{20,16},{24,28},{28,24},{1,5},{5... | collective-permute-start | bytes 786440 | tf_op jit(solution)/shard_map/ppermute | solution.py:155
  33.5 15.3 %collective-permute-start.4 = (bf16[32,3584]{1,0:T(8,128)(2,1)S(1)}, bf16[32,3584]{1,0:T(8,128)(2,1)}, u32[]{:S(2)}, u32[]{:S(2)}) collective-permute-start(bf16[32,3584]{1,0:T(8,128)(2,1)S(1)} %collective-permute-done.refs_1_), channel_id=1, source_target_pairs={{0,4},{4,0},{8,12},{12,8},{16,20},{20,16},{24,28},{28,24},{1,5},{5... | collective-permute-start | bytes 688136 | tf_op jit(solution)/shard_map/ppermute | solution.py:155
  35.6 13.3 %collective-permute-start.6 = (bf16[32,3584]{1,0:T(8,128)(2,1)S(1)}, bf16[32,3584]{1,0:T(8,128)(2,1)}, u32[]{:S(2)}, u32[]{:S(2)}) collective-permute-start(bf16[32,3584]{1,0:T(8,128)(2,1)S(1)} %collective-permute-done.2.refs_3_), channel_id=1, source_target_pairs={{0,4},{4,0},{8,12},{12,8},{16,20},{20,16},{24,28},{28,24},{1,5},{5... | collective-permute-start | bytes 688136 | tf_op jit(solution)/shard_map/ppermute | solution.py:155
  36.5 5.2 %copy-start = (bf16[28,2048,128]{2,1,0:T(8,128)(2,1)S(1)}, bf16[28,2048,128]{2,1,0:T(8,128)(2,1)}, u32[]{:S(2)}) copy-start(bf16[28,2048,128]{2,1,0:T(8,128)(2,1)} %weight_ref.1) | copy-start | bytes 44040196
  41.6 0.9 %copy-start.1 = (bf16[32,3584]{1,0:T(8,128)(2,1)S(1)}, bf16[32,3584]{1,0:T(8,128)(2,1)}, u32[]{:S(2)}) copy-start(bf16[32,3584]{1,0:T(8,128)(2,1)} %up_ref.1) | copy-start | bytes 688132
  42.6 0.9 %copy-start.2 = (bf16[32,3584]{1,0:T(8,128)(2,1)S(1)}, bf16[32,3584]{1,0:T(8,128)(2,1)}, u32[]{:S(2)}) copy-start(bf16[32,3584]{1,0:T(8,128)(2,1)} %gate_ref.1) | copy-start | bytes 688132

commit v2 on v0

--- a/solution.py
+++ b/solution.py
@@ -1,10 +1,14 @@
+import functools
+
 import jax
 import jax.numpy as jnp
 from jax import lax
+from jax.experimental import pallas as pl
+from jax.experimental.pallas import tpu as pltpu
 from jax.sharding import PartitionSpec as P
 
 
-def local(gate_act, up_act, cotangent, down_blocks, down_index):
+def reduced(gate_act, up_act, cotangent, down_blocks, down_index):
     gathered = lax.all_gather(cotangent, "tensor", axis=0, tiled=True)
     row_count = gathered.shape[0]
     local_blocks, kept_span, block_size = down_blocks.shape
@@ -51,6 +55,246 @@
     return (down_grad, gate_out, up_out)
 
 
+IN_VMEM = pl.BlockSpec(memory_space=pltpu.VMEM)
+IN_SMEM = pl.BlockSpec(memory_space=pltpu.SMEM)
+ANYWHERE = pl.BlockSpec(memory_space=pl.ANY)
+
+
+def resident(array):
+    return pltpu.with_memory_space_constraint(array, pltpu.VMEM)
+
+
+def remaining(array):
+    return pltpu.with_memory_space_constraint(array, pltpu.HBM)
+
+
+def assemble_kernel(*refs, parts):
+    pieces, out_ref = refs[:parts], refs[-1]
+    here = lax.axis_index("tensor")
+    for place in range(parts):
+
+        @pl.when(here == place)
+        def _():
+            out_ref[...] = jnp.concatenate([pieces[place ^ q][...] for q in range(parts)], axis=0)
+
+
+def assemble(pieces, after):
+    rows, width = pieces[0].shape
+    parts = len(pieces)
+    return pl.pallas_call(
+        functools.partial(assemble_kernel, parts=parts),
+        in_specs=[IN_VMEM] * (parts + len(after)),
+        out_specs=IN_VMEM,
+        out_shape=pltpu.VMEM((parts * rows, width), pieces[0].dtype),
+        compiler_params=pltpu.CompilerParams(vmem_limit_bytes=4 * 2**20),
+        name="assemble",
+    )(*map(resident, pieces), *map(resident, after))
+
+
+def hidden_kernel(*refs, kept):
+    sources, hidden_ref, targets, sems = refs[:kept], refs[kept], refs[kept + 1 : -1], refs[-1]
+    loads = [pltpu.make_async_copy(source, target, sems.at[i]) for i, (source, target) in enumerate(zip(sources, targets))]
+    for load in loads:
+        load.start()
+    for load in loads:
+        load.wait()
+    gate = targets[0][...].astype(jnp.float32)
+    up = targets[1][...].astype(jnp.float32)
+    hidden_ref[...] = (gate * jax.nn.sigmoid(gate) * up).astype(hidden_ref.dtype)
+
+
+def hidden_units(*arrays):
+    outs = [pltpu.VMEM(array.shape, array.dtype) for array in arrays]
+    return pl.pallas_call(
+        functools.partial(hidden_kernel, kept=len(arrays)),
+        in_specs=[ANYWHERE] * len(arrays),
+        out_specs=[IN_VMEM] * (1 + len(arrays)),
+        out_shape=[outs[0]] + outs,
+        scratch_shapes=[pltpu.SemaphoreType.DMA((len(arrays),))],
+        compiler_params=pltpu.CompilerParams(vmem_limit_bytes=4 * 2**20),
+        name="hidden_units",
+    )(*map(remaining, arrays))
+
+
+def fetch_kernel(weight_ref, out_ref, sems, *, start, chunk):
+    blocks = out_ref.shape[0]
+    loads = [
+        pltpu.make_async_copy(weight_ref.at[pl.ds(start + j, chunk)], out_ref.at[pl.ds(j, chunk)], sems.at[j // chunk])
+        for j in range(0, blocks, chunk)
+    ]
+    for load in loads:
+        load.start()
+    for load in loads:
+        load.wait()
+
+
+def fetch(weights, start, blocks, chunk=2):
+    return pl.pallas_call(
+        functools.partial(fetch_kernel, start=start, chunk=chunk),
+        in_specs=[ANYWHERE],
+        out_specs=IN_VMEM,
+        out_shape=pltpu.VMEM((blocks,) + weights.shape[1:], weights.dtype),
+        scratch_shapes=[pltpu.SemaphoreType.DMA((blocks // chunk,))],
+        compiler_params=pltpu.CompilerParams(vmem_limit_bytes=4 * 2**20),
+        cost_estimate=pl.CostEstimate(flops=0, bytes_accessed=2**25, transcendentals=0),
+        name="fetch",
+    )(remaining(weights))
+
+
+def hidden_grad_kernel(index_ref, cot_ref, gate_ref, up_ref, held, weight_ref, gate_out, up_out, rest, sems, *, chunk):
+    ready, span, size = held.shape
+    loads = [
+        pltpu.make_async_copy(weight_ref.at[pl.ds(ready + j, chunk)], rest.at[pl.ds(j, chunk)], sems.at[j // chunk])
+        for j in range(0, rest.shape[0], chunk)
+    ]
+    for load in loads:
+        load.start()
+    for block in range(weight_ref.shape[0]):
+        chosen = jnp.concatenate(
+            [cot_ref[:, pl.ds(pl.multiple_of(index_ref[k, block] * size, size), size)] for k in range(span // size)],
+            axis=1,
+        )
+        if block < ready:
+            weight = held[block]
+        else:
+            if (block - ready) % chunk == 0:
+                loads[(block - ready) // chunk].wait()
+            weight = rest[block - ready]
+        grad = jnp.dot(chosen, weight, preferred_element_type=jnp.float32)
+        here = slice(block * size, (block + 1) * size)
+        gate = gate_ref[:, here].astype(jnp.float32)
+        up = up_ref[:, here].astype(jnp.float32)
+        sig = jax.nn.sigmoid(gate)
+        gate_out[:, here] = (grad * up * sig * (1.0 + gate * (1.0 - sig))).astype(jnp.bfloat16)
+        up_out[:, here] = (grad * gate * sig).astype(jnp.bfloat16)
+
+
+def hidden_grads(index, cot, gate, up, held, weights, chunk=2):
+    blocks, span, size = weights.shape
+    rows = cot.shape[0]
+    left = blocks - held.shape[0]
+    return pl.pallas_call(
+        functools.partial(hidden_grad_kernel, chunk=chunk),
+        in_specs=[IN_SMEM] + [IN_VMEM] * 4 + [ANYWHERE],
+        out_specs=[IN_VMEM] * 2,
+        out_shape=[jax.ShapeDtypeStruct(gate.shape, gate.dtype)] * 2,
+        scratch_shapes=[
+            pltpu.VMEM((left, span, size), weights.dtype),
+            pltpu.SemaphoreType.DMA((left // chunk,)),
+        ],
+        compiler_params=pltpu.CompilerParams(vmem_limit_bytes=10 * 2**20),
+        cost_estimate=pl.CostEstimate(
+            flops=2 * rows * blocks * span * size, bytes_accessed=2 * blocks * span * size, transcendentals=0
+        ),
+        name="hidden_grads",
+    )(index, *map(resident, (cot, gate, up, held)), remaining(weights))
+
+
+def turn_kernel(*refs):
+    pieces, out_ref = refs[:-1], refs[-1]
+    for d in range(out_ref.shape[0]):
+        span = slice(d * 128, (d + 1) * 128)
+        out_ref[d] = jnp.concatenate([piece[:, span] for piece in pieces], axis=0).T
+
+
+def turn(pieces):
+    rows, width = pieces[0].shape
+    return pl.pallas_call(
+        turn_kernel,
+        in_specs=[IN_VMEM] * len(pieces),
+        out_specs=IN_VMEM,
+        out_shape=pltpu.VMEM((width // 128, 128, len(pieces) * rows), pieces[0].dtype),
+        compiler_params=pltpu.CompilerParams(vmem_limit_bytes=4 * 2**20),
+        name="turn",
+    )(*map(resident, pieces))
+
+
+def down_grad_kernel(index_ref, *refs, halves, pieces, kept, chunk, scale):
+    turned, hidden = refs[:halves], refs[halves : halves + pieces]
+    out_ref, held, sems = refs[halves + pieces :]
+    first = lax.axis_index("dp") * kept
+    blocks = held.shape[0]
+    copies = []
+    for start in range(0, blocks, chunk):
+        for block in range(start, start + chunk):
+            right = jnp.concatenate([h[:, block * 128 : (block + 1) * 128] for h in hidden], axis=0)
+            left = jnp.concatenate(
+                [jnp.concatenate([t[index_ref[first + k, block]] for t in turned], axis=1) for k in range(kept)], axis=0
+            )
+            held[block] = jnp.dot(left, right, preferred_element_type=jnp.float32) * scale
+        span = pl.ds(start, chunk)
+        copy = pltpu.make_async_copy(held.at[span], out_ref.at[span], sems.at[start // chunk])
+        copy.start()
+        copies.append(copy)
+    for copy in copies:
+        copy.wait()
+
+
+def down_grads(index, turned, hidden, kept, scale, chunk=4):
+    rows, width = hidden[0].shape
+    pieces = len(hidden)
+    blocks = width // 128
+    shape = (blocks, kept * 128, 128)
+    return pl.pallas_call(
+        functools.partial(
+            down_grad_kernel, halves=len(turned), pieces=pieces, kept=kept, chunk=chunk, scale=scale
+        ),
+        in_specs=[IN_SMEM] + [IN_VMEM] * (len(turned) + pieces),
+        out_specs=ANYWHERE,
+        out_shape=jax.ShapeDtypeStruct(shape, jnp.float32),
+        scratch_shapes=[pltpu.VMEM(shape, jnp.float32), pltpu.SemaphoreType.DMA((blocks // chunk,))],
+        compiler_params=pltpu.CompilerParams(vmem_limit_bytes=12 * 2**20),
+        cost_estimate=pl.CostEstimate(
+            flops=2 * pieces * rows * kept * 128 * width, bytes_accessed=4 * kept * 128 * width, transcendentals=0
+        ),
+        name="down_grads",
+    )(index, *map(resident, turned), *map(resident, hidden))
+
+
+def gathered(gate_act, up_act, cotangent, down_blocks, down_index):
+    replicas = lax.axis_size("dp")
+    parts = lax.axis_size("tensor")
+    kept = down_index.shape[1] // replicas
+
+    first = functools.partial(
+        lax.ppermute, axis_name="dp", perm=[(i, i ^ (2 if i % 2 == 0 else 4)) for i in range(replicas)]
+    )
+    second = functools.partial(
+        lax.ppermute, axis_name="dp", perm=[(i, i ^ (4 if i % 2 == 0 else 2)) for i in range(replicas)]
+    )
+    other = functools.partial(lax.ppermute, axis_name="dp", perm=[(i, i ^ 1) for i in range(replicas)])
+
+    hidden, gate, up, index, near = hidden_units(gate_act, up_act, down_index.T, cotangent)
+    h1, h2, h0x = first(hidden), second(hidden), other(hidden)
+    slices = [near] + [
+        lax.ppermute(cotangent, "tensor", [(i, i ^ s) for i in range(parts)]) for s in range(1, parts)
+    ]
+    held = fetch(down_blocks, 0, 20)
+    cot = assemble(slices, [h1, h2, held])
+    h3 = second(h1)
+    c1, c2, c0x = first(cot), second(cot), other(cot)
+    h1x, h2x = other(h1), other(h2)
+    grads = hidden_grads(index, cot, gate, up, held, down_blocks)
+    c1, c2, grads, h3 = lax.optimization_barrier((c1, c2, grads, h3))
+    gate_out, up_out = grads
+    c3 = second(c1)
+    c1x, c2x, h3x = other(c1), other(c2), other(h3)
+    early = turn([cot, c0x, c1, c1x])
+    c3, early, h0x, h1x, h2x, h3x, c2x = lax.optimization_barrier((c3, early, h0x, h1x, h2x, h3x, c2x))
+    c3x = other(c3)
+    late = turn([c2, c2x, c3, c3x])
+    pieces = [hidden, h0x, h1, h1x, h2, h2x, h3, h3x]
+    down_grad = down_grads(index, [early, late], pieces, kept, 1.0 / replicas)
+    return down_grad.transpose(1, 0, 2), gate_out, up_out
+
+
+def local(gate_act, up_act, cotangent, down_blocks, down_index):
+    sizes = (lax.axis_size("dp"), lax.axis_size("tensor"), gate_act.shape[0], down_blocks.shape[0] % 4)
+    if sizes == (8, 4, 32, 0):
+        return gathered(gate_act, up_act, cotangent, down_blocks, down_index)
+    return reduced(gate_act, up_act, cotangent, down_blocks, down_index)
+
+
 def solution(mesh):
     in_specs = (
         P("dp", "tensor"),

time: 334 us -> 38.1 us (0.11)
  waiting for transfers between devices: 180 us -> 9.27 us
  matrix products: 77.2 us -> 0 us
  local copies, waits for them, and re-layouts: 38.7 us -> 0 us
  blocking collectives: 15.8 us -> 0 us
  Pallas kernels: 0 us -> 14.5 us
  starting transfers between devices: 0.04 us -> 13.6 us
  between operations: 14.1 us -> 0.7 us
  other arithmetic: 5.71 us -> 0 us
    reduce_scatter x1 -> x0, waiting for transfers between devices: 180 us -> none  [local(): lax.psum_scatter(lax.map(one_term, (down_index, hidden_blocks)).transpose...]
    dot_general x56 -> x0, matrix products: 77.2 us -> none  [the longest x28 40.9 us: one_term(): jnp.dot(part_rows.T, hidden_block, preferred_element_type=jnp.float32)]
    gather x56 -> x0, local copies, waits for them, and re-layouts: 32.2 us -> none  [select(): jnp.take(feature_view, index_row, axis=1).reshape(row_count, kept_span)]
    all_gather x1 -> x0, blocking collectives: 15.8 us -> none  [local(): gathered = lax.all_gather(cotangent, 'tensor', axis=0, tiled=True)]
    pallas_call x0 -> x7, Pallas kernels: none -> 14.5 us  [the longest x1 5.62 us: hidden_grads(): pl.pallas_call(functools.partial(hidden_grad_kernel, chunk=chunk), in_spe...]
    ppermute x0 -> x17, starting transfers between devices: none -> 13.6 us  [the longest x3 5.03 us: gathered(): h1, h2, h0x = (first(hidden), second(hidden), other(hidden))]
    ppermute x0 -> x17, waiting for transfers between devices: none -> 9.27 us  [the longest x1 2.89 us: gathered(): c3 = second(c1)]
    div x1 -> x0, other arithmetic: 4.25 us -> none  [local(): down_grad = summed / replicas]
  transfers between devices with their start and end apart: 1 -> 17, of which waited for: 1 -> 8; matrix products, arithmetic and copies ran while one was open for 0% -> 0% of each run, Pallas kernels for 0% -> 26%
where the time goes in v2:
time: 38.1 us; the launch traced here: 38 us
  Pallas kernels  14.5 us (38%)
  starting transfers between devices  13.6 us (36%)
  waiting for transfers between devices  9.27 us (24%)
  between operations  0.7 us (2%)
    pallas_call x1, Pallas kernels, hidden_grads(): pl.pallas_call(functools.partial(hidden_grad_kernel, chunk=chunk), in_spe...  5.62 us
    ppermute x3, starting transfers between devices, gathered(): h1, h2, h0x = (first(hidden), second(hidden), other(hidden))  5.03 us
    ppermute x3, starting transfers between devices, gathered(): lax.ppermute(cotangent, 'tensor', [(i, i ^ s) for i in range(parts)])  4.39 us
    pallas_call x1, Pallas kernels, fetch(): pl.pallas_call(functools.partial(fetch_kernel, start=start, chunk=chunk),...  4.09 us
    ppermute x1, waiting for transfers between devices, gathered(): c3 = second(c1)  2.89 us
    pallas_call x1, Pallas kernels, down_grads(): pl.pallas_call(functools.partial(down_grad_kernel, halves=len(turned), pi...  2.85 us
    ppermute x3, waiting for transfers between devices, gathered(): lax.ppermute(cotangent, 'tensor', [(i, i ^ s) for i in range(parts)])  1.95 us
    ppermute x1, waiting for transfers between devices, gathered(): c3x = other(c3)  1.53 us
  transfers between devices with their start and end apart: 17, of which 8 were waited for; matrix products, arithmetic and copies ran while one was open for 0% of the time, Pallas kernels for 26%

profile of v2, /device:TPU:0, one launch (start us, length us, event | category | flops | bytes accessed | tf_op | source)
XLA Modules:
  0.0 38.0 jit_solution(9711883816773745922)
XLA Ops:
  0.6 1.2 %hidden_units.1 = (bf16[32,3584]{1,0:T(8,128)(2,1)S(1)}, bf16[32,3584]{1,0:T(8,128)(2,1)S(1)}, bf16[32,3584]{1,0:T(8,128)(2,1)S(1)}, s32[16,28]{1,0:T(8,128)S(1)}, bf16[8,4096]{1,0:T(8,128)(2,1)S(1)}) custom-call(bf16[32,3584]{1,0:T(8,128)(2,1)} %refs_0_.1, bf16[32,3584]{1,0:T(8,128)(2,1)} %refs_1_.1, s32[16,28]{1,0:T(8,128)} %bitcast.3, bf16[8,4096]{1,0:T(8,128)(2,1)} %refs_3_.1), custom_call_target="tpu_custom_call" | custom-call | tf_op jit(solution)/shard_map/hidden_units/pallas_call | solution.py:108
  1.9 3.0 %collective-permute-start.3 = (bf16[32,3584]{1,0:T(8,128)(2,1)S(1)}, bf16[32,3584]{1,0:T(8,128)(2,1)S(1)}, u32[]{:S(2)}, u32[]{:S(2)}) collective-permute-start(bf16[32,3584]{1,0:T(8,128)(2,1)S(1)} %get-tuple-element.24.refs_2_), channel_id=1, source_target_pairs={{0,8},{4,20},{8,0},{12,28},{16,24},{20,4},{24,16},{28,12},{1,9},{5... | collective-permute-start | bytes 688136 | tf_op jit(solution)/shard_map/ppermute | solution.py:268
  4.9 1.5 %collective-permute-start.4 = (bf16[32,3584]{1,0:T(8,128)(2,1)S(1)}, bf16[32,3584]{1,0:T(8,128)(2,1)S(1)}, u32[]{:S(2)}, u32[]{:S(2)}) collective-permute-start(bf16[32,3584]{1,0:T(8,128)(2,1)S(1)} %get-tuple-element.24.refs_2_), channel_id=1, source_target_pairs={{0,16},{4,12},{8,24},{12,4},{16,0},{20,28},{24,8},{28,20},{1,17},{... | collective-permute-start | bytes 688136 | tf_op jit(solution)/shard_map/ppermute | solution.py:268
  6.4 1.6 %collective-permute-start = (bf16[8,4096]{1,0:T(8,128)(2,1)}, bf16[8,4096]{1,0:T(8,128)(2,1)S(1)}, u32[]{:S(2)}, u32[]{:S(2)}) collective-permute-start(bf16[8,4096]{1,0:T(8,128)(2,1)} %refs_3_.1), channel_id=1, source_target_pairs={{0,1},{1,0},{2,3},{3,2},{4,5},{5,4},{6,7},{7,6},{8,9},{9,8},{10,11... | collective-permute-start | bytes 196616 | tf_op jit(solution)/shard_map/ppermute | solution.py:270
  8.0 2.6 %collective-permute-start.1 = (bf16[8,4096]{1,0:T(8,128)(2,1)}, bf16[8,4096]{1,0:T(8,128)(2,1)S(1)}, u32[]{:S(2)}, u32[]{:S(2)}) collective-permute-start(bf16[8,4096]{1,0:T(8,128)(2,1)} %refs_3_.1), channel_id=1, source_target_pairs={{0,2},{1,3},{2,0},{3,1},{4,6},{5,7},{6,4},{7,5},{8,10},{9,11},{10,... | collective-permute-start | bytes 196616 | tf_op jit(solution)/shard_map/ppermute | solution.py:270
  10.5 0.2 collective-permute-start.2
  10.8 4.1 %fetch.1.refs_6_.held = bf16[20,2048,128]{2,1,0:T(8,128)(2,1)S(1)} custom-call(bf16[28,2048,128]{2,1,0:T(8,128)(2,1)} %weight_ref.3), custom_call_target="tpu_custom_call" | custom-call | bytes 33554432 | tf_op jit(solution)/shard_map/fetch/pallas_call | solution.py:132
  14.9 0.0 collective-permute-done.refs_1_
  14.9 0.0 collective-permute-done.1.refs_2_
  14.9 1.9 %collective-permute-done.2.refs_3_ = bf16[8,4096]{1,0:T(8,128)(2,1)S(1)} collective-permute-done((bf16[8,4096]{1,0:T(8,128)(2,1)}, bf16[8,4096]{1,0:T(8,128)(2,1)S(1)}, u32[]{:S(2)}, u32[]{:S(2)}) %collective-permute-start.2) | collective-permute-done | bytes 65568 | tf_op jit(solution)/shard_map/ppermute | solution.py:270
  16.8 0.0 collective-permute-done.3.refs_4_
  16.8 0.0 collective-permute-done.4.refs_5_.refs_6_
  16.8 0.1 assemble.1.cot_ref.refs_0_
  16.9 0.6 %collective-permute-start.5 = (bf16[32,4096]{1,0:T(8,128)(2,1)S(1)}, bf16[32,4096]{1,0:T(8,128)(2,1)S(1)}, u32[]{:S(2)}, u32[]{:S(2)}) collective-permute-start(bf16[32,4096]{1,0:T(8,128)(2,1)S(1)} %assemble.1.cot_ref.refs_0_), channel_id=1, source_target_pairs={{0,8},{4,20},{8,0},{12,28},{16,24},{20,4},{24,16},{28,12},{1,9},{5... | collective-permute-start | bytes 786440 | tf_op jit(solution)/shard_map/ppermute | solution.py:275
  17.5 0.5 %collective-permute-start.6 = (bf16[32,4096]{1,0:T(8,128)(2,1)S(1)}, bf16[32,4096]{1,0:T(8,128)(2,1)S(1)}, u32[]{:S(2)}, u32[]{:S(2)}) collective-permute-start(bf16[32,4096]{1,0:T(8,128)(2,1)S(1)} %assemble.1.cot_ref.refs_0_), channel_id=1, source_target_pairs={{0,16},{4,12},{8,24},{12,4},{16,0},{20,28},{24,8},{28,20},{1,17},{... | collective-permute-start | bytes 786440 | tf_op jit(solution)/shard_map/ppermute | solution.py:275
  18.0 1.5 %collective-permute-start.7 = (bf16[32,3584]{1,0:T(8,128)(2,1)S(1)}, bf16[32,3584]{1,0:T(8,128)(2,1)S(1)}, u32[]{:S(2)}, u32[]{:S(2)}) collective-permute-start(bf16[32,3584]{1,0:T(8,128)(2,1)S(1)} %collective-permute-done.3.refs_4_), channel_id=1, source_target_pairs={{0,16},{4,12},{8,24},{12,4},{16,0},{20,28},{24,8},{28,20},{1,17},{... | collective-permute-start | bytes 688136 | tf_op jit(solution)/shard_map/ppermute | solution.py:274
  19.5 0.0 collective-permute-start.9
  19.5 5.6 %hidden_grads.1 = (bf16[32,3584]{1,0:T(8,128)(2,1)}, bf16[32,3584]{1,0:T(8,128)(2,1)}) custom-call(s32[16,28]{1,0:T(8,128)S(1)} %get-tuple-element.22.index_ref, bf16[32,4096]{1,0:T(8,128)(2,1)S(1)} %assemble.1.cot_ref.refs_0_, bf16[32,3584]{1,0:T(8,128)(2,1)S(1)} %get-tuple-element.25.gate_ref, bf16[32,3584]{1,0:T(8,128)(2,1)S(1)} %get-tuple-element.26.up_ref, ...), custom_call_target="tpu_custom_call" | custom-call | flops 469762048 | bytes 14680064 | tf_op jit(solution)/shard_map/hidden_grads/pallas_call | solution.py:176
  25.1 1.2 %collective-permute-done.7.refs_8_ = bf16[32,3584]{1,0:T(8,128)(2,1)S(1)} collective-permute-done((bf16[32,3584]{1,0:T(8,128)(2,1)S(1)}, bf16[32,3584]{1,0:T(8,128)(2,1)S(1)}, u32[]{:S(2)}, u32[]{:S(2)}) %collective-permute-start.7) | collective-permute-done | bytes 229408 | tf_op jit(solution)/shard_map/ppermute | solution.py:274
  26.3 0.0 collective-permute-done.5.refs_2_
  26.3 0.0 collective-permute-done.6.refs_0_
  26.3 0.0 collective-permute-start.10
  26.3 0.5 %collective-permute-start.11 = (bf16[32,3584]{1,0:T(8,128)(2,1)S(1)}, bf16[32,3584]{1,0:T(8,128)(2,1)S(1)}, u32[]{:S(2)}, u32[]{:S(2)}) collective-permute-start(bf16[32,3584]{1,0:T(8,128)(2,1)S(1)} %get-tuple-element.24.refs_2_), channel_id=1, source_target_pairs={{0,4},{4,0},{8,12},{12,8},{16,20},{20,16},{24,28},{28,24},{1,5},{5... | collective-permute-start | bytes 688136 | tf_op jit(solution)/shard_map/ppermute | solution.py:268
  26.8 0.1 collective-permute-start.15
  26.9 0.6 %collective-permute-start.8 = (bf16[32,4096]{1,0:T(8,128)(2,1)S(1)}, bf16[32,4096]{1,0:T(8,128)(2,1)S(1)}, u32[]{:S(2)}, u32[]{:S(2)}) collective-permute-start(bf16[32,4096]{1,0:T(8,128)(2,1)S(1)} %collective-permute-done.5.refs_2_), channel_id=1, source_target_pairs={{0,16},{4,12},{8,24},{12,4},{16,0},{20,28},{24,8},{28,20},{1,17},{... | collective-permute-start | bytes 786440 | tf_op jit(solution)/shard_map/ppermute | solution.py:280
  27.5 0.7 %collective-permute-done.11.refs_3_ = bf16[32,3584]{1,0:T(8,128)(2,1)S(1)} collective-permute-done((bf16[32,3584]{1,0:T(8,128)(2,1)S(1)}, bf16[32,3584]{1,0:T(8,128)(2,1)S(1)}, u32[]{:S(2)}, u32[]{:S(2)}) %collective-permute-start.11) | collective-permute-done | bytes 229408 | tf_op jit(solution)/shard_map/ppermute | solution.py:268
  28.2 0.4 collective-permute-start.12
  28.6 0.0 collective-permute-done.9.refs_1_
  28.6 0.1 collective-permute-start.13
  28.7 0.0 collective-permute-done.10.refs_3_
  28.7 0.4 collective-permute-start.14
  29.1 0.3 turn.2.refs_0_
  29.4 0.3 collective-permute-done.12.refs_5_
  29.7 0.4 collective-permute-done.13.refs_7_
  30.1 0.3 collective-permute-done.14.refs_9_
  30.4 0.0 collective-permute-done.15.refs_1_
  30.4 2.9 %collective-permute-done.8.refs_2_ = bf16[32,4096]{1,0:T(8,128)(2,1)S(1)} collective-permute-done((bf16[32,4096]{1,0:T(8,128)(2,1)S(1)}, bf16[32,4096]{1,0:T(8,128)(2,1)S(1)}, u32[]{:S(2)}, u32[]{:S(2)}) %collective-permute-start.8) | collective-permute-done | bytes 262176 | tf_op jit(solution)/shard_map/ppermute | solution.py:280
  33.3 0.0 collective-permute-start.16
  33.3 1.5 %collective-permute-done.16.refs_3_ = bf16[32,4096]{1,0:T(8,128)(2,1)S(1)} collective-permute-done((bf16[32,4096]{1,0:T(8,128)(2,1)S(1)}, bf16[32,4096]{1,0:T(8,128)(2,1)S(1)}, u32[]{:S(2)}, u32[]{:S(2)}) %collective-permute-start.16) | collective-permute-done | bytes 262176 | tf_op jit(solution)/shard_map/ppermute | solution.py:284
  34.8 0.3 turn.3.refs_1_
  35.1 2.8 %down_grads.1 = f32[28,256,128]{2,1,0:T(8,128)} custom-call(s32[16,28]{1,0:T(8,128)S(1)} %get-tuple-element.22.index_ref, bf16[32,128,128]{2,1,0:T(8,128)(2,1)S(1)} %turn.2.refs_0_, bf16[32,128,128]{2,1,0:T(8,128)(2,1)S(1)} %turn.3.refs_1_, bf16[32,3584]{1,0:T(8,128)(2,1)S(1)} %get-tuple-element.24.refs_2_, ...), custom_call_target="tpu_custom_call" | custom-call | flops 469762048 | bytes 3670016 | tf_op jit(solution)/shard_map/down_grads/pallas_call | solution.py:238
Async XLA Ops:
  1.9 15.0 %collective-permute-start.3 = (bf16[32,3584]{1,0:T(8,128)(2,1)S(1)}, bf16[32,3584]{1,0:T(8,128)(2,1)S(1)}, u32[]{:S(2)}, u32[]{:S(2)}) collective-permute-start(bf16[32,3584]{1,0:T(8,128)(2,1)S(1)} %get-tuple-element.24.refs_2_), channel_id=1, source_target_pairs={{0,8},{4,20},{8,0},{12,28},{16,24},{20,4},{24,16},{28,12},{1,9},{5... | collective-permute-start | bytes 688136 | tf_op jit(solution)/shard_map/ppermute | solution.py:268
  4.9 12.0 %collective-permute-start.4 = (bf16[32,3584]{1,0:T(8,128)(2,1)S(1)}, bf16[32,3584]{1,0:T(8,128)(2,1)S(1)}, u32[]{:S(2)}, u32[]{:S(2)}) collective-permute-start(bf16[32,3584]{1,0:T(8,128)(2,1)S(1)} %get-tuple-element.24.refs_2_), channel_id=1, source_target_pairs={{0,16},{4,12},{8,24},{12,4},{16,0},{20,28},{24,8},{28,20},{1,17},{... | collective-permute-start | bytes 688136 | tf_op jit(solution)/shard_map/ppermute | solution.py:268
  6.4 8.5 %collective-permute-start = (bf16[8,4096]{1,0:T(8,128)(2,1)}, bf16[8,4096]{1,0:T(8,128)(2,1)S(1)}, u32[]{:S(2)}, u32[]{:S(2)}) collective-permute-start(bf16[8,4096]{1,0:T(8,128)(2,1)} %refs_3_.1), channel_id=1, source_target_pairs={{0,1},{1,0},{2,3},{3,2},{4,5},{5,4},{6,7},{7,6},{8,9},{9,8},{10,11... | collective-permute-start | bytes 196616 | tf_op jit(solution)/shard_map/ppermute | solution.py:270
  8.0 6.9 %collective-permute-start.1 = (bf16[8,4096]{1,0:T(8,128)(2,1)}, bf16[8,4096]{1,0:T(8,128)(2,1)S(1)}, u32[]{:S(2)}, u32[]{:S(2)}) collective-permute-start(bf16[8,4096]{1,0:T(8,128)(2,1)} %refs_3_.1), channel_id=1, source_target_pairs={{0,2},{1,3},{2,0},{3,1},{4,6},{5,7},{6,4},{7,5},{8,10},{9,11},{10,... | collective-permute-start | bytes 196616 | tf_op jit(solution)/shard_map/ppermute | solution.py:270
  10.5 6.3 %collective-permute-start.2 = (bf16[8,4096]{1,0:T(8,128)(2,1)}, bf16[8,4096]{1,0:T(8,128)(2,1)S(1)}, u32[]{:S(2)}, u32[]{:S(2)}) collective-permute-start(bf16[8,4096]{1,0:T(8,128)(2,1)} %refs_3_.1), channel_id=1, source_target_pairs={{0,3},{1,2},{2,1},{3,0},{4,7},{5,6},{6,5},{7,4},{8,11},{9,10},{10,... | collective-permute-start | bytes 196616 | tf_op jit(solution)/shard_map/ppermute | solution.py:270
  16.9 9.4 %collective-permute-start.5 = (bf16[32,4096]{1,0:T(8,128)(2,1)S(1)}, bf16[32,4096]{1,0:T(8,128)(2,1)S(1)}, u32[]{:S(2)}, u32[]{:S(2)}) collective-permute-start(bf16[32,4096]{1,0:T(8,128)(2,1)S(1)} %assemble.1.cot_ref.refs_0_), channel_id=1, source_target_pairs={{0,8},{4,20},{8,0},{12,28},{16,24},{20,4},{24,16},{28,12},{1,9},{5... | collective-permute-start | bytes 786440 | tf_op jit(solution)/shard_map/ppermute | solution.py:275
  17.5 8.8 %collective-permute-start.6 = (bf16[32,4096]{1,0:T(8,128)(2,1)S(1)}, bf16[32,4096]{1,0:T(8,128)(2,1)S(1)}, u32[]{:S(2)}, u32[]{:S(2)}) collective-permute-start(bf16[32,4096]{1,0:T(8,128)(2,1)S(1)} %assemble.1.cot_ref.refs_0_), channel_id=1, source_target_pairs={{0,16},{4,12},{8,24},{12,4},{16,0},{20,28},{24,8},{28,20},{1,17},{... | collective-permute-start | bytes 786440 | tf_op jit(solution)/shard_map/ppermute | solution.py:275
  18.0 8.3 %collective-permute-start.7 = (bf16[32,3584]{1,0:T(8,128)(2,1)S(1)}, bf16[32,3584]{1,0:T(8,128)(2,1)S(1)}, u32[]{:S(2)}, u32[]{:S(2)}) collective-permute-start(bf16[32,3584]{1,0:T(8,128)(2,1)S(1)} %collective-permute-done.3.refs_4_), channel_id=1, source_target_pairs={{0,16},{4,12},{8,24},{12,4},{16,0},{20,28},{24,8},{28,20},{1,17},{... | collective-permute-start | bytes 688136 | tf_op jit(solution)/shard_map/ppermute | solution.py:274
  19.5 9.1 %collective-permute-start.9 = (bf16[32,4096]{1,0:T(8,128)(2,1)S(1)}, bf16[32,4096]{1,0:T(8,128)(2,1)S(1)}, u32[]{:S(2)}, u32[]{:S(2)}) collective-permute-start(bf16[32,4096]{1,0:T(8,128)(2,1)S(1)} %assemble.1.cot_ref.refs_0_), channel_id=1, source_target_pairs={{0,4},{4,0},{8,12},{12,8},{16,20},{20,16},{24,28},{28,24},{1,5},{5... | collective-permute-start | bytes 786440 | tf_op jit(solution)/shard_map/ppermute | solution.py:275
  26.3 2.4 %collective-permute-start.10 = (bf16[32,4096]{1,0:T(8,128)(2,1)S(1)}, bf16[32,4096]{1,0:T(8,128)(2,1)S(1)}, u32[]{:S(2)}, u32[]{:S(2)}) collective-permute-start(bf16[32,4096]{1,0:T(8,128)(2,1)S(1)} %collective-permute-done.5.refs_2_), channel_id=1, source_target_pairs={{0,4},{4,0},{8,12},{12,8},{16,20},{20,16},{24,28},{28,24},{1,5},{5... | collective-permute-start | bytes 786440 | tf_op jit(solution)/shard_map/ppermute | solution.py:281
  26.3 1.9 %collective-permute-start.11 = (bf16[32,3584]{1,0:T(8,128)(2,1)S(1)}, bf16[32,3584]{1,0:T(8,128)(2,1)S(1)}, u32[]{:S(2)}, u32[]{:S(2)}) collective-permute-start(bf16[32,3584]{1,0:T(8,128)(2,1)S(1)} %get-tuple-element.24.refs_2_), channel_id=1, source_target_pairs={{0,4},{4,0},{8,12},{12,8},{16,20},{20,16},{24,28},{28,24},{1,5},{5... | collective-permute-start | bytes 688136 | tf_op jit(solution)/shard_map/ppermute | solution.py:268
  26.8 3.5 %collective-permute-start.15 = (bf16[32,4096]{1,0:T(8,128)(2,1)S(1)}, bf16[32,4096]{1,0:T(8,128)(2,1)S(1)}, u32[]{:S(2)}, u32[]{:S(2)}) collective-permute-start(bf16[32,4096]{1,0:T(8,128)(2,1)S(1)} %collective-permute-done.6.refs_0_), channel_id=1, source_target_pairs={{0,4},{4,0},{8,12},{12,8},{16,20},{20,16},{24,28},{28,24},{1,5},{5... | collective-permute-start | bytes 786440 | tf_op jit(solution)/shard_map/ppermute | solution.py:281
  26.9 6.4 %collective-permute-start.8 = (bf16[32,4096]{1,0:T(8,128)(2,1)S(1)}, bf16[32,4096]{1,0:T(8,128)(2,1)S(1)}, u32[]{:S(2)}, u32[]{:S(2)}) collective-permute-start(bf16[32,4096]{1,0:T(8,128)(2,1)S(1)} %collective-permute-done.5.refs_2_), channel_id=1, source_target_pairs={{0,16},{4,12},{8,24},{12,4},{16,0},{20,28},{24,8},{28,20},{1,17},{... | collective-permute-start | bytes 786440 | tf_op jit(solution)/shard_map/ppermute | solution.py:280
  28.2 1.5 %collective-permute-start.12 = (bf16[32,3584]{1,0:T(8,128)(2,1)S(1)}, bf16[32,3584]{1,0:T(8,128)(2,1)S(1)}, u32[]{:S(2)}, u32[]{:S(2)}) collective-permute-start(bf16[32,3584]{1,0:T(8,128)(2,1)S(1)} %collective-permute-done.3.refs_4_), channel_id=1, source_target_pairs={{0,4},{4,0},{8,12},{12,8},{16,20},{20,16},{24,28},{28,24},{1,5},{5... | collective-permute-start | bytes 688136 | tf_op jit(solution)/shard_map/ppermute | solution.py:276
  28.6 1.5 %collective-permute-start.13 = (bf16[32,3584]{1,0:T(8,128)(2,1)S(1)}, bf16[32,3584]{1,0:T(8,128)(2,1)S(1)}, u32[]{:S(2)}, u32[]{:S(2)}) collective-permute-start(bf16[32,3584]{1,0:T(8,128)(2,1)S(1)} %collective-permute-done.4.refs_5_.refs_6_), channel_id=1, source_target_pairs={{0,4},{4,0},{8,12},{12,8},{16,20},{20,16},{24,28},{28,24},{1,5},{5... | collective-permute-start | bytes 688136 | tf_op jit(solution)/shard_map/ppermute | solution.py:276
  28.7 1.7 %collective-permute-start.14 = (bf16[32,3584]{1,0:T(8,128)(2,1)S(1)}, bf16[32,3584]{1,0:T(8,128)(2,1)S(1)}, u32[]{:S(2)}, u32[]{:S(2)}) collective-permute-start(bf16[32,3584]{1,0:T(8,128)(2,1)S(1)} %collective-permute-done.7.refs_8_), channel_id=1, source_target_pairs={{0,4},{4,0},{8,12},{12,8},{16,20},{20,16},{24,28},{28,24},{1,5},{5... | collective-permute-start | bytes 688136 | tf_op jit(solution)/shard_map/ppermute | solution.py:281
  33.3 1.5 %collective-permute-start.16 = (bf16[32,4096]{1,0:T(8,128)(2,1)S(1)}, bf16[32,4096]{1,0:T(8,128)(2,1)S(1)}, u32[]{:S(2)}, u32[]{:S(2)}) collective-permute-start(bf16[32,4096]{1,0:T(8,128)(2,1)S(1)} %collective-permute-done.8.refs_2_), channel_id=1, source_target_pairs={{0,4},{4,0},{8,12},{12,8},{16,20},{20,16},{24,28},{28,24},{1,5},{5... | collective-permute-start | bytes 786440 | tf_op jit(solution)/shard_map/ppermute | solution.py:284

commit v3 on v2

--- a/solution.py
+++ b/solution.py
@@ -55,6 +55,7 @@
     return (down_grad, gate_out, up_out)
 
 
+LONG = 2**27
 IN_VMEM = pl.BlockSpec(memory_space=pltpu.VMEM)
 IN_SMEM = pl.BlockSpec(memory_space=pltpu.SMEM)
 ANYWHERE = pl.BlockSpec(memory_space=pl.ANY)
@@ -69,7 +70,7 @@
 
 
 def assemble_kernel(*refs, parts):
-    pieces, out_ref = refs[:parts], refs[-1]
+    pieces, out_ref = refs[:parts][::-1], refs[-1]
     here = lax.axis_index("tensor")
     for place in range(parts):
 
@@ -87,8 +88,9 @@
         out_specs=IN_VMEM,
         out_shape=pltpu.VMEM((parts * rows, width), pieces[0].dtype),
         compiler_params=pltpu.CompilerParams(vmem_limit_bytes=4 * 2**20),
+        cost_estimate=pl.CostEstimate(flops=0, bytes_accessed=LONG, transcendentals=0),
         name="assemble",
-    )(*map(resident, pieces), *map(resident, after))
+    )(*map(resident, pieces[::-1]), *map(resident, after))
 
 
 def hidden_kernel(*refs, kept):
@@ -112,15 +114,16 @@
         out_shape=[outs[0]] + outs,
         scratch_shapes=[pltpu.SemaphoreType.DMA((len(arrays),))],
         compiler_params=pltpu.CompilerParams(vmem_limit_bytes=4 * 2**20),
+        cost_estimate=pl.CostEstimate(flops=0, bytes_accessed=LONG, transcendentals=0),
         name="hidden_units",
     )(*map(remaining, arrays))
 
 
-def fetch_kernel(weight_ref, out_ref, sems, *, start, chunk):
-    blocks = out_ref.shape[0]
+def fetch_kernel(weight_ref, *refs, start, chunk):
+    out_ref, sems = refs[-2:]
     loads = [
         pltpu.make_async_copy(weight_ref.at[pl.ds(start + j, chunk)], out_ref.at[pl.ds(j, chunk)], sems.at[j // chunk])
-        for j in range(0, blocks, chunk)
+        for j in range(0, out_ref.shape[0], chunk)
     ]
     for load in loads:
         load.start()
@@ -128,66 +131,98 @@
         load.wait()
 
 
-def fetch(weights, start, blocks, chunk=2):
+def fetch(weights, start, blocks, after=(), chunk=2):
+    shape = (blocks,) + weights.shape[1:]
     return pl.pallas_call(
         functools.partial(fetch_kernel, start=start, chunk=chunk),
-        in_specs=[ANYWHERE],
+        in_specs=[ANYWHERE] + [IN_VMEM] * len(after),
         out_specs=IN_VMEM,
-        out_shape=pltpu.VMEM((blocks,) + weights.shape[1:], weights.dtype),
+        out_shape=pltpu.VMEM(shape, weights.dtype),
         scratch_shapes=[pltpu.SemaphoreType.DMA((blocks // chunk,))],
         compiler_params=pltpu.CompilerParams(vmem_limit_bytes=4 * 2**20),
-        cost_estimate=pl.CostEstimate(flops=0, bytes_accessed=2**25, transcendentals=0),
+        cost_estimate=pl.CostEstimate(flops=0, bytes_accessed=2**18 * blocks, transcendentals=0),
         name="fetch",
-    )(remaining(weights))
-
-
-def hidden_grad_kernel(index_ref, cot_ref, gate_ref, up_ref, held, weight_ref, gate_out, up_out, rest, sems, *, chunk):
-    ready, span, size = held.shape
-    loads = [
-        pltpu.make_async_copy(weight_ref.at[pl.ds(ready + j, chunk)], rest.at[pl.ds(j, chunk)], sems.at[j // chunk])
-        for j in range(0, rest.shape[0], chunk)
-    ]
-    for load in loads:
+    )(remaining(weights), *map(resident, after))
+
+
+def hidden_grad_kernel(*refs, start, fetched, earlier, ahead):
+    index_ref, cot_ref, gate_ref, up_ref = refs[:4]
+    held = refs[4 : 4 + fetched]
+    done = refs[4 + fetched : 4 + fetched + earlier]
+    span, size = held[0].shape[1:]
+    if ahead:
+        weight_ref, (gate_out, up_out, next_ref, sem) = refs[4 + fetched + earlier], refs[-4:]
+        load = pltpu.make_async_copy(weight_ref.at[pl.ds(weight_ref.shape[0] - ahead, ahead)], next_ref, sem)
         load.start()
-    for block in range(weight_ref.shape[0]):
+    else:
+        gate_out, up_out = refs[-2:]
+    places = [(ref, j) for ref in held for j in range(ref.shape[0])]
+    for source, target in zip(done, (gate_out, up_out)):
+        target[:, : start * size] = source[...]
+    for block in range(start, gate_out.shape[1] // size):
         chosen = jnp.concatenate(
             [cot_ref[:, pl.ds(pl.multiple_of(index_ref[k, block] * size, size), size)] for k in range(span // size)],
             axis=1,
         )
-        if block < ready:
-            weight = held[block]
-        else:
-            if (block - ready) % chunk == 0:
-                loads[(block - ready) // chunk].wait()
-            weight = rest[block - ready]
-        grad = jnp.dot(chosen, weight, preferred_element_type=jnp.float32)
+        ref, j = places[block]
+        grad = jnp.dot(chosen, ref[j], preferred_element_type=jnp.float32)
         here = slice(block * size, (block + 1) * size)
         gate = gate_ref[:, here].astype(jnp.float32)
         up = up_ref[:, here].astype(jnp.float32)
         sig = jax.nn.sigmoid(gate)
         gate_out[:, here] = (grad * up * sig * (1.0 + gate * (1.0 - sig))).astype(jnp.bfloat16)
         up_out[:, here] = (grad * gate * sig).astype(jnp.bfloat16)
-
-
-def hidden_grads(index, cot, gate, up, held, weights, chunk=2):
-    blocks, span, size = weights.shape
+    if ahead:
+        load.wait()
+
+
+def hidden_grads(index, cot, gate, up, held, start, stop, earlier=(), weights=None, ahead=0):
+    _, span, size = held[0].shape
     rows = cot.shape[0]
-    left = blocks - held.shape[0]
-    return pl.pallas_call(
-        functools.partial(hidden_grad_kernel, chunk=chunk),
-        in_specs=[IN_SMEM] + [IN_VMEM] * 4 + [ANYWHERE],
-        out_specs=[IN_VMEM] * 2,
-        out_shape=[jax.ShapeDtypeStruct(gate.shape, gate.dtype)] * 2,
-        scratch_shapes=[
-            pltpu.VMEM((left, span, size), weights.dtype),
-            pltpu.SemaphoreType.DMA((left // chunk,)),
-        ],
-        compiler_params=pltpu.CompilerParams(vmem_limit_bytes=10 * 2**20),
+    shape = (rows, stop * size)
+    outs = [jax.ShapeDtypeStruct(shape, gate.dtype)] * 2
+    if ahead:
+        outs = [pltpu.VMEM(shape, gate.dtype)] * 2 + [pltpu.VMEM((ahead, span, size), weights.dtype)]
+    return pl.pallas_call(
+        functools.partial(
+            hidden_grad_kernel, start=start, fetched=len(held), earlier=len(earlier), ahead=ahead
+        ),
+        in_specs=[IN_SMEM] + [IN_VMEM] * (3 + len(held) + len(earlier)) + [ANYWHERE] * bool(ahead),
+        out_specs=[IN_VMEM] * len(outs),
+        out_shape=outs,
+        scratch_shapes=[pltpu.SemaphoreType.DMA] * bool(ahead),
+        compiler_params=pltpu.CompilerParams(vmem_limit_bytes=4 * 2**20),
         cost_estimate=pl.CostEstimate(
-            flops=2 * rows * blocks * span * size, bytes_accessed=2 * blocks * span * size, transcendentals=0
+            flops=2 * rows * (stop - start) * span * size,
+            bytes_accessed=2 * (stop - start) * span * size,
+            transcendentals=0,
         ),
         name="hidden_grads",
-    )(index, *map(resident, (cot, gate, up, held)), remaining(weights))
+    )(
+        index,
+        *map(resident, (cot, gate, up, *held, *earlier)),
+        *([remaining(weights)] if ahead else []),
+    )
+
+
+def pack_kernel(*refs, count):
+    pieces, out_ref = refs[:count], refs[-1]
+    rows = pieces[0].shape[0]
+    for i, piece in enumerate(pieces):
+        out_ref[i * rows : (i + 1) * rows, :] = piece[...]
+
+
+def pack(pieces, after):
+    rows, width = pieces[0].shape
+    return pl.pallas_call(
+        functools.partial(pack_kernel, count=len(pieces)),
+        in_specs=[IN_VMEM] * (len(pieces) + len(after)),
+        out_specs=IN_VMEM,
+        out_shape=pltpu.VMEM((len(pieces) * rows, width), pieces[0].dtype),
+        compiler_params=pltpu.CompilerParams(vmem_limit_bytes=4 * 2**20),
+        cost_estimate=pl.CostEstimate(flops=0, bytes_accessed=LONG, transcendentals=0),
+        name="pack",
+    )(*map(resident, pieces), *map(resident, after))
 
 
 def turn_kernel(*refs):
@@ -209,15 +244,19 @@
     )(*map(resident, pieces))
 
 
-def down_grad_kernel(index_ref, *refs, halves, pieces, kept, chunk, scale):
-    turned, hidden = refs[:halves], refs[halves : halves + pieces]
-    out_ref, held, sems = refs[halves + pieces :]
+def down_grad_kernel(index_ref, *refs, halves, groups, rows, kept, chunk, scale):
+    turned, hidden, (out_ref, held, sems) = refs[:halves], list(refs[halves:-3]), refs[-3:]
+    pieces = []
+    for count in groups:
+        group = [hidden.pop(0) for _ in range(count)]
+        pieces += [(h, i) for i in range(group[0].shape[0] // rows) for h in group]
     first = lax.axis_index("dp") * kept
     blocks = held.shape[0]
     copies = []
     for start in range(0, blocks, chunk):
         for block in range(start, start + chunk):
-            right = jnp.concatenate([h[:, block * 128 : (block + 1) * 128] for h in hidden], axis=0)
+            span = slice(block * 128, (block + 1) * 128)
+            right = jnp.concatenate([h[i * rows : (i + 1) * rows, span] for h, i in pieces], axis=0)
             left = jnp.concatenate(
                 [jnp.concatenate([t[index_ref[first + k, block]] for t in turned], axis=1) for k in range(kept)], axis=0
             )
@@ -230,25 +269,26 @@
         copy.wait()
 
 
-def down_grads(index, turned, hidden, kept, scale, chunk=4):
-    rows, width = hidden[0].shape
-    pieces = len(hidden)
+def down_grads(index, turned, hidden, rows, kept, scale, chunk=4):
+    width = hidden[0][0].shape[1]
+    arrays = [array for group in hidden for array in group]
+    tokens = sum(array.shape[0] for array in arrays)
     blocks = width // 128
     shape = (blocks, kept * 128, 128)
     return pl.pallas_call(
         functools.partial(
-            down_grad_kernel, halves=len(turned), pieces=pieces, kept=kept, chunk=chunk, scale=scale
+            down_grad_kernel, halves=len(turned), groups=list(map(len, hidden)), rows=rows, kept=kept, chunk=chunk, scale=scale
         ),
-        in_specs=[IN_SMEM] + [IN_VMEM] * (len(turned) + pieces),
+        in_specs=[IN_SMEM] + [IN_VMEM] * (len(turned) + len(arrays)),
         out_specs=ANYWHERE,
         out_shape=jax.ShapeDtypeStruct(shape, jnp.float32),
         scratch_shapes=[pltpu.VMEM(shape, jnp.float32), pltpu.SemaphoreType.DMA((blocks // chunk,))],
         compiler_params=pltpu.CompilerParams(vmem_limit_bytes=12 * 2**20),
         cost_estimate=pl.CostEstimate(
-            flops=2 * pieces * rows * kept * 128 * width, bytes_accessed=4 * kept * 128 * width, transcendentals=0
+            flops=2 * tokens * kept * 128 * width, bytes_accessed=4 * kept * 128 * width, transcendentals=0
         ),
         name="down_grads",
-    )(index, *map(resident, turned), *map(resident, hidden))
+    )(index, *map(resident, (*turned, *arrays)))
 
 
 def gathered(gate_act, up_act, cotangent, down_blocks, down_index):
@@ -262,29 +302,35 @@
     second = functools.partial(
         lax.ppermute, axis_name="dp", perm=[(i, i ^ (4 if i % 2 == 0 else 2)) for i in range(replicas)]
     )
+    across = functools.partial(lax.ppermute, axis_name="dp", perm=[(i, i ^ 6) for i in range(replicas)])
     other = functools.partial(lax.ppermute, axis_name="dp", perm=[(i, i ^ 1) for i in range(replicas)])
 
+    slices = [lax.ppermute(cotangent, "tensor", [(i, i ^ s) for i in range(parts)]) for s in range(1, parts)]
     hidden, gate, up, index, near = hidden_units(gate_act, up_act, down_index.T, cotangent)
-    h1, h2, h0x = first(hidden), second(hidden), other(hidden)
-    slices = [near] + [
-        lax.ppermute(cotangent, "tensor", [(i, i ^ s) for i in range(parts)]) for s in range(1, parts)
-    ]
-    held = fetch(down_blocks, 0, 20)
-    cot = assemble(slices, [h1, h2, held])
+    h1, h2 = first(hidden), second(hidden)
+    blocks = down_blocks.shape[0]
+    half = blocks // 2
+    ahead = blocks * 3 // 14
+    held = [fetch(down_blocks, 0, blocks - ahead)]
+    cot = assemble([near] + slices, [hidden, *held])
+    c1, c2 = first(cot), second(cot)
+    packed = pack([hidden, h1, h2], [cot])
     h3 = second(h1)
-    c1, c2, c0x = first(cot), second(cot), other(cot)
-    h1x, h2x = other(h1), other(h2)
-    grads = hidden_grads(index, cot, gate, up, held, down_blocks)
-    c1, c2, grads, h3 = lax.optimization_barrier((c1, c2, grads, h3))
-    gate_out, up_out = grads
+    packed_x, c0x = other(packed), other(cot)
+    *grads, rest = hidden_grads(index, cot, gate, up, held, 0, half, weights=down_blocks, ahead=ahead)
+    c1, c2, grads = lax.optimization_barrier((c1, c2, grads))
     c3 = second(c1)
-    c1x, c2x, h3x = other(c1), other(c2), other(h3)
+    c1x, c2x = other(c1), other(c2)
+    rest, h3 = lax.optimization_barrier((rest, h3))
+    h3x = other(h3)
+    grads = hidden_grads(index, cot, gate, up, held + [rest], half, blocks, grads)
     early = turn([cot, c0x, c1, c1x])
-    c3, early, h0x, h1x, h2x, h3x, c2x = lax.optimization_barrier((c3, early, h0x, h1x, h2x, h3x, c2x))
+    c3, early, c2x, h3x, packed_x, (gate_out, up_out) = lax.optimization_barrier(
+        (c3, early, c2x, h3x, packed_x, grads)
+    )
     c3x = other(c3)
     late = turn([c2, c2x, c3, c3x])
-    pieces = [hidden, h0x, h1, h1x, h2, h2x, h3, h3x]
-    down_grad = down_grads(index, [early, late], pieces, kept, 1.0 / replicas)
+    down_grad = down_grads(index, [early, late], [[packed, packed_x], [h3, h3x]], hidden.shape[0], kept, 1.0 / replicas)
     return down_grad.transpose(1, 0, 2), gate_out, up_out
 
 

time: 38.1 us -> 36.2 us (0.950)
  waiting for transfers between devices: 9.27 us -> 6.87 us
  Pallas kernels: 14.5 us -> 15.6 us
  starting transfers between devices: 13.6 us -> 12.8 us
    ppermute x1, waiting for transfers between devices: 2.89 us -> 0.87 us  [gathered(): c3 = second(c1)]
    ppermute x3, waiting for transfers between devices: 1.95 us -> 0.27 us  [gathered(): lax.ppermute(cotangent, 'tensor', [(i, i ^ s) for i in range(parts)])]
    ppermute x11 -> x9, waiting for transfers between devices: 1.72 us -> 2.91 us  [the longest x2 2.9 us: gathered(): c1, c2 = (first(cot), second(cot))]
    pallas_call x2 -> x4, Pallas kernels: 8.47 us -> 9.34 us  [the longest x2 6.46 us: hidden_grads(): pl.pallas_call(functools.partial(hidden_grad_kernel, start=start, fetched...]
    ppermute x11 -> x9, starting transfers between devices: 7.09 us -> 6.22 us  [the longest x2 4.52 us: gathered(): h1, h2 = (first(hidden), second(hidden))]
  transfers between devices with their start and end apart: 17 -> 15, of which waited for: 8 -> 5; matrix products, arithmetic and copies ran while one was open for 0% -> 0% of each run, Pallas kernels for 26% -> 31%
where the time goes in v3:
time: 36.2 us; the launch traced here: 36.1 us
  Pallas kernels  15.6 us (43%)
  starting transfers between devices  12.8 us (35%)
  waiting for transfers between devices  6.87 us (19%)
  between operations  0.74 us (2%)
    pallas_call x2, Pallas kernels, hidden_grads(): pl.pallas_call(functools.partial(hidden_grad_kernel, start=start, fetched...  6.46 us
    ppermute x2, starting transfers between devices, gathered(): h1, h2 = (first(hidden), second(hidden))  4.52 us
    pallas_call x1, Pallas kernels, fetch(): pl.pallas_call(functools.partial(fetch_kernel, start=start, chunk=chunk),...  4.39 us
    ppermute x3, starting transfers between devices, gathered(): lax.ppermute(cotangent, 'tensor', [(i, i ^ s) for i in range(parts)])  4.39 us
    ppermute x2, waiting for transfers between devices, gathered(): c1, c2 = (first(cot), second(cot))  2.9 us
    pallas_call x1, Pallas kernels, down_grads(): pl.pallas_call(functools.partial(down_grad_kernel, halves=len(turned), gr...  2.84 us
    ppermute x1, waiting for transfers between devices, gathered(): c3x = other(c3)  1.52 us
    ppermute x1, starting transfers between devices, gathered(): h3 = second(h1)  1.52 us
  transfers between devices with their start and end apart: 15, of which 5 were waited for; matrix products, arithmetic and copies ran while one was open for 0% of the time, Pallas kernels for 31%

profile of v3, /device:TPU:0, one launch (start us, length us, event | category | flops | bytes accessed | tf_op | source)
XLA Modules:
  0.0 36.1 jit_solution(694485794499606814)
XLA Ops:
  0.6 1.2 %hidden_units.1 = (bf16[32,3584]{1,0:T(8,128)(2,1)S(1)}, bf16[32,3584]{1,0:T(8,128)(2,1)S(1)}, bf16[32,3584]{1,0:T(8,128)(2,1)S(1)}, s32[16,28]{1,0:T(8,128)S(1)}, bf16[8,4096]{1,0:T(8,128)(2,1)S(1)}) custom-call(bf16[32,3584]{1,0:T(8,128)(2,1)} %refs_0_.1, bf16[32,3584]{1,0:T(8,128)(2,1)} %refs_1_.1, s32[16,28]{1,0:T(8,128)} %bitcast.3, bf16[8,4096]{1,0:T(8,128)(2,1)} %refs_3_.1), custom_call_target="tpu_custom_call" | custom-call | bytes 134217728 | tf_op jit(solution)/shard_map/hidden_units/pallas_call | solution.py:110
  1.9 3.0 %collective-permute-start.9 = (bf16[32,3584]{1,0:T(8,128)(2,1)S(1)}, bf16[32,3584]{1,0:T(8,128)(2,1)S(1)}, u32[]{:S(2)}, u32[]{:S(2)}) collective-permute-start(bf16[32,3584]{1,0:T(8,128)(2,1)S(1)} %get-tuple-element.28.refs_4_.refs_0_), channel_id=1, source_target_pairs={{0,8},{4,20},{8,0},{12,28},{16,24},{20,4},{24,16},{28,12},{1,9},{5... | collective-permute-start | bytes 688136 | tf_op jit(solution)/shard_map/ppermute | solution.py:310
  4.9 1.5 %collective-permute-start.12 = (bf16[32,3584]{1,0:T(8,128)(2,1)S(1)}, bf16[32,3584]{1,0:T(8,128)(2,1)S(1)}, u32[]{:S(2)}, u32[]{:S(2)}) collective-permute-start(bf16[32,3584]{1,0:T(8,128)(2,1)S(1)} %get-tuple-element.28.refs_4_.refs_0_), channel_id=1, source_target_pairs={{0,16},{4,12},{8,24},{12,4},{16,0},{20,28},{24,8},{28,20},{1,17},{... | collective-permute-start | bytes 688136 | tf_op jit(solution)/shard_map/ppermute | solution.py:310
  6.4 3.6 %collective-permute-start = (bf16[8,4096]{1,0:T(8,128)(2,1)}, bf16[8,4096]{1,0:T(8,128)(2,1)S(1)}, u32[]{:S(2)}, u32[]{:S(2)}) collective-permute-start(bf16[8,4096]{1,0:T(8,128)(2,1)} %refs_3_.1), channel_id=1, source_target_pairs={{0,3},{1,2},{2,1},{3,0},{4,7},{5,6},{6,5},{7,4},{8,11},{9,10},{10,... | collective-permute-start | bytes 196616 | tf_op jit(solution)/shard_map/ppermute | solution.py:308
  10.0 0.0 collective-permute-start.1
  10.0 0.8 %collective-permute-start.2 = (bf16[8,4096]{1,0:T(8,128)(2,1)}, bf16[8,4096]{1,0:T(8,128)(2,1)S(1)}, u32[]{:S(2)}, u32[]{:S(2)}) collective-permute-start(bf16[8,4096]{1,0:T(8,128)(2,1)} %refs_3_.1), channel_id=1, source_target_pairs={{0,1},{1,0},{2,3},{3,2},{4,5},{5,4},{6,7},{7,6},{8,9},{9,8},{10,11... | collective-permute-start | bytes 196616 | tf_op jit(solution)/shard_map/ppermute | solution.py:308
  10.8 4.4 %fetch.1.refs_5_.refs_4_ = bf16[22,2048,128]{2,1,0:T(8,128)(2,1)S(1)} custom-call(bf16[28,2048,128]{2,1,0:T(8,128)(2,1)} %refs_5_.1), custom_call_target="tpu_custom_call" | custom-call | bytes 5767168 | tf_op jit(solution)/shard_map/fetch/pallas_call | solution.py:136
  15.2 0.0 collective-permute-done.refs_0_
  15.2 0.3 collective-permute-done.1.refs_1_
  15.4 0.0 collective-permute-done.2.refs_2_
  15.4 0.1 assemble.1.refs_1_.refs_0_.refs_3_
  15.5 0.0 collective-permute-done.9.refs_1_
  15.5 0.0 collective-permute-done.12.refs_2_
  15.6 0.1 collective-permute-start.13
  15.7 0.6 %collective-permute-start.3 = (bf16[32,4096]{1,0:T(8,128)(2,1)S(1)}, bf16[32,4096]{1,0:T(8,128)(2,1)S(1)}, u32[]{:S(2)}, u32[]{:S(2)}) collective-permute-start(bf16[32,4096]{1,0:T(8,128)(2,1)S(1)} %assemble.1.refs_1_.refs_0_.refs_3_), channel_id=1, source_target_pairs={{0,8},{4,20},{8,0},{12,28},{16,24},{20,4},{24,16},{28,12},{1,9},{5... | collective-permute-start | bytes 786440 | tf_op jit(solution)/shard_map/ppermute | solution.py:316
  16.3 0.5 %collective-permute-start.4 = (bf16[32,4096]{1,0:T(8,128)(2,1)S(1)}, bf16[32,4096]{1,0:T(8,128)(2,1)S(1)}, u32[]{:S(2)}, u32[]{:S(2)}) collective-permute-start(bf16[32,4096]{1,0:T(8,128)(2,1)S(1)} %assemble.1.refs_1_.refs_0_.refs_3_), channel_id=1, source_target_pairs={{0,16},{4,12},{8,24},{12,4},{16,0},{20,28},{24,8},{28,20},{1,17},{... | collective-permute-start | bytes 786440 | tf_op jit(solution)/shard_map/ppermute | solution.py:316
  16.8 1.5 %collective-permute-start.10 = (bf16[32,3584]{1,0:T(8,128)(2,1)S(1)}, bf16[32,3584]{1,0:T(8,128)(2,1)S(1)}, u32[]{:S(2)}, u32[]{:S(2)}) collective-permute-start(bf16[32,3584]{1,0:T(8,128)(2,1)S(1)} %collective-permute-done.9.refs_1_), channel_id=1, source_target_pairs={{0,16},{4,12},{8,24},{12,4},{16,0},{20,28},{24,8},{28,20},{1,17},{... | collective-permute-start | bytes 688136 | tf_op jit(solution)/shard_map/ppermute | solution.py:318
  18.3 0.0 collective-permute-start.6
  18.3 3.7 %hidden_grads.2 = (bf16[32,1792]{1,0:T(8,128)(2,1)S(1)}, bf16[32,1792]{1,0:T(8,128)(2,1)S(1)}, bf16[6,2048,128]{2,1,0:T(8,128)(2,1)S(1)}) custom-call(s32[16,28]{1,0:T(8,128)S(1)} %get-tuple-element.26.refs_0_.index_ref, bf16[32,4096]{1,0:T(8,128)(2,1)S(1)} %assemble.1.refs_1_.refs_0_.refs_3_, bf16[32,3584]{1,0:T(8,128)(2,1)S(1)} %get-tuple-element.29.refs_2_, ...), custom_call_target="tpu_custom_call" | custom-call | flops 234881024 | bytes 7340032 | tf_op jit(solution)/shard_map/hidden_grads/pallas_call | solution.py:186
  22.0 2.9 %collective-permute-done.3.refs_2_ = bf16[32,4096]{1,0:T(8,128)(2,1)S(1)} collective-permute-done((bf16[32,4096]{1,0:T(8,128)(2,1)S(1)}, bf16[32,4096]{1,0:T(8,128)(2,1)S(1)}, u32[]{:S(2)}, u32[]{:S(2)}) %collective-permute-start.3) | collective-permute-done | bytes 262176 | tf_op jit(solution)/shard_map/ppermute | solution.py:316
  24.9 0.0 collective-permute-done.4.refs_0_
  24.9 0.0 collective-permute-start.7
  24.9 0.6 %collective-permute-start.5 = (bf16[32,4096]{1,0:T(8,128)(2,1)S(1)}, bf16[32,4096]{1,0:T(8,128)(2,1)S(1)}, u32[]{:S(2)}, u32[]{:S(2)}) collective-permute-start(bf16[32,4096]{1,0:T(8,128)(2,1)S(1)} %collective-permute-done.3.refs_2_), channel_id=1, source_target_pairs={{0,16},{4,12},{8,24},{12,4},{16,0},{20,28},{24,8},{28,20},{1,17},{... | collective-permute-start | bytes 786440 | tf_op jit(solution)/shard_map/ppermute | solution.py:322
  25.5 1.3 %collective-permute-done.10.refs_4_ = bf16[32,3584]{1,0:T(8,128)(2,1)S(1)} collective-permute-done((bf16[32,3584]{1,0:T(8,128)(2,1)S(1)}, bf16[32,3584]{1,0:T(8,128)(2,1)S(1)}, u32[]{:S(2)}, u32[]{:S(2)}) %collective-permute-start.10) | collective-permute-done | bytes 229408 | tf_op jit(solution)/shard_map/ppermute | solution.py:318
  26.8 0.1 collective-permute-start.8
  26.9 0.0 collective-permute-done.6.refs_1_
  26.9 0.4 %collective-permute-start.11 = (bf16[32,3584]{1,0:T(8,128)(2,1)S(1)}, bf16[32,3584]{1,0:T(8,128)(2,1)S(1)}, u32[]{:S(2)}, u32[]{:S(2)}) collective-permute-start(bf16[32,3584]{1,0:T(8,128)(2,1)S(1)} %collective-permute-done.10.refs_4_), channel_id=1, source_target_pairs={{0,4},{4,0},{8,12},{12,8},{16,20},{20,16},{24,28},{28,24},{1,5},{5... | collective-permute-start | bytes 688136 | tf_op jit(solution)/shard_map/ppermute | solution.py:325
  27.3 2.7 %hidden_grads.3 = (bf16[32,3584]{1,0:T(8,128)(2,1)}, bf16[32,3584]{1,0:T(8,128)(2,1)}) custom-call(s32[16,28]{1,0:T(8,128)S(1)} %get-tuple-element.26.refs_0_.index_ref, bf16[32,4096]{1,0:T(8,128)(2,1)S(1)} %assemble.1.refs_1_.refs_0_.refs_3_, bf16[32,3584]{1,0:T(8,128)(2,1)S(1)} %get-tuple-element.29.refs_2_, ...), custom_call_target="tpu_custom_call" | custom-call | flops 234881024 | bytes 7340032 | tf_op jit(solution)/shard_map/hidden_grads/pallas_call | solution.py:186
  30.1 0.0 collective-permute-done.7.refs_3_
  30.1 0.3 turn.2.refs_0_
  30.4 0.9 %collective-permute-done.5.refs_2_ = bf16[32,4096]{1,0:T(8,128)(2,1)S(1)} collective-permute-done((bf16[32,4096]{1,0:T(8,128)(2,1)S(1)}, bf16[32,4096]{1,0:T(8,128)(2,1)S(1)}, u32[]{:S(2)}, u32[]{:S(2)}) %collective-permute-start.5) | collective-permute-done | bytes 262176 | tf_op jit(solution)/shard_map/ppermute | solution.py:322
  31.3 0.0 collective-permute-done.8.refs_1_
  31.3 0.0 collective-permute-done.11.refs_5_
  31.3 0.0 collective-permute-done.13.refs_3_
  31.3 0.1 collective-permute-start.14
  31.4 1.5 %collective-permute-done.14.refs_3_ = bf16[32,4096]{1,0:T(8,128)(2,1)S(1)} collective-permute-done((bf16[32,4096]{1,0:T(8,128)(2,1)S(1)}, bf16[32,4096]{1,0:T(8,128)(2,1)S(1)}, u32[]{:S(2)}, u32[]{:S(2)}) %collective-permute-start.14) | collective-permute-done | bytes 262176 | tf_op jit(solution)/shard_map/ppermute | solution.py:331
  32.9 0.3 turn.3.refs_1_
  33.2 2.8 %down_grads.1 = f32[28,256,128]{2,1,0:T(8,128)} custom-call(s32[16,28]{1,0:T(8,128)S(1)} %get-tuple-element.26.refs_0_.index_ref, bf16[32,128,128]{2,1,0:T(8,128)(2,1)S(1)} %turn.2.refs_0_, bf16[32,128,128]{2,1,0:T(8,128)(2,1)S(1)} %turn.3.refs_1_, bf16[96,3584]{1,0:T(8,128)(2,1)S(1)} %pack.1.refs_2_, bf16[96,3584]{1,0:T(8,128)(2,1)S(1)} %collective-permute-done.13.refs_3_, ...), custom_call_target="tpu_custom_call" | custom-call | flops 469762048 | bytes 3670016 | tf_op jit(solution)/shard_map/down_grads/pallas_call | solution.py:278
  (1 shorter events, 0.0 us)
Async XLA Ops:
  1.9 13.7 %collective-permute-start.9 = (bf16[32,3584]{1,0:T(8,128)(2,1)S(1)}, bf16[32,3584]{1,0:T(8,128)(2,1)S(1)}, u32[]{:S(2)}, u32[]{:S(2)}) collective-permute-start(bf16[32,3584]{1,0:T(8,128)(2,1)S(1)} %get-tuple-element.28.refs_4_.refs_0_), channel_id=1, source_target_pairs={{0,8},{4,20},{8,0},{12,28},{16,24},{20,4},{24,16},{28,12},{1,9},{5... | collective-permute-start | bytes 688136 | tf_op jit(solution)/shard_map/ppermute | solution.py:310
  4.9 10.7 %collective-permute-start.12 = (bf16[32,3584]{1,0:T(8,128)(2,1)S(1)}, bf16[32,3584]{1,0:T(8,128)(2,1)S(1)}, u32[]{:S(2)}, u32[]{:S(2)}) collective-permute-start(bf16[32,3584]{1,0:T(8,128)(2,1)S(1)} %get-tuple-element.28.refs_4_.refs_0_), channel_id=1, source_target_pairs={{0,16},{4,12},{8,24},{12,4},{16,0},{20,28},{24,8},{28,20},{1,17},{... | collective-permute-start | bytes 688136 | tf_op jit(solution)/shard_map/ppermute | solution.py:310
  6.4 8.8 %collective-permute-start = (bf16[8,4096]{1,0:T(8,128)(2,1)}, bf16[8,4096]{1,0:T(8,128)(2,1)S(1)}, u32[]{:S(2)}, u32[]{:S(2)}) collective-permute-start(bf16[8,4096]{1,0:T(8,128)(2,1)} %refs_3_.1), channel_id=1, source_target_pairs={{0,3},{1,2},{2,1},{3,0},{4,7},{5,6},{6,5},{7,4},{8,11},{9,10},{10,... | collective-permute-start | bytes 196616 | tf_op jit(solution)/shard_map/ppermute | solution.py:308
  10.0 5.5 %collective-permute-start.1 = (bf16[8,4096]{1,0:T(8,128)(2,1)}, bf16[8,4096]{1,0:T(8,128)(2,1)S(1)}, u32[]{:S(2)}, u32[]{:S(2)}) collective-permute-start(bf16[8,4096]{1,0:T(8,128)(2,1)} %refs_3_.1), channel_id=1, source_target_pairs={{0,2},{1,3},{2,0},{3,1},{4,6},{5,7},{6,4},{7,5},{8,10},{9,11},{10,... | collective-permute-start | bytes 196616 | tf_op jit(solution)/shard_map/ppermute | solution.py:308
  10.0 5.5 %collective-permute-start.2 = (bf16[8,4096]{1,0:T(8,128)(2,1)}, bf16[8,4096]{1,0:T(8,128)(2,1)S(1)}, u32[]{:S(2)}, u32[]{:S(2)}) collective-permute-start(bf16[8,4096]{1,0:T(8,128)(2,1)} %refs_3_.1), channel_id=1, source_target_pairs={{0,1},{1,0},{2,3},{3,2},{4,5},{5,4},{6,7},{7,6},{8,9},{9,8},{10,11... | collective-permute-start | bytes 196616 | tf_op jit(solution)/shard_map/ppermute | solution.py:308
  15.6 15.7 %collective-permute-start.13 = (bf16[96,3584]{1,0:T(8,128)(2,1)S(1)}, bf16[96,3584]{1,0:T(8,128)(2,1)S(1)}, u32[]{:S(2)}, u32[]{:S(2)}) collective-permute-start(bf16[96,3584]{1,0:T(8,128)(2,1)S(1)} %pack.1.refs_2_), channel_id=1, source_target_pairs={{0,4},{4,0},{8,12},{12,8},{16,20},{20,16},{24,28},{28,24},{1,5},{5... | collective-permute-start | bytes 2064392 | tf_op jit(solution)/shard_map/ppermute | solution.py:319
  15.7 9.2 %collective-permute-start.3 = (bf16[32,4096]{1,0:T(8,128)(2,1)S(1)}, bf16[32,4096]{1,0:T(8,128)(2,1)S(1)}, u32[]{:S(2)}, u32[]{:S(2)}) collective-permute-start(bf16[32,4096]{1,0:T(8,128)(2,1)S(1)} %assemble.1.refs_1_.refs_0_.refs_3_), channel_id=1, source_target_pairs={{0,8},{4,20},{8,0},{12,28},{16,24},{20,4},{24,16},{28,12},{1,9},{5... | collective-permute-start | bytes 786440 | tf_op jit(solution)/shard_map/ppermute | solution.py:316
  16.3 8.6 %collective-permute-start.4 = (bf16[32,4096]{1,0:T(8,128)(2,1)S(1)}, bf16[32,4096]{1,0:T(8,128)(2,1)S(1)}, u32[]{:S(2)}, u32[]{:S(2)}) collective-permute-start(bf16[32,4096]{1,0:T(8,128)(2,1)S(1)} %assemble.1.refs_1_.refs_0_.refs_3_), channel_id=1, source_target_pairs={{0,16},{4,12},{8,24},{12,4},{16,0},{20,28},{24,8},{28,20},{1,17},{... | collective-permute-start | bytes 786440 | tf_op jit(solution)/shard_map/ppermute | solution.py:316
  16.8 10.1 %collective-permute-start.10 = (bf16[32,3584]{1,0:T(8,128)(2,1)S(1)}, bf16[32,3584]{1,0:T(8,128)(2,1)S(1)}, u32[]{:S(2)}, u32[]{:S(2)}) collective-permute-start(bf16[32,3584]{1,0:T(8,128)(2,1)S(1)} %collective-permute-done.9.refs_1_), channel_id=1, source_target_pairs={{0,16},{4,12},{8,24},{12,4},{16,0},{20,28},{24,8},{28,20},{1,17},{... | collective-permute-start | bytes 688136 | tf_op jit(solution)/shard_map/ppermute | solution.py:318
  18.3 8.7 %collective-permute-start.6 = (bf16[32,4096]{1,0:T(8,128)(2,1)S(1)}, bf16[32,4096]{1,0:T(8,128)(2,1)S(1)}, u32[]{:S(2)}, u32[]{:S(2)}) collective-permute-start(bf16[32,4096]{1,0:T(8,128)(2,1)S(1)} %assemble.1.refs_1_.refs_0_.refs_3_), channel_id=1, source_target_pairs={{0,4},{4,0},{8,12},{12,8},{16,20},{20,16},{24,28},{28,24},{1,5},{5... | collective-permute-start | bytes 786440 | tf_op jit(solution)/shard_map/ppermute | solution.py:319
  24.9 5.2 %collective-permute-start.7 = (bf16[32,4096]{1,0:T(8,128)(2,1)S(1)}, bf16[32,4096]{1,0:T(8,128)(2,1)S(1)}, u32[]{:S(2)}, u32[]{:S(2)}) collective-permute-start(bf16[32,4096]{1,0:T(8,128)(2,1)S(1)} %collective-permute-done.3.refs_2_), channel_id=1, source_target_pairs={{0,4},{4,0},{8,12},{12,8},{16,20},{20,16},{24,28},{28,24},{1,5},{5... | collective-permute-start | bytes 786440 | tf_op jit(solution)/shard_map/ppermute | solution.py:323
  24.9 6.4 %collective-permute-start.5 = (bf16[32,4096]{1,0:T(8,128)(2,1)S(1)}, bf16[32,4096]{1,0:T(8,128)(2,1)S(1)}, u32[]{:S(2)}, u32[]{:S(2)}) collective-permute-start(bf16[32,4096]{1,0:T(8,128)(2,1)S(1)} %collective-permute-done.3.refs_2_), channel_id=1, source_target_pairs={{0,16},{4,12},{8,24},{12,4},{16,0},{20,28},{24,8},{28,20},{1,17},{... | collective-permute-start | bytes 786440 | tf_op jit(solution)/shard_map/ppermute | solution.py:322
  26.8 4.5 %collective-permute-start.8 = (bf16[32,4096]{1,0:T(8,128)(2,1)S(1)}, bf16[32,4096]{1,0:T(8,128)(2,1)S(1)}, u32[]{:S(2)}, u32[]{:S(2)}) collective-permute-start(bf16[32,4096]{1,0:T(8,128)(2,1)S(1)} %collective-permute-done.4.refs_0_), channel_id=1, source_target_pairs={{0,4},{4,0},{8,12},{12,8},{16,20},{20,16},{24,28},{28,24},{1,5},{5... | collective-permute-start | bytes 786440 | tf_op jit(solution)/shard_map/ppermute | solution.py:323
  26.9 4.3 %collective-permute-start.11 = (bf16[32,3584]{1,0:T(8,128)(2,1)S(1)}, bf16[32,3584]{1,0:T(8,128)(2,1)S(1)}, u32[]{:S(2)}, u32[]{:S(2)}) collective-permute-start(bf16[32,3584]{1,0:T(8,128)(2,1)S(1)} %collective-permute-done.10.refs_4_), channel_id=1, source_target_pairs={{0,4},{4,0},{8,12},{12,8},{16,20},{20,16},{24,28},{28,24},{1,5},{5... | collective-permute-start | bytes 688136 | tf_op jit(solution)/shard_map/ppermute | solution.py:325
  31.3 1.6 %collective-permute-start.14 = (bf16[32,4096]{1,0:T(8,128)(2,1)S(1)}, bf16[32,4096]{1,0:T(8,128)(2,1)S(1)}, u32[]{:S(2)}, u32[]{:S(2)}) collective-permute-start(bf16[32,4096]{1,0:T(8,128)(2,1)S(1)} %collective-permute-done.5.refs_2_), channel_id=1, source_target_pairs={{0,4},{4,0},{8,12},{12,8},{16,20},{20,16},{24,28},{28,24},{1,5},{5... | collective-permute-start | bytes 786440 | tf_op jit(solution)/shard_map/ppermute | solution.py:331

commit v4 on v3

--- a/solution.py
+++ b/solution.py
@@ -65,12 +65,16 @@
     return pltpu.with_memory_space_constraint(array, pltpu.VMEM)
 
 
+def scalar(array):
+    return pltpu.with_memory_space_constraint(array, pltpu.SMEM)
+
+
 def remaining(array):
     return pltpu.with_memory_space_constraint(array, pltpu.HBM)
 
 
 def assemble_kernel(*refs, parts):
-    pieces, out_ref = refs[:parts][::-1], refs[-1]
+    pieces, (out_ref, sent_ref) = refs[:parts][::-1], refs[-2:]
     here = lax.axis_index("tensor")
     for place in range(parts):
 
@@ -78,15 +82,25 @@
         def _():
             out_ref[...] = jnp.concatenate([pieces[place ^ q][...] for q in range(parts)], axis=0)
 
+    width = out_ref.shape[1]
+    sent_ref[:, :width] = jnp.concatenate([piece[...] for piece in pieces[2:]], axis=0)
+    sent_ref[:, width:] = stacked(pieces[1][...])
+
+
+def stacked(rows):
+    half = rows.shape[1] // 2
+    return jnp.concatenate([rows[:, :half], rows[:, half:]], axis=0)
+
 
 def assemble(pieces, after):
     rows, width = pieces[0].shape
     parts = len(pieces)
+    dtype = pieces[0].dtype
     return pl.pallas_call(
         functools.partial(assemble_kernel, parts=parts),
         in_specs=[IN_VMEM] * (parts + len(after)),
-        out_specs=IN_VMEM,
-        out_shape=pltpu.VMEM((parts * rows, width), pieces[0].dtype),
+        out_specs=[IN_VMEM] * 2,
+        out_shape=[pltpu.VMEM((parts * rows, width), dtype), pltpu.VMEM((2 * rows, width * 3 // 2), dtype)],
         compiler_params=pltpu.CompilerParams(vmem_limit_bytes=4 * 2**20),
         cost_estimate=pl.CostEstimate(flops=0, bytes_accessed=LONG, transcendentals=0),
         name="assemble",
@@ -94,7 +108,7 @@
 
 
 def hidden_kernel(*refs, kept):
-    sources, hidden_ref, targets, sems = refs[:kept], refs[kept], refs[kept + 1 : -1], refs[-1]
+    sources, message_ref, targets, (hidden, sems) = refs[:kept], refs[kept], refs[kept + 1 : -2], refs[-2:]
     loads = [pltpu.make_async_copy(source, target, sems.at[i]) for i, (source, target) in enumerate(zip(sources, targets))]
     for load in loads:
         load.start()
@@ -102,19 +116,37 @@
         load.wait()
     gate = targets[0][...].astype(jnp.float32)
     up = targets[1][...].astype(jnp.float32)
-    hidden_ref[...] = (gate * jax.nn.sigmoid(gate) * up).astype(hidden_ref.dtype)
+    hidden[...] = gate * jax.nn.sigmoid(gate) * up
+    rows, width = hidden.shape
+    cot = targets[-1]
+    size = cot.shape[0]
+    parts = rows // size
+    here = lax.axis_index("tensor")
+    for place in range(parts):
+
+        @pl.when(here == place)
+        def _():
+            groups = [hidden[(place ^ j) * size : ((place ^ j) + 1) * size, :] for j in range(parts)]
+            for i in range(parts // 2):
+                pair = jnp.concatenate(groups[2 * i : 2 * i + 2], axis=0)
+                message_ref[:, i * width : (i + 1) * width] = pair.astype(message_ref.dtype)
+
+    message_ref[:, rows * width // (2 * size) :] = stacked(cot[...])
 
 
 def hidden_units(*arrays):
-    outs = [pltpu.VMEM(array.shape, array.dtype) for array in arrays]
+    gate, cot = arrays[0], arrays[-1]
+    spaces = [pltpu.SMEM if array.dtype == jnp.int32 else pltpu.VMEM for array in arrays]
+    outs = [space(array.shape, array.dtype) for space, array in zip(spaces, arrays)]
+    rows = 2 * cot.shape[0]
+    message = pltpu.VMEM((rows, (gate.size + cot.size) // rows), gate.dtype)
     return pl.pallas_call(
         functools.partial(hidden_kernel, kept=len(arrays)),
         in_specs=[ANYWHERE] * len(arrays),
-        out_specs=[IN_VMEM] * (1 + len(arrays)),
-        out_shape=[outs[0]] + outs,
-        scratch_shapes=[pltpu.SemaphoreType.DMA((len(arrays),))],
-        compiler_params=pltpu.CompilerParams(vmem_limit_bytes=4 * 2**20),
-        cost_estimate=pl.CostEstimate(flops=0, bytes_accessed=LONG, transcendentals=0),
+        out_specs=[IN_VMEM] + [pl.BlockSpec(memory_space=space) for space in spaces],
+        out_shape=[message] + outs,
+        scratch_shapes=[pltpu.VMEM(gate.shape, jnp.float32), pltpu.SemaphoreType.DMA((len(arrays),))],
+        compiler_params=pltpu.CompilerParams(vmem_limit_bytes=4 * 2**20),
         name="hidden_units",
     )(*map(remaining, arrays))
 
@@ -199,7 +231,7 @@
         ),
         name="hidden_grads",
     )(
-        index,
+        scalar(index),
         *map(resident, (cot, gate, up, *held, *earlier)),
         *([remaining(weights)] if ahead else []),
     )
@@ -225,38 +257,54 @@
     )(*map(resident, pieces), *map(resident, after))
 
 
-def turn_kernel(*refs):
-    pieces, out_ref = refs[:-1], refs[-1]
-    for d in range(out_ref.shape[0]):
-        span = slice(d * 128, (d + 1) * 128)
-        out_ref[d] = jnp.concatenate([piece[:, span] for piece in pieces], axis=0).T
-
-
-def turn(pieces):
-    rows, width = pieces[0].shape
-    return pl.pallas_call(
-        turn_kernel,
-        in_specs=[IN_VMEM] * len(pieces),
+def turn_kernel(*refs, places, rows):
+    out_ref = refs[-1]
+    features = out_ref.shape[0]
+    per_half = features // 2
+    for d in range(features):
+        slices = []
+        low, column = (d // per_half) * rows, (d % per_half) * 128
+        for (i, i_row), (j, j_row) in places:
+            start = refs[i].shape[1] - per_half * 128 + column
+            own = refs[i][i_row : i_row + 2 * rows, start : start + 128]
+            start = features * 128 + column
+            near = refs[j][j_row : j_row + 2 * rows, start : start + 128]
+            slices += [own[low : low + rows], near[low : low + rows]]
+            slices.append(refs[j][j_row : j_row + 2 * rows, d * 128 : (d + 1) * 128])
+        out_ref[d] = jnp.concatenate(slices, axis=0).T
+
+
+def turn(pieces, rows):
+    arrays = []
+    for piece in pieces:
+        arrays += [array for array, _ in piece if not any(array is other for other in arrays)]
+    places = [[([array is other for other in arrays].index(True), row) for array, row in piece] for piece in pieces]
+    width = pieces[0][1][0].shape[1] * 2 // 3
+    return pl.pallas_call(
+        functools.partial(turn_kernel, places=places, rows=rows),
+        in_specs=[IN_VMEM] * len(arrays),
         out_specs=IN_VMEM,
-        out_shape=pltpu.VMEM((width // 128, 128, len(pieces) * rows), pieces[0].dtype),
+        out_shape=pltpu.VMEM((width // 128, 128, len(pieces) * 4 * rows), arrays[0].dtype),
         compiler_params=pltpu.CompilerParams(vmem_limit_bytes=4 * 2**20),
         name="turn",
-    )(*map(resident, pieces))
-
-
-def down_grad_kernel(index_ref, *refs, halves, groups, rows, kept, chunk, scale):
-    turned, hidden, (out_ref, held, sems) = refs[:halves], list(refs[halves:-3]), refs[-3:]
-    pieces = []
-    for count in groups:
-        group = [hidden.pop(0) for _ in range(count)]
-        pieces += [(h, i) for i in range(group[0].shape[0] // rows) for h in group]
+    )(*map(resident, arrays))
+
+
+def down_grad_kernel(index_ref, *refs, halves, places, rows, kept, chunk, scale):
+    turned, messages, (out_ref, held, sems) = refs[:halves], refs[halves:-3], refs[-3:]
     first = lax.axis_index("dp") * kept
     blocks = held.shape[0]
     copies = []
     for start in range(0, blocks, chunk):
         for block in range(start, start + chunk):
-            span = slice(block * 128, (block + 1) * 128)
-            right = jnp.concatenate([h[i * rows : (i + 1) * rows, span] for h, i in pieces], axis=0)
+            right = jnp.concatenate(
+                [
+                    messages[i][row : row + rows, column * 128 : (column + 1) * 128]
+                    for i, row in places
+                    for column in (block, blocks + block)
+                ],
+                axis=0,
+            )
             left = jnp.concatenate(
                 [jnp.concatenate([t[index_ref[first + k, block]] for t in turned], axis=1) for k in range(kept)], axis=0
             )
@@ -269,15 +317,15 @@
         copy.wait()
 
 
-def down_grads(index, turned, hidden, rows, kept, scale, chunk=4):
-    width = hidden[0][0].shape[1]
-    arrays = [array for group in hidden for array in group]
-    tokens = sum(array.shape[0] for array in arrays)
-    blocks = width // 128
+def down_grads(index, turned, messages, blocks, rows, kept, scale, chunk=4):
+    arrays = []
+    for array, _ in messages:
+        arrays += [array] * (not any(array is other for other in arrays))
+    places = [([array is other for other in arrays].index(True), row) for array, row in messages]
     shape = (blocks, kept * 128, 128)
     return pl.pallas_call(
         functools.partial(
-            down_grad_kernel, halves=len(turned), groups=list(map(len, hidden)), rows=rows, kept=kept, chunk=chunk, scale=scale
+            down_grad_kernel, halves=len(turned), places=places, rows=rows, kept=kept, chunk=chunk, scale=scale
         ),
         in_specs=[IN_SMEM] + [IN_VMEM] * (len(turned) + len(arrays)),
         out_specs=ANYWHERE,
@@ -285,10 +333,12 @@
         scratch_shapes=[pltpu.VMEM(shape, jnp.float32), pltpu.SemaphoreType.DMA((blocks // chunk,))],
         compiler_params=pltpu.CompilerParams(vmem_limit_bytes=12 * 2**20),
         cost_estimate=pl.CostEstimate(
-            flops=2 * tokens * kept * 128 * width, bytes_accessed=4 * kept * 128 * width, transcendentals=0
+            flops=4 * len(messages) * rows * kept * 128 * blocks * 128,
+            bytes_accessed=4 * kept * blocks * 128 * 128,
+            transcendentals=0,
         ),
         name="down_grads",
-    )(index, *map(resident, (*turned, *arrays)))
+    )(scalar(index), *map(resident, (*turned, *arrays)))
 
 
 def gathered(gate_act, up_act, cotangent, down_blocks, down_index):
@@ -305,32 +355,33 @@
     across = functools.partial(lax.ppermute, axis_name="dp", perm=[(i, i ^ 6) for i in range(replicas)])
     other = functools.partial(lax.ppermute, axis_name="dp", perm=[(i, i ^ 1) for i in range(replicas)])
 
-    slices = [lax.ppermute(cotangent, "tensor", [(i, i ^ s) for i in range(parts)]) for s in range(1, parts)]
-    hidden, gate, up, index, near = hidden_units(gate_act, up_act, down_index.T, cotangent)
-    h1, h2 = first(hidden), second(hidden)
+    message, gate, up, index, near = hidden_units(gate_act, up_act, down_index.T, cotangent)
+    rows = message.shape[0]
+    m1, m2 = first(message), second(message)
+    slices = [lax.ppermute(near, "tensor", [(i, i ^ s) for i in range(parts)]) for s in range(1, parts)]
     blocks = down_blocks.shape[0]
     half = blocks // 2
     ahead = blocks * 3 // 14
     held = [fetch(down_blocks, 0, blocks - ahead)]
-    cot = assemble([near] + slices, [hidden, *held])
-    c1, c2 = first(cot), second(cot)
-    packed = pack([hidden, h1, h2], [cot])
-    h3 = second(h1)
-    packed_x, c0x = other(packed), other(cot)
+    cot, sent = assemble([near] + slices, held)
+    c1, c2 = first(sent), second(sent)
+    packed = pack([message, m1, m2], [cot])
+    m3 = second(m1)
+    packed_x, c0x = other(packed), other(sent)
     *grads, rest = hidden_grads(index, cot, gate, up, held, 0, half, weights=down_blocks, ahead=ahead)
     c1, c2, grads = lax.optimization_barrier((c1, c2, grads))
     c3 = second(c1)
     c1x, c2x = other(c1), other(c2)
-    rest, h3 = lax.optimization_barrier((rest, h3))
-    h3x = other(h3)
     grads = hidden_grads(index, cot, gate, up, held + [rest], half, blocks, grads)
-    early = turn([cot, c0x, c1, c1x])
-    c3, early, c2x, h3x, packed_x, (gate_out, up_out) = lax.optimization_barrier(
-        (c3, early, c2x, h3x, packed_x, grads)
-    )
-    c3x = other(c3)
-    late = turn([c2, c2x, c3, c3x])
-    down_grad = down_grads(index, [early, late], [[packed, packed_x], [h3, h3x]], hidden.shape[0], kept, 1.0 / replicas)
+    messages = [(array, i * rows) for i in range(3) for array in (packed, packed_x)]
+    early = turn(list(zip(messages[:4], [(sent, 0), (c0x, 0), (c1, 0), (c1x, 0)])), rows // 2)
+    c3, m3, early, c2x, packed_x, (gate_out, up_out) = lax.optimization_barrier(
+        (c3, m3, early, c2x, packed_x, grads)
+    )
+    m3x, c3x = other(m3), other(c3)
+    messages = [(array, i * rows) for i in range(3) for array in (packed, packed_x)] + [(m3, 0), (m3x, 0)]
+    late = turn(list(zip(messages[4:], [(c2, 0), (c2x, 0), (c3, 0), (c3x, 0)])), rows // 2)
+    down_grad = down_grads(index, [early, late], messages, blocks, rows, kept, 1.0 / replicas)
     return down_grad.transpose(1, 0, 2), gate_out, up_out
 
 

time: 36.2 us -> 34.1 us (0.942)
  Pallas kernels: 15.6 us -> 13.7 us
    ppermute x12, waiting for transfers between devices: 5.99 us -> 3.6 us  [the longest x2 2.17 us: gathered(): c1, c2 = (first(sent), second(sent))]
    ppermute x1, waiting for transfers between devices: 0.87 us -> 3.16 us  [gathered(): c3 = second(c1)]
    pallas_call x2, Pallas kernels: 6.46 us -> 5.08 us  [hidden_grads(): pl.pallas_call(functools.partial(hidden_grad_kernel, start=start, fetched...]
    pallas_call x3, Pallas kernels: 3.49 us -> 2.83 us  [the longest x1 2.18 us: down_grads(): pl.pallas_call(functools.partial(down_grad_kernel, halves=len(turned), pl...]
    ppermute x1, starting transfers between devices: 0.62 us -> 0.12 us  [gathered(): c3 = second(c1)]
    ppermute x2, starting transfers between devices: 0.12 us -> 0.51 us  [gathered(): c1x, c2x = (other(c1), other(c2))]
  transfers between devices with their start and end apart: 15 -> 15, of which waited for: 5 -> 4; matrix products, arithmetic and copies ran while one was open for 0% -> 0% of each run, Pallas kernels for 31% -> 29%
where the time goes in v4:
time: 34.1 us; the launch traced here: 33.9 us
  Pallas kernels  13.7 us (40%)
  starting transfers between devices  12.7 us (37%)
  waiting for transfers between devices  6.77 us (20%)
  between operations  0.73 us (2%)
    pallas_call x2, Pallas kernels, hidden_grads(): pl.pallas_call(functools.partial(hidden_grad_kernel, start=start, fetched...  5.08 us
    ppermute x2, starting transfers between devices, gathered(): m1, m2 = (first(message), second(message))  4.52 us
    pallas_call x1, Pallas kernels, fetch(): pl.pallas_call(functools.partial(fetch_kernel, start=start, chunk=chunk),...  4.39 us
    ppermute x3, starting transfers between devices, gathered(): lax.ppermute(near, 'tensor', [(i, i ^ s) for i in range(parts)])  4.39 us
    ppermute x1, waiting for transfers between devices, gathered(): c3 = second(c1)  3.16 us
    pallas_call x1, Pallas kernels, down_grads(): pl.pallas_call(functools.partial(down_grad_kernel, halves=len(turned), pl...  2.18 us
    ppermute x2, waiting for transfers between devices, gathered(): c1, c2 = (first(sent), second(sent))  2.17 us
    ppermute x1, starting transfers between devices, gathered(): m3 = second(m1)  1.52 us
  transfers between devices with their start and end apart: 15, of which 4 were waited for; matrix products, arithmetic and copies ran while one was open for 0% of the time, Pallas kernels for 29%

profile of v4, /device:TPU:0, one launch (start us, length us, event | category | flops | bytes accessed | tf_op | source)
XLA Modules:
  0.0 33.9 jit_solution(611266240246346060)
XLA Ops:
  0.6 1.2 %hidden_units.1 = (bf16[16,9216]{1,0:T(8,128)(2,1)S(1)}, bf16[32,3584]{1,0:T(8,128)(2,1)S(1)}, bf16[32,3584]{1,0:T(8,128)(2,1)S(1)}, s32[16,28]{1,0:T(8,128)S(4)}, bf16[8,4096]{1,0:T(8,128)(2,1)S(1)}) custom-call(bf16[32,3584]{1,0:T(8,128)(2,1)} %refs_0_.1, bf16[32,3584]{1,0:T(8,128)(2,1)} %refs_1_.1, s32[16,28]{1,0:T(8,128)} %bitcast.3, bf16[8,4096]{1,0:T(8,128)(2,1)} %refs_3_.1), custom_call_target="tpu_custom_call" | custom-call | tf_op jit(solution)/shard_map/hidden_units/pallas_call | solution.py:143
  1.9 3.0 %collective-permute-start.6 = (bf16[16,9216]{1,0:T(8,128)(2,1)S(1)}, bf16[16,9216]{1,0:T(8,128)(2,1)S(1)}, u32[]{:S(2)}, u32[]{:S(2)}) collective-permute-start(bf16[16,9216]{1,0:T(8,128)(2,1)S(1)} %get-tuple-element.35.refs_0_), channel_id=1, source_target_pairs={{0,8},{4,20},{8,0},{12,28},{16,24},{20,4},{24,16},{28,12},{1,9},{5... | collective-permute-start | bytes 884744 | tf_op jit(solution)/shard_map/ppermute | solution.py:360
  4.9 1.5 %collective-permute-start.8 = (bf16[16,9216]{1,0:T(8,128)(2,1)S(1)}, bf16[16,9216]{1,0:T(8,128)(2,1)S(1)}, u32[]{:S(2)}, u32[]{:S(2)}) collective-permute-start(bf16[16,9216]{1,0:T(8,128)(2,1)S(1)} %get-tuple-element.35.refs_0_), channel_id=1, source_target_pairs={{0,16},{4,12},{8,24},{12,4},{16,0},{20,28},{24,8},{28,20},{1,17},{... | collective-permute-start | bytes 884744 | tf_op jit(solution)/shard_map/ppermute | solution.py:360
  6.4 3.6 %collective-permute-start = (bf16[8,4096]{1,0:T(8,128)(2,1)S(1)}, bf16[8,4096]{1,0:T(8,128)(2,1)S(1)}, u32[]{:S(2)}, u32[]{:S(2)}) collective-permute-start(bf16[8,4096]{1,0:T(8,128)(2,1)S(1)} %get-tuple-element.27.refs_3_), channel_id=1, source_target_pairs={{0,3},{1,2},{2,1},{3,0},{4,7},{5,6},{6,5},{7,4},{8,11},{9,10},{10,... | collective-permute-start | bytes 196616 | tf_op jit(solution)/shard_map/ppermute | solution.py:361
  10.0 0.0 collective-permute-start.1
  10.0 0.8 %collective-permute-start.2 = (bf16[8,4096]{1,0:T(8,128)(2,1)S(1)}, bf16[8,4096]{1,0:T(8,128)(2,1)S(1)}, u32[]{:S(2)}, u32[]{:S(2)}) collective-permute-start(bf16[8,4096]{1,0:T(8,128)(2,1)S(1)} %get-tuple-element.27.refs_3_), channel_id=1, source_target_pairs={{0,1},{1,0},{2,3},{3,2},{4,5},{5,4},{6,7},{7,6},{8,9},{9,8},{10,11... | collective-permute-start | bytes 196616 | tf_op jit(solution)/shard_map/ppermute | solution.py:361
  10.8 4.4 %fetch.1.refs_4_ = bf16[22,2048,128]{2,1,0:T(8,128)(2,1)S(1)} custom-call(bf16[28,2048,128]{2,1,0:T(8,128)(2,1)} %refs_5_.1), custom_call_target="tpu_custom_call" | custom-call | bytes 5767168 | tf_op jit(solution)/shard_map/fetch/pallas_call | solution.py:168
  15.2 0.0 collective-permute-done.refs_0_
  15.2 0.1 collective-permute-done.1.refs_1_
  15.2 0.0 collective-permute-done.2.refs_2_
  15.3 0.1 assemble.1
  15.3 0.0 collective-permute-done.6.refs_1_
  15.3 0.0 collective-permute-done.8.refs_2_
  15.4 0.1 pack.1.refs_0_.refs_2_
  15.4 0.1 collective-permute-start.9
  15.5 0.6 %collective-permute-start.3 = (bf16[16,6144]{1,0:T(8,128)(2,1)S(1)}, bf16[16,6144]{1,0:T(8,128)(2,1)S(1)}, u32[]{:S(2)}, u32[]{:S(2)}) collective-permute-start(bf16[16,6144]{1,0:T(8,128)(2,1)S(1)} %get-tuple-element.28.refs_1_), channel_id=1, source_target_pairs={{0,8},{4,20},{8,0},{12,28},{16,24},{20,4},{24,16},{28,12},{1,9},{5... | collective-permute-start | bytes 589832 | tf_op jit(solution)/shard_map/ppermute | solution.py:367
  16.1 0.5 %collective-permute-start.4 = (bf16[16,6144]{1,0:T(8,128)(2,1)S(1)}, bf16[16,6144]{1,0:T(8,128)(2,1)S(1)}, u32[]{:S(2)}, u32[]{:S(2)}) collective-permute-start(bf16[16,6144]{1,0:T(8,128)(2,1)S(1)} %get-tuple-element.28.refs_1_), channel_id=1, source_target_pairs={{0,16},{4,12},{8,24},{12,4},{16,0},{20,28},{24,8},{28,20},{1,17},{... | collective-permute-start | bytes 589832 | tf_op jit(solution)/shard_map/ppermute | solution.py:367
  16.6 0.0 collective-permute-start.10
  16.6 1.5 %collective-permute-start.7 = (bf16[16,9216]{1,0:T(8,128)(2,1)S(1)}, bf16[16,9216]{1,0:T(8,128)(2,1)S(1)}, u32[]{:S(2)}, u32[]{:S(2)}) collective-permute-start(bf16[16,9216]{1,0:T(8,128)(2,1)S(1)} %collective-permute-done.6.refs_1_), channel_id=1, source_target_pairs={{0,16},{4,12},{8,24},{12,4},{16,0},{20,28},{24,8},{28,20},{1,17},{... | collective-permute-start | bytes 884744 | tf_op jit(solution)/shard_map/ppermute | solution.py:369
  18.1 3.0 %hidden_grads.2 = (bf16[32,1792]{1,0:T(8,128)(2,1)S(1)}, bf16[32,1792]{1,0:T(8,128)(2,1)S(1)}, bf16[6,2048,128]{2,1,0:T(8,128)(2,1)S(1)}) custom-call(s32[16,28]{1,0:T(8,128)S(4)} %get-tuple-element.26.refs_0_.index_ref, bf16[32,4096]{1,0:T(8,128)(2,1)S(1)} %get-tuple-element.29.refs_1_.refs_3_, bf16[32,3584]{1,0:T(8,128)(2,1)S(1)} %get-tuple-element.30.refs_2_, ...), custom_call_target="tpu_custom_call" | custom-call | flops 234881024 | bytes 7340032 | tf_op jit(solution)/shard_map/hidden_grads/pallas_call | solution.py:218
  21.2 2.2 %collective-permute-done.3.refs_4_ = bf16[16,6144]{1,0:T(8,128)(2,1)S(1)} collective-permute-done((bf16[16,6144]{1,0:T(8,128)(2,1)S(1)}, bf16[16,6144]{1,0:T(8,128)(2,1)S(1)}, u32[]{:S(2)}, u32[]{:S(2)}) %collective-permute-start.3) | collective-permute-done | bytes 196640 | tf_op jit(solution)/shard_map/ppermute | solution.py:367
  23.3 0.0 collective-permute-done.4.refs_1_
  23.3 0.0 collective-permute-start.11
  23.4 0.5 %collective-permute-start.12 = (bf16[16,6144]{1,0:T(8,128)(2,1)S(1)}, bf16[16,6144]{1,0:T(8,128)(2,1)S(1)}, u32[]{:S(2)}, u32[]{:S(2)}) collective-permute-start(bf16[16,6144]{1,0:T(8,128)(2,1)S(1)} %collective-permute-done.4.refs_1_), channel_id=1, source_target_pairs={{0,4},{4,0},{8,12},{12,8},{16,20},{20,16},{24,28},{28,24},{1,5},{5... | collective-permute-start | bytes 589832 | tf_op jit(solution)/shard_map/ppermute | solution.py:374
  23.9 0.0 collective-permute-done.10.refs_3_
  23.9 0.1 collective-permute-start.5
  24.0 2.0 %hidden_grads.3 = (bf16[32,3584]{1,0:T(8,128)(2,1)}, bf16[32,3584]{1,0:T(8,128)(2,1)}) custom-call(s32[16,28]{1,0:T(8,128)S(4)} %get-tuple-element.26.refs_0_.index_ref, bf16[32,4096]{1,0:T(8,128)(2,1)S(1)} %get-tuple-element.29.refs_1_.refs_3_, bf16[32,3584]{1,0:T(8,128)(2,1)S(1)} %get-tuple-element.30.refs_2_, ...), custom_call_target="tpu_custom_call" | custom-call | flops 234881024 | bytes 7340032 | tf_op jit(solution)/shard_map/hidden_grads/pallas_call | solution.py:218
  26.0 0.0 collective-permute-done.11.refs_5_
  26.0 0.0 collective-permute-done.9.refs_2_.refs_3_
  26.0 0.3 turn.2.refs_0_
  26.4 0.0 collective-permute-done.12.refs_3_
  26.4 3.2 %collective-permute-done.5.refs_5_ = bf16[16,6144]{1,0:T(8,128)(2,1)S(1)} collective-permute-done((bf16[16,6144]{1,0:T(8,128)(2,1)S(1)}, bf16[16,6144]{1,0:T(8,128)(2,1)S(1)}, u32[]{:S(2)}, u32[]{:S(2)}) %collective-permute-start.5) | collective-permute-done | bytes 196640 | tf_op jit(solution)/shard_map/ppermute | solution.py:373
  29.5 0.0 collective-permute-done.7.refs_4_
  29.5 0.0 collective-permute-start.13
  29.5 0.5 %collective-permute-start.14 = (bf16[16,6144]{1,0:T(8,128)(2,1)S(1)}, bf16[16,6144]{1,0:T(8,128)(2,1)S(1)}, u32[]{:S(2)}, u32[]{:S(2)}) collective-permute-start(bf16[16,6144]{1,0:T(8,128)(2,1)S(1)} %collective-permute-done.5.refs_5_), channel_id=1, source_target_pairs={{0,4},{4,0},{8,12},{12,8},{16,20},{20,16},{24,28},{28,24},{1,5},{5... | collective-permute-start | bytes 589832 | tf_op jit(solution)/shard_map/ppermute | solution.py:381
  30.1 1.4 %collective-permute-done.14.refs_7_ = bf16[16,6144]{1,0:T(8,128)(2,1)S(1)} collective-permute-done((bf16[16,6144]{1,0:T(8,128)(2,1)S(1)}, bf16[16,6144]{1,0:T(8,128)(2,1)S(1)}, u32[]{:S(2)}, u32[]{:S(2)}) %collective-permute-start.14) | collective-permute-done | bytes 196640 | tf_op jit(solution)/shard_map/ppermute | solution.py:381
  31.4 0.0 collective-permute-done.13.refs_6_.refs_5_
  31.4 0.3 turn.3.refs_1_
  31.7 2.2 %down_grads.1 = f32[28,256,128]{2,1,0:T(8,128)} custom-call(s32[16,28]{1,0:T(8,128)S(4)} %get-tuple-element.26.refs_0_.index_ref, bf16[32,128,128]{2,1,0:T(8,128)(2,1)S(1)} %turn.2.refs_0_, bf16[32,128,128]{2,1,0:T(8,128)(2,1)S(1)} %turn.3.refs_1_, bf16[48,9216]{1,0:T(8,128)(2,1)S(1)} %pack.1.refs_0_.refs_2_, ...), custom_call_target="tpu_custom_call" | custom-call | flops 469762048 | bytes 3670016 | tf_op jit(solution)/shard_map/down_grads/pallas_call | solution.py:326
Async XLA Ops:
  1.9 13.5 %collective-permute-start.6 = (bf16[16,9216]{1,0:T(8,128)(2,1)S(1)}, bf16[16,9216]{1,0:T(8,128)(2,1)S(1)}, u32[]{:S(2)}, u32[]{:S(2)}) collective-permute-start(bf16[16,9216]{1,0:T(8,128)(2,1)S(1)} %get-tuple-element.35.refs_0_), channel_id=1, source_target_pairs={{0,8},{4,20},{8,0},{12,28},{16,24},{20,4},{24,16},{28,12},{1,9},{5... | collective-permute-start | bytes 884744 | tf_op jit(solution)/shard_map/ppermute | solution.py:360
  4.9 10.5 %collective-permute-start.8 = (bf16[16,9216]{1,0:T(8,128)(2,1)S(1)}, bf16[16,9216]{1,0:T(8,128)(2,1)S(1)}, u32[]{:S(2)}, u32[]{:S(2)}) collective-permute-start(bf16[16,9216]{1,0:T(8,128)(2,1)S(1)} %get-tuple-element.35.refs_0_), channel_id=1, source_target_pairs={{0,16},{4,12},{8,24},{12,4},{16,0},{20,28},{24,8},{28,20},{1,17},{... | collective-permute-start | bytes 884744 | tf_op jit(solution)/shard_map/ppermute | solution.py:360
  6.4 8.8 %collective-permute-start = (bf16[8,4096]{1,0:T(8,128)(2,1)S(1)}, bf16[8,4096]{1,0:T(8,128)(2,1)S(1)}, u32[]{:S(2)}, u32[]{:S(2)}) collective-permute-start(bf16[8,4096]{1,0:T(8,128)(2,1)S(1)} %get-tuple-element.27.refs_3_), channel_id=1, source_target_pairs={{0,3},{1,2},{2,1},{3,0},{4,7},{5,6},{6,5},{7,4},{8,11},{9,10},{10,... | collective-permute-start | bytes 196616 | tf_op jit(solution)/shard_map/ppermute | solution.py:361
  10.0 5.2 %collective-permute-start.1 = (bf16[8,4096]{1,0:T(8,128)(2,1)S(1)}, bf16[8,4096]{1,0:T(8,128)(2,1)S(1)}, u32[]{:S(2)}, u32[]{:S(2)}) collective-permute-start(bf16[8,4096]{1,0:T(8,128)(2,1)S(1)} %get-tuple-element.27.refs_3_), channel_id=1, source_target_pairs={{0,2},{1,3},{2,0},{3,1},{4,6},{5,7},{6,4},{7,5},{8,10},{9,11},{10,... | collective-permute-start | bytes 196616 | tf_op jit(solution)/shard_map/ppermute | solution.py:361
  10.0 5.2 %collective-permute-start.2 = (bf16[8,4096]{1,0:T(8,128)(2,1)S(1)}, bf16[8,4096]{1,0:T(8,128)(2,1)S(1)}, u32[]{:S(2)}, u32[]{:S(2)}) collective-permute-start(bf16[8,4096]{1,0:T(8,128)(2,1)S(1)} %get-tuple-element.27.refs_3_), channel_id=1, source_target_pairs={{0,1},{1,0},{2,3},{3,2},{4,5},{5,4},{6,7},{7,6},{8,9},{9,8},{10,11... | collective-permute-start | bytes 196616 | tf_op jit(solution)/shard_map/ppermute | solution.py:361
  15.4 10.6 %collective-permute-start.9 = (bf16[48,9216]{1,0:T(8,128)(2,1)S(1)}, bf16[48,9216]{1,0:T(8,128)(2,1)S(1)}, u32[]{:S(2)}, u32[]{:S(2)}) collective-permute-start(bf16[48,9216]{1,0:T(8,128)(2,1)S(1)} %pack.1.refs_0_.refs_2_), channel_id=1, source_target_pairs={{0,4},{4,0},{8,12},{12,8},{16,20},{20,16},{24,28},{28,24},{1,5},{5... | collective-permute-start | bytes 2654216 | tf_op jit(solution)/shard_map/ppermute | solution.py:370
  15.5 7.8 %collective-permute-start.3 = (bf16[16,6144]{1,0:T(8,128)(2,1)S(1)}, bf16[16,6144]{1,0:T(8,128)(2,1)S(1)}, u32[]{:S(2)}, u32[]{:S(2)}) collective-permute-start(bf16[16,6144]{1,0:T(8,128)(2,1)S(1)} %get-tuple-element.28.refs_1_), channel_id=1, source_target_pairs={{0,8},{4,20},{8,0},{12,28},{16,24},{20,4},{24,16},{28,12},{1,9},{5... | collective-permute-start | bytes 589832 | tf_op jit(solution)/shard_map/ppermute | solution.py:367
  16.1 7.2 %collective-permute-start.4 = (bf16[16,6144]{1,0:T(8,128)(2,1)S(1)}, bf16[16,6144]{1,0:T(8,128)(2,1)S(1)}, u32[]{:S(2)}, u32[]{:S(2)}) collective-permute-start(bf16[16,6144]{1,0:T(8,128)(2,1)S(1)} %get-tuple-element.28.refs_1_), channel_id=1, source_target_pairs={{0,16},{4,12},{8,24},{12,4},{16,0},{20,28},{24,8},{28,20},{1,17},{... | collective-permute-start | bytes 589832 | tf_op jit(solution)/shard_map/ppermute | solution.py:367
  16.6 7.2 %collective-permute-start.10 = (bf16[16,6144]{1,0:T(8,128)(2,1)S(1)}, bf16[16,6144]{1,0:T(8,128)(2,1)S(1)}, u32[]{:S(2)}, u32[]{:S(2)}) collective-permute-start(bf16[16,6144]{1,0:T(8,128)(2,1)S(1)} %get-tuple-element.28.refs_1_), channel_id=1, source_target_pairs={{0,4},{4,0},{8,12},{12,8},{16,20},{20,16},{24,28},{28,24},{1,5},{5... | collective-permute-start | bytes 589832 | tf_op jit(solution)/shard_map/ppermute | solution.py:370
  16.6 12.9 %collective-permute-start.7 = (bf16[16,9216]{1,0:T(8,128)(2,1)S(1)}, bf16[16,9216]{1,0:T(8,128)(2,1)S(1)}, u32[]{:S(2)}, u32[]{:S(2)}) collective-permute-start(bf16[16,9216]{1,0:T(8,128)(2,1)S(1)} %collective-permute-done.6.refs_1_), channel_id=1, source_target_pairs={{0,16},{4,12},{8,24},{12,4},{16,0},{20,28},{24,8},{28,20},{1,17},{... | collective-permute-start | bytes 884744 | tf_op jit(solution)/shard_map/ppermute | solution.py:369
  23.3 2.7 %collective-permute-start.11 = (bf16[16,6144]{1,0:T(8,128)(2,1)S(1)}, bf16[16,6144]{1,0:T(8,128)(2,1)S(1)}, u32[]{:S(2)}, u32[]{:S(2)}) collective-permute-start(bf16[16,6144]{1,0:T(8,128)(2,1)S(1)} %collective-permute-done.3.refs_4_), channel_id=1, source_target_pairs={{0,4},{4,0},{8,12},{12,8},{16,20},{20,16},{24,28},{28,24},{1,5},{5... | collective-permute-start | bytes 589832 | tf_op jit(solution)/shard_map/ppermute | solution.py:374
  23.4 3.0 %collective-permute-start.12 = (bf16[16,6144]{1,0:T(8,128)(2,1)S(1)}, bf16[16,6144]{1,0:T(8,128)(2,1)S(1)}, u32[]{:S(2)}, u32[]{:S(2)}) collective-permute-start(bf16[16,6144]{1,0:T(8,128)(2,1)S(1)} %collective-permute-done.4.refs_1_), channel_id=1, source_target_pairs={{0,4},{4,0},{8,12},{12,8},{16,20},{20,16},{24,28},{28,24},{1,5},{5... | collective-permute-start | bytes 589832 | tf_op jit(solution)/shard_map/ppermute | solution.py:374
  23.9 5.7 %collective-permute-start.5 = (bf16[16,6144]{1,0:T(8,128)(2,1)S(1)}, bf16[16,6144]{1,0:T(8,128)(2,1)S(1)}, u32[]{:S(2)}, u32[]{:S(2)}) collective-permute-start(bf16[16,6144]{1,0:T(8,128)(2,1)S(1)} %collective-permute-done.3.refs_4_), channel_id=1, source_target_pairs={{0,16},{4,12},{8,24},{12,4},{16,0},{20,28},{24,8},{28,20},{1,17},{... | collective-permute-start | bytes 589832 | tf_op jit(solution)/shard_map/ppermute | solution.py:373
  29.5 1.9 %collective-permute-start.13 = (bf16[16,9216]{1,0:T(8,128)(2,1)S(1)}, bf16[16,9216]{1,0:T(8,128)(2,1)S(1)}, u32[]{:S(2)}, u32[]{:S(2)}) collective-permute-start(bf16[16,9216]{1,0:T(8,128)(2,1)S(1)} %collective-permute-done.7.refs_4_), channel_id=1, source_target_pairs={{0,4},{4,0},{8,12},{12,8},{16,20},{20,16},{24,28},{28,24},{1,5},{5... | collective-permute-start | bytes 884744 | tf_op jit(solution)/shard_map/ppermute | solution.py:381
  29.5 1.9 %collective-permute-start.14 = (bf16[16,6144]{1,0:T(8,128)(2,1)S(1)}, bf16[16,6144]{1,0:T(8,128)(2,1)S(1)}, u32[]{:S(2)}, u32[]{:S(2)}) collective-permute-start(bf16[16,6144]{1,0:T(8,128)(2,1)S(1)} %collective-permute-done.5.refs_5_), channel_id=1, source_target_pairs={{0,4},{4,0},{8,12},{12,8},{16,20},{20,16},{24,28},{28,24},{1,5},{5... | collective-permute-start | bytes 589832 | tf_op jit(solution)/shard_map/ppermute | solution.py:381

commit v5 on v4

--- a/solution.py
+++ b/solution.py
@@ -366,10 +366,10 @@
     cot, sent = assemble([near] + slices, held)
     c1, c2 = first(sent), second(sent)
     packed = pack([message, m1, m2], [cot])
-    m3 = second(m1)
+    m3 = first(m2)
     packed_x, c0x = other(packed), other(sent)
     *grads, rest = hidden_grads(index, cot, gate, up, held, 0, half, weights=down_blocks, ahead=ahead)
-    c1, c2, grads = lax.optimization_barrier((c1, c2, grads))
+    c1, grads = lax.optimization_barrier((c1, grads))
     c3 = second(c1)
     c1x, c2x = other(c1), other(c2)
     grads = hidden_grads(index, cot, gate, up, held + [rest], half, blocks, grads)

time: 34.1 us -> 33.5 us (0.982)
  starting transfers between devices: 12.7 us -> 12.3 us
    ppermute x2, starting transfers between devices: 1.11 us -> 2.12 us  [gathered(): c1, c2 = (first(sent), second(sent))]
    ppermute x1, starting transfers between devices: 1.52 us -> 0.53 us  [gathered(): m3 = first(m2)]
    ppermute x1, waiting for transfers between devices: 3.16 us -> 2.53 us  [gathered(): c3 = second(c1)]
    ppermute x2, waiting for transfers between devices: 2.17 us -> 2.69 us  [gathered(): c1, c2 = (first(sent), second(sent))]
    ppermute x2, starting transfers between devices: 0.51 us -> 0.01 us  [gathered(): c1x, c2x = (other(c1), other(c2))]
  transfers between devices with their start and end apart: 15 -> 15, of which waited for: 4 -> 5; matrix products, arithmetic and copies ran while one was open for 0% -> 0% of each run, Pallas kernels for 29% -> 30%
where the time goes in v5:
time: 33.5 us; the launch traced here: 33.3 us
  Pallas kernels  13.7 us (41%)
  starting transfers between devices  12.3 us (37%)
  waiting for transfers between devices  6.65 us (20%)
  between operations  0.74 us (2%)
    pallas_call x2, Pallas kernels, hidden_grads(): pl.pallas_call(functools.partial(hidden_grad_kernel, start=start, fetched...  5.09 us
    ppermute x2, starting transfers between devices, gathered(): m1, m2 = (first(message), second(message))  4.52 us
    pallas_call x1, Pallas kernels, fetch(): pl.pallas_call(functools.partial(fetch_kernel, start=start, chunk=chunk),...  4.39 us
    ppermute x3, starting transfers between devices, gathered(): lax.ppermute(near, 'tensor', [(i, i ^ s) for i in range(parts)])  4.39 us
    ppermute x2, waiting for transfers between devices, gathered(): c1, c2 = (first(sent), second(sent))  2.69 us
    ppermute x1, waiting for transfers between devices, gathered(): c3 = second(c1)  2.53 us
    pallas_call x1, Pallas kernels, down_grads(): pl.pallas_call(functools.partial(down_grad_kernel, halves=len(turned), pl...  2.18 us
    ppermute x2, starting transfers between devices, gathered(): c1, c2 = (first(sent), second(sent))  2.12 us
  transfers between devices with their start and end apart: 15, of which 5 were waited for; matrix products, arithmetic and copies ran while one was open for 0% of the time, Pallas kernels for 30%

profile of v5, /device:TPU:0, one launch (start us, length us, event | category | flops | bytes accessed | tf_op | source)
XLA Modules:
  0.0 33.3 jit_solution(11793073487475464695)
XLA Ops:
  0.6 1.2 %hidden_units.1 = (bf16[16,9216]{1,0:T(8,128)(2,1)S(1)}, bf16[32,3584]{1,0:T(8,128)(2,1)S(1)}, bf16[32,3584]{1,0:T(8,128)(2,1)S(1)}, s32[16,28]{1,0:T(8,128)S(4)}, bf16[8,4096]{1,0:T(8,128)(2,1)S(1)}) custom-call(bf16[32,3584]{1,0:T(8,128)(2,1)} %refs_0_.1, bf16[32,3584]{1,0:T(8,128)(2,1)} %refs_1_.1, s32[16,28]{1,0:T(8,128)} %bitcast.3, bf16[8,4096]{1,0:T(8,128)(2,1)} %refs_3_.1), custom_call_target="tpu_custom_call" | custom-call | tf_op jit(solution)/shard_map/hidden_units/pallas_call | solution.py:143
  1.9 3.0 %collective-permute-start.5 = (bf16[16,9216]{1,0:T(8,128)(2,1)S(1)}, bf16[16,9216]{1,0:T(8,128)(2,1)S(1)}, u32[]{:S(2)}, u32[]{:S(2)}) collective-permute-start(bf16[16,9216]{1,0:T(8,128)(2,1)S(1)} %get-tuple-element.34.refs_0_), channel_id=1, source_target_pairs={{0,16},{4,12},{8,24},{12,4},{16,0},{20,28},{24,8},{28,20},{1,17},{... | collective-permute-start | bytes 884744 | tf_op jit(solution)/shard_map/ppermute | solution.py:360
  4.9 1.5 %collective-permute-start.7 = (bf16[16,9216]{1,0:T(8,128)(2,1)S(1)}, bf16[16,9216]{1,0:T(8,128)(2,1)S(1)}, u32[]{:S(2)}, u32[]{:S(2)}) collective-permute-start(bf16[16,9216]{1,0:T(8,128)(2,1)S(1)} %get-tuple-element.34.refs_0_), channel_id=1, source_target_pairs={{0,8},{4,20},{8,0},{12,28},{16,24},{20,4},{24,16},{28,12},{1,9},{5... | collective-permute-start | bytes 884744 | tf_op jit(solution)/shard_map/ppermute | solution.py:360
  6.4 3.6 %collective-permute-start = (bf16[8,4096]{1,0:T(8,128)(2,1)S(1)}, bf16[8,4096]{1,0:T(8,128)(2,1)S(1)}, u32[]{:S(2)}, u32[]{:S(2)}) collective-permute-start(bf16[8,4096]{1,0:T(8,128)(2,1)S(1)} %get-tuple-element.26.refs_3_), channel_id=1, source_target_pairs={{0,3},{1,2},{2,1},{3,0},{4,7},{5,6},{6,5},{7,4},{8,11},{9,10},{10,... | collective-permute-start | bytes 196616 | tf_op jit(solution)/shard_map/ppermute | solution.py:361
  10.0 0.0 collective-permute-start.1
  10.0 0.8 %collective-permute-start.2 = (bf16[8,4096]{1,0:T(8,128)(2,1)S(1)}, bf16[8,4096]{1,0:T(8,128)(2,1)S(1)}, u32[]{:S(2)}, u32[]{:S(2)}) collective-permute-start(bf16[8,4096]{1,0:T(8,128)(2,1)S(1)} %get-tuple-element.26.refs_3_), channel_id=1, source_target_pairs={{0,1},{1,0},{2,3},{3,2},{4,5},{5,4},{6,7},{7,6},{8,9},{9,8},{10,11... | collective-permute-start | bytes 196616 | tf_op jit(solution)/shard_map/ppermute | solution.py:361
  10.8 4.4 %fetch.1.refs_4_ = bf16[22,2048,128]{2,1,0:T(8,128)(2,1)S(1)} custom-call(bf16[28,2048,128]{2,1,0:T(8,128)(2,1)} %refs_5_.1), custom_call_target="tpu_custom_call" | custom-call | bytes 5767168 | tf_op jit(solution)/shard_map/fetch/pallas_call | solution.py:168
  15.2 0.0 collective-permute-done.refs_0_
  15.2 0.1 collective-permute-done.1.refs_1_
  15.2 0.0 collective-permute-done.2.refs_2_
  15.3 0.1 assemble.1
  15.3 0.0 collective-permute-done.5.refs_2_
  15.3 0.0 collective-permute-done.7.refs_1_
  15.4 0.1 pack.1.refs_0_.refs_2_
  15.4 0.1 collective-permute-start.8
  15.5 0.6 %collective-permute-start.3 = (bf16[16,6144]{1,0:T(8,128)(2,1)S(1)}, bf16[16,6144]{1,0:T(8,128)(2,1)S(1)}, u32[]{:S(2)}, u32[]{:S(2)}) collective-permute-start(bf16[16,6144]{1,0:T(8,128)(2,1)S(1)} %get-tuple-element.27.refs_1_), channel_id=1, source_target_pairs={{0,8},{4,20},{8,0},{12,28},{16,24},{20,4},{24,16},{28,12},{1,9},{5... | collective-permute-start | bytes 589832 | tf_op jit(solution)/shard_map/ppermute | solution.py:367
  16.1 0.1 collective-permute-start.9
  16.2 1.5 %collective-permute-start.11 = (bf16[16,6144]{1,0:T(8,128)(2,1)S(1)}, bf16[16,6144]{1,0:T(8,128)(2,1)S(1)}, u32[]{:S(2)}, u32[]{:S(2)}) collective-permute-start(bf16[16,6144]{1,0:T(8,128)(2,1)S(1)} %get-tuple-element.27.refs_1_), channel_id=1, source_target_pairs={{0,16},{4,12},{8,24},{12,4},{16,0},{20,28},{24,8},{28,20},{1,17},{... | collective-permute-start | bytes 589832 | tf_op jit(solution)/shard_map/ppermute | solution.py:367
  17.8 0.5 %collective-permute-start.6 = (bf16[16,9216]{1,0:T(8,128)(2,1)S(1)}, bf16[16,9216]{1,0:T(8,128)(2,1)S(1)}, u32[]{:S(2)}, u32[]{:S(2)}) collective-permute-start(bf16[16,9216]{1,0:T(8,128)(2,1)S(1)} %collective-permute-done.5.refs_2_), channel_id=1, source_target_pairs={{0,8},{4,20},{8,0},{12,28},{16,24},{20,4},{24,16},{28,12},{1,9},{5... | collective-permute-start | bytes 884744 | tf_op jit(solution)/shard_map/ppermute | solution.py:369
  18.3 3.0 %hidden_grads.2 = (bf16[32,1792]{1,0:T(8,128)(2,1)S(1)}, bf16[32,1792]{1,0:T(8,128)(2,1)S(1)}, bf16[6,2048,128]{2,1,0:T(8,128)(2,1)S(1)}) custom-call(s32[16,28]{1,0:T(8,128)S(4)} %get-tuple-element.25.refs_0_.index_ref, bf16[32,4096]{1,0:T(8,128)(2,1)S(1)} %get-tuple-element.28.refs_1_.refs_3_, bf16[32,3584]{1,0:T(8,128)(2,1)S(1)} %get-tuple-element.29.refs_2_, ...), custom_call_target="tpu_custom_call" | custom-call | flops 234881024 | bytes 7340032 | tf_op jit(solution)/shard_map/hidden_grads/pallas_call | solution.py:218
  21.3 1.9 %collective-permute-done.3.refs_4_ = bf16[16,6144]{1,0:T(8,128)(2,1)S(1)} collective-permute-done((bf16[16,6144]{1,0:T(8,128)(2,1)S(1)}, bf16[16,6144]{1,0:T(8,128)(2,1)S(1)}, u32[]{:S(2)}, u32[]{:S(2)}) %collective-permute-start.3) | collective-permute-done | bytes 196640 | tf_op jit(solution)/shard_map/ppermute | solution.py:367
  23.3 0.0 collective-permute-start.10
  23.3 0.0 collective-permute-done.9.refs_3_
  23.3 0.0 collective-permute-start.4
  23.3 0.7 %collective-permute-done.11.refs_1_ = bf16[16,6144]{1,0:T(8,128)(2,1)S(1)} collective-permute-done((bf16[16,6144]{1,0:T(8,128)(2,1)S(1)}, bf16[16,6144]{1,0:T(8,128)(2,1)S(1)}, u32[]{:S(2)}, u32[]{:S(2)}) %collective-permute-start.11) | collective-permute-done | bytes 196640 | tf_op jit(solution)/shard_map/ppermute | solution.py:367
  24.0 0.0 collective-permute-start.12
  24.0 2.0 %hidden_grads.3 = (bf16[32,3584]{1,0:T(8,128)(2,1)}, bf16[32,3584]{1,0:T(8,128)(2,1)}) custom-call(s32[16,28]{1,0:T(8,128)S(4)} %get-tuple-element.25.refs_0_.index_ref, bf16[32,4096]{1,0:T(8,128)(2,1)S(1)} %get-tuple-element.28.refs_1_.refs_3_, bf16[32,3584]{1,0:T(8,128)(2,1)S(1)} %get-tuple-element.29.refs_2_, ...), custom_call_target="tpu_custom_call" | custom-call | flops 234881024 | bytes 7340032 | tf_op jit(solution)/shard_map/hidden_grads/pallas_call | solution.py:218
  26.1 0.0 collective-permute-done.10.refs_5_
  26.1 0.0 collective-permute-done.8.refs_2_.refs_3_
  26.1 0.3 turn.2.refs_0_
  26.4 2.5 %collective-permute-done.4.refs_5_ = bf16[16,6144]{1,0:T(8,128)(2,1)S(1)} collective-permute-done((bf16[16,6144]{1,0:T(8,128)(2,1)S(1)}, bf16[16,6144]{1,0:T(8,128)(2,1)S(1)}, u32[]{:S(2)}, u32[]{:S(2)}) %collective-permute-start.4) | collective-permute-done | bytes 196640 | tf_op jit(solution)/shard_map/ppermute | solution.py:373
  29.0 0.0 collective-permute-done.12.refs_3_
  29.0 0.0 collective-permute-done.6.refs_4_
  29.0 0.0 collective-permute-start.13
  29.0 0.5 %collective-permute-start.14 = (bf16[16,6144]{1,0:T(8,128)(2,1)S(1)}, bf16[16,6144]{1,0:T(8,128)(2,1)S(1)}, u32[]{:S(2)}, u32[]{:S(2)}) collective-permute-start(bf16[16,6144]{1,0:T(8,128)(2,1)S(1)} %collective-permute-done.4.refs_5_), channel_id=1, source_target_pairs={{0,4},{4,0},{8,12},{12,8},{16,20},{20,16},{24,28},{28,24},{1,5},{5... | collective-permute-start | bytes 589832 | tf_op jit(solution)/shard_map/ppermute | solution.py:381
  29.5 1.4 %collective-permute-done.14.refs_7_ = bf16[16,6144]{1,0:T(8,128)(2,1)S(1)} collective-permute-done((bf16[16,6144]{1,0:T(8,128)(2,1)S(1)}, bf16[16,6144]{1,0:T(8,128)(2,1)S(1)}, u32[]{:S(2)}, u32[]{:S(2)}) %collective-permute-start.14) | collective-permute-done | bytes 196640 | tf_op jit(solution)/shard_map/ppermute | solution.py:381
  30.8 0.0 collective-permute-done.13.refs_6_.refs_5_
  30.8 0.3 turn.3.refs_1_
  31.2 2.2 %down_grads.1 = f32[28,256,128]{2,1,0:T(8,128)} custom-call(s32[16,28]{1,0:T(8,128)S(4)} %get-tuple-element.25.refs_0_.index_ref, bf16[32,128,128]{2,1,0:T(8,128)(2,1)S(1)} %turn.2.refs_0_, bf16[32,128,128]{2,1,0:T(8,128)(2,1)S(1)} %turn.3.refs_1_, bf16[48,9216]{1,0:T(8,128)(2,1)S(1)} %pack.1.refs_0_.refs_2_, ...), custom_call_target="tpu_custom_call" | custom-call | flops 469762048 | bytes 3670016 | tf_op jit(solution)/shard_map/down_grads/pallas_call | solution.py:326
Async XLA Ops:
  1.9 13.5 %collective-permute-start.5 = (bf16[16,9216]{1,0:T(8,128)(2,1)S(1)}, bf16[16,9216]{1,0:T(8,128)(2,1)S(1)}, u32[]{:S(2)}, u32[]{:S(2)}) collective-permute-start(bf16[16,9216]{1,0:T(8,128)(2,1)S(1)} %get-tuple-element.34.refs_0_), channel_id=1, source_target_pairs={{0,16},{4,12},{8,24},{12,4},{16,0},{20,28},{24,8},{28,20},{1,17},{... | collective-permute-start | bytes 884744 | tf_op jit(solution)/shard_map/ppermute | solution.py:360
  4.9 10.5 %collective-permute-start.7 = (bf16[16,9216]{1,0:T(8,128)(2,1)S(1)}, bf16[16,9216]{1,0:T(8,128)(2,1)S(1)}, u32[]{:S(2)}, u32[]{:S(2)}) collective-permute-start(bf16[16,9216]{1,0:T(8,128)(2,1)S(1)} %get-tuple-element.34.refs_0_), channel_id=1, source_target_pairs={{0,8},{4,20},{8,0},{12,28},{16,24},{20,4},{24,16},{28,12},{1,9},{5... | collective-permute-start | bytes 884744 | tf_op jit(solution)/shard_map/ppermute | solution.py:360
  6.4 8.8 %collective-permute-start = (bf16[8,4096]{1,0:T(8,128)(2,1)S(1)}, bf16[8,4096]{1,0:T(8,128)(2,1)S(1)}, u32[]{:S(2)}, u32[]{:S(2)}) collective-permute-start(bf16[8,4096]{1,0:T(8,128)(2,1)S(1)} %get-tuple-element.26.refs_3_), channel_id=1, source_target_pairs={{0,3},{1,2},{2,1},{3,0},{4,7},{5,6},{6,5},{7,4},{8,11},{9,10},{10,... | collective-permute-start | bytes 196616 | tf_op jit(solution)/shard_map/ppermute | solution.py:361
  10.0 5.2 %collective-permute-start.1 = (bf16[8,4096]{1,0:T(8,128)(2,1)S(1)}, bf16[8,4096]{1,0:T(8,128)(2,1)S(1)}, u32[]{:S(2)}, u32[]{:S(2)}) collective-permute-start(bf16[8,4096]{1,0:T(8,128)(2,1)S(1)} %get-tuple-element.26.refs_3_), channel_id=1, source_target_pairs={{0,2},{1,3},{2,0},{3,1},{4,6},{5,7},{6,4},{7,5},{8,10},{9,11},{10,... | collective-permute-start | bytes 196616 | tf_op jit(solution)/shard_map/ppermute | solution.py:361
  10.0 5.2 %collective-permute-start.2 = (bf16[8,4096]{1,0:T(8,128)(2,1)S(1)}, bf16[8,4096]{1,0:T(8,128)(2,1)S(1)}, u32[]{:S(2)}, u32[]{:S(2)}) collective-permute-start(bf16[8,4096]{1,0:T(8,128)(2,1)S(1)} %get-tuple-element.26.refs_3_), channel_id=1, source_target_pairs={{0,1},{1,0},{2,3},{3,2},{4,5},{5,4},{6,7},{7,6},{8,9},{9,8},{10,11... | collective-permute-start | bytes 196616 | tf_op jit(solution)/shard_map/ppermute | solution.py:361
  15.4 10.7 %collective-permute-start.8 = (bf16[48,9216]{1,0:T(8,128)(2,1)S(1)}, bf16[48,9216]{1,0:T(8,128)(2,1)S(1)}, u32[]{:S(2)}, u32[]{:S(2)}) collective-permute-start(bf16[48,9216]{1,0:T(8,128)(2,1)S(1)} %pack.1.refs_0_.refs_2_), channel_id=1, source_target_pairs={{0,4},{4,0},{8,12},{12,8},{16,20},{20,16},{24,28},{28,24},{1,5},{5... | collective-permute-start | bytes 2654216 | tf_op jit(solution)/shard_map/ppermute | solution.py:370
  15.5 7.8 %collective-permute-start.3 = (bf16[16,6144]{1,0:T(8,128)(2,1)S(1)}, bf16[16,6144]{1,0:T(8,128)(2,1)S(1)}, u32[]{:S(2)}, u32[]{:S(2)}) collective-permute-start(bf16[16,6144]{1,0:T(8,128)(2,1)S(1)} %get-tuple-element.27.refs_1_), channel_id=1, source_target_pairs={{0,8},{4,20},{8,0},{12,28},{16,24},{20,4},{24,16},{28,12},{1,9},{5... | collective-permute-start | bytes 589832 | tf_op jit(solution)/shard_map/ppermute | solution.py:367
  16.1 7.2 %collective-permute-start.9 = (bf16[16,6144]{1,0:T(8,128)(2,1)S(1)}, bf16[16,6144]{1,0:T(8,128)(2,1)S(1)}, u32[]{:S(2)}, u32[]{:S(2)}) collective-permute-start(bf16[16,6144]{1,0:T(8,128)(2,1)S(1)} %get-tuple-element.27.refs_1_), channel_id=1, source_target_pairs={{0,4},{4,0},{8,12},{12,8},{16,20},{20,16},{24,28},{28,24},{1,5},{5... | collective-permute-start | bytes 589832 | tf_op jit(solution)/shard_map/ppermute | solution.py:370
  16.2 7.8 %collective-permute-start.11 = (bf16[16,6144]{1,0:T(8,128)(2,1)S(1)}, bf16[16,6144]{1,0:T(8,128)(2,1)S(1)}, u32[]{:S(2)}, u32[]{:S(2)}) collective-permute-start(bf16[16,6144]{1,0:T(8,128)(2,1)S(1)} %get-tuple-element.27.refs_1_), channel_id=1, source_target_pairs={{0,16},{4,12},{8,24},{12,4},{16,0},{20,28},{24,8},{28,20},{1,17},{... | collective-permute-start | bytes 589832 | tf_op jit(solution)/shard_map/ppermute | solution.py:367
  17.8 11.2 %collective-permute-start.6 = (bf16[16,9216]{1,0:T(8,128)(2,1)S(1)}, bf16[16,9216]{1,0:T(8,128)(2,1)S(1)}, u32[]{:S(2)}, u32[]{:S(2)}) collective-permute-start(bf16[16,9216]{1,0:T(8,128)(2,1)S(1)} %collective-permute-done.5.refs_2_), channel_id=1, source_target_pairs={{0,8},{4,20},{8,0},{12,28},{16,24},{20,4},{24,16},{28,12},{1,9},{5... | collective-permute-start | bytes 884744 | tf_op jit(solution)/shard_map/ppermute | solution.py:369
  23.3 2.8 %collective-permute-start.10 = (bf16[16,6144]{1,0:T(8,128)(2,1)S(1)}, bf16[16,6144]{1,0:T(8,128)(2,1)S(1)}, u32[]{:S(2)}, u32[]{:S(2)}) collective-permute-start(bf16[16,6144]{1,0:T(8,128)(2,1)S(1)} %collective-permute-done.3.refs_4_), channel_id=1, source_target_pairs={{0,4},{4,0},{8,12},{12,8},{16,20},{20,16},{24,28},{28,24},{1,5},{5... | collective-permute-start | bytes 589832 | tf_op jit(solution)/shard_map/ppermute | solution.py:374
  23.3 5.7 %collective-permute-start.4 = (bf16[16,6144]{1,0:T(8,128)(2,1)S(1)}, bf16[16,6144]{1,0:T(8,128)(2,1)S(1)}, u32[]{:S(2)}, u32[]{:S(2)}) collective-permute-start(bf16[16,6144]{1,0:T(8,128)(2,1)S(1)} %collective-permute-done.3.refs_4_), channel_id=1, source_target_pairs={{0,16},{4,12},{8,24},{12,4},{16,0},{20,28},{24,8},{28,20},{1,17},{... | collective-permute-start | bytes 589832 | tf_op jit(solution)/shard_map/ppermute | solution.py:373
  24.0 4.9 %collective-permute-start.12 = (bf16[16,6144]{1,0:T(8,128)(2,1)S(1)}, bf16[16,6144]{1,0:T(8,128)(2,1)S(1)}, u32[]{:S(2)}, u32[]{:S(2)}) collective-permute-start(bf16[16,6144]{1,0:T(8,128)(2,1)S(1)} %collective-permute-done.11.refs_1_), channel_id=1, source_target_pairs={{0,4},{4,0},{8,12},{12,8},{16,20},{20,16},{24,28},{28,24},{1,5},{5... | collective-permute-start | bytes 589832 | tf_op jit(solution)/shard_map/ppermute | solution.py:374
  29.0 1.9 %collective-permute-start.13 = (bf16[16,9216]{1,0:T(8,128)(2,1)S(1)}, bf16[16,9216]{1,0:T(8,128)(2,1)S(1)}, u32[]{:S(2)}, u32[]{:S(2)}) collective-permute-start(bf16[16,9216]{1,0:T(8,128)(2,1)S(1)} %collective-permute-done.6.refs_4_), channel_id=1, source_target_pairs={{0,4},{4,0},{8,12},{12,8},{16,20},{20,16},{24,28},{28,24},{1,5},{5... | collective-permute-start | bytes 884744 | tf_op jit(solution)/shard_map/ppermute | solution.py:381
  29.0 1.9 %collective-permute-start.14 = (bf16[16,6144]{1,0:T(8,128)(2,1)S(1)}, bf16[16,6144]{1,0:T(8,128)(2,1)S(1)}, u32[]{:S(2)}, u32[]{:S(2)}) collective-permute-start(bf16[16,6144]{1,0:T(8,128)(2,1)S(1)} %collective-permute-done.4.refs_5_), channel_id=1, source_target_pairs={{0,4},{4,0},{8,12},{12,8},{16,20},{20,16},{24,28},{28,24},{1,5},{5... | collective-permute-start | bytes 589832 | tf_op jit(solution)/shard_map/ppermute | solution.py:381

commit v6 on v5

--- a/solution.py
+++ b/solution.py
@@ -290,24 +290,40 @@
     )(*map(resident, arrays))
 
 
-def down_grad_kernel(index_ref, *refs, halves, places, rows, kept, chunk, scale):
-    turned, messages, (out_ref, held, sems) = refs[:halves], refs[halves:-3], refs[-3:]
+def down_grad_kernel(index_ref, turned, *refs, places, pieces, rows, kept, chunk, scale):
+    arrays, (out_ref, held, sems) = refs[:-3], refs[-3:]
     first = lax.axis_index("dp") * kept
     blocks = held.shape[0]
+    features = turned.shape[0]
+    per_half = features // 2
     copies = []
+
+    def late(feature):
+        low = feature < per_half
+        column = jnp.where(low, feature, feature - per_half) * 128
+        slices = []
+        for (i, i_row), (j, j_row) in pieces:
+            for ref, row, start in (
+                (arrays[i], i_row, arrays[i].shape[1] - per_half * 128),
+                (arrays[j], j_row, features * 128),
+            ):
+                both = ref[row : row + rows, pl.ds(pl.multiple_of(start + column, 128), 128)]
+                slices.append(jnp.where(low, both[: rows // 2], both[rows // 2 :]))
+            slices.append(arrays[j][j_row : j_row + rows, pl.ds(pl.multiple_of(feature * 128, 128), 128)])
+        return jnp.concatenate(slices, axis=0).T
+
     for start in range(0, blocks, chunk):
         for block in range(start, start + chunk):
             right = jnp.concatenate(
                 [
-                    messages[i][row : row + rows, column * 128 : (column + 1) * 128]
+                    arrays[i][row : row + rows, column * 128 : (column + 1) * 128]
                     for i, row in places
                     for column in (block, blocks + block)
                 ],
                 axis=0,
             )
-            left = jnp.concatenate(
-                [jnp.concatenate([t[index_ref[first + k, block]] for t in turned], axis=1) for k in range(kept)], axis=0
-            )
+            chosen = [index_ref[first + k, block] for k in range(kept)]
+            left = jnp.concatenate([jnp.concatenate([turned[d], late(d)], axis=1) for d in chosen], axis=0)
             held[block] = jnp.dot(left, right, preferred_element_type=jnp.float32) * scale
         span = pl.ds(start, chunk)
         copy = pltpu.make_async_copy(held.at[span], out_ref.at[span], sems.at[start // chunk])
@@ -317,17 +333,22 @@
         copy.wait()
 
 
-def down_grads(index, turned, messages, blocks, rows, kept, scale, chunk=4):
+def down_grads(index, turned, messages, sent, blocks, rows, kept, scale, chunk=4):
     arrays = []
-    for array, _ in messages:
+    for array, _ in messages + sent:
         arrays += [array] * (not any(array is other for other in arrays))
-    places = [([array is other for other in arrays].index(True), row) for array, row in messages]
+
+    def place(array, row):
+        return [array is other for other in arrays].index(True), row
+
+    places = [place(*message) for message in messages]
+    pieces = [(place(*m), place(*c)) for m, c in zip(messages[-len(sent) :], sent)]
     shape = (blocks, kept * 128, 128)
     return pl.pallas_call(
         functools.partial(
-            down_grad_kernel, halves=len(turned), places=places, rows=rows, kept=kept, chunk=chunk, scale=scale
+            down_grad_kernel, places=places, pieces=pieces, rows=rows, kept=kept, chunk=chunk, scale=scale
         ),
-        in_specs=[IN_SMEM] + [IN_VMEM] * (len(turned) + len(arrays)),
+        in_specs=[IN_SMEM] + [IN_VMEM] * (1 + len(arrays)),
         out_specs=ANYWHERE,
         out_shape=jax.ShapeDtypeStruct(shape, jnp.float32),
         scratch_shapes=[pltpu.VMEM(shape, jnp.float32), pltpu.SemaphoreType.DMA((blocks // chunk,))],
@@ -338,7 +359,7 @@
             transcendentals=0,
         ),
         name="down_grads",
-    )(scalar(index), *map(resident, (*turned, *arrays)))
+    )(scalar(index), *map(resident, (turned, *arrays)))
 
 
 def gathered(gate_act, up_act, cotangent, down_blocks, down_index):
@@ -380,8 +401,8 @@
     )
     m3x, c3x = other(m3), other(c3)
     messages = [(array, i * rows) for i in range(3) for array in (packed, packed_x)] + [(m3, 0), (m3x, 0)]
-    late = turn(list(zip(messages[4:], [(c2, 0), (c2x, 0), (c3, 0), (c3x, 0)])), rows // 2)
-    down_grad = down_grads(index, [early, late], messages, blocks, rows, kept, 1.0 / replicas)
+    late = [(c2, 0), (c2x, 0), (c3, 0), (c3x, 0)]
+    down_grad = down_grads(index, early, messages, late, blocks, rows, kept, 1.0 / replicas)
     return down_grad.transpose(1, 0, 2), gate_out, up_out
 
 

time: 33.5 us -> 33.3 us (level)
  no operation moved by 1% of the time
where the time goes in v6:
time: 33.3 us; the launch traced here: 33.1 us
  Pallas kernels  13.5 us (41%)
  starting transfers between devices  12.3 us (37%)
  waiting for transfers between devices  6.66 us (20%)
  between operations  0.73 us (2%)
    pallas_call x2, Pallas kernels, hidden_grads(): pl.pallas_call(functools.partial(hidden_grad_kernel, start=start, fetched...  5.08 us
    ppermute x2, starting transfers between devices, gathered(): m1, m2 = (first(message), second(message))  4.52 us
    pallas_call x1, Pallas kernels, fetch(): pl.pallas_call(functools.partial(fetch_kernel, start=start, chunk=chunk),...  4.39 us
    ppermute x3, starting transfers between devices, gathered(): lax.ppermute(near, 'tensor', [(i, i ^ s) for i in range(parts)])  4.39 us
    ppermute x2, waiting for transfers between devices, gathered(): c1, c2 = (first(sent), second(sent))  2.69 us
    ppermute x1, waiting for transfers between devices, gathered(): c3 = second(c1)  2.53 us
    pallas_call x1, Pallas kernels, down_grads(): pl.pallas_call(functools.partial(down_grad_kernel, places=places, pieces=...  2.31 us
    ppermute x2, starting transfers between devices, gathered(): c1, c2 = (first(sent), second(sent))  2.12 us
  transfers between devices with their start and end apart: 15, of which 5 were waited for; matrix products, arithmetic and copies ran while one was open for 0% of the time, Pallas kernels for 30%

profile of v6, /device:TPU:0, one launch (start us, length us, event | category | flops | bytes accessed | tf_op | source)
XLA Modules:
  0.0 33.1 jit_solution(6064513679724629052)
XLA Ops:
  0.6 1.2 %hidden_units.1 = (bf16[16,9216]{1,0:T(8,128)(2,1)S(1)}, bf16[32,3584]{1,0:T(8,128)(2,1)S(1)}, bf16[32,3584]{1,0:T(8,128)(2,1)S(1)}, s32[16,28]{1,0:T(8,128)S(4)}, bf16[8,4096]{1,0:T(8,128)(2,1)S(1)}) custom-call(bf16[32,3584]{1,0:T(8,128)(2,1)} %refs_0_.1, bf16[32,3584]{1,0:T(8,128)(2,1)} %refs_1_.1, s32[16,28]{1,0:T(8,128)} %bitcast.3, bf16[8,4096]{1,0:T(8,128)(2,1)} %refs_3_.1), custom_call_target="tpu_custom_call" | custom-call | tf_op jit(solution)/shard_map/hidden_units/pallas_call | solution.py:143
  1.9 3.0 %collective-permute-start.5 = (bf16[16,9216]{1,0:T(8,128)(2,1)S(1)}, bf16[16,9216]{1,0:T(8,128)(2,1)S(1)}, u32[]{:S(2)}, u32[]{:S(2)}) collective-permute-start(bf16[16,9216]{1,0:T(8,128)(2,1)S(1)} %get-tuple-element.34.refs_0_), channel_id=1, source_target_pairs={{0,16},{4,12},{8,24},{12,4},{16,0},{20,28},{24,8},{28,20},{1,17},{... | collective-permute-start | bytes 884744 | tf_op jit(solution)/shard_map/ppermute | solution.py:381
  4.9 1.5 %collective-permute-start.7 = (bf16[16,9216]{1,0:T(8,128)(2,1)S(1)}, bf16[16,9216]{1,0:T(8,128)(2,1)S(1)}, u32[]{:S(2)}, u32[]{:S(2)}) collective-permute-start(bf16[16,9216]{1,0:T(8,128)(2,1)S(1)} %get-tuple-element.34.refs_0_), channel_id=1, source_target_pairs={{0,8},{4,20},{8,0},{12,28},{16,24},{20,4},{24,16},{28,12},{1,9},{5... | collective-permute-start | bytes 884744 | tf_op jit(solution)/shard_map/ppermute | solution.py:381
  6.4 3.6 %collective-permute-start = (bf16[8,4096]{1,0:T(8,128)(2,1)S(1)}, bf16[8,4096]{1,0:T(8,128)(2,1)S(1)}, u32[]{:S(2)}, u32[]{:S(2)}) collective-permute-start(bf16[8,4096]{1,0:T(8,128)(2,1)S(1)} %get-tuple-element.26.refs_3_), channel_id=1, source_target_pairs={{0,3},{1,2},{2,1},{3,0},{4,7},{5,6},{6,5},{7,4},{8,11},{9,10},{10,... | collective-permute-start | bytes 196616 | tf_op jit(solution)/shard_map/ppermute | solution.py:382
  10.0 0.0 collective-permute-start.1
  10.0 0.8 %collective-permute-start.2 = (bf16[8,4096]{1,0:T(8,128)(2,1)S(1)}, bf16[8,4096]{1,0:T(8,128)(2,1)S(1)}, u32[]{:S(2)}, u32[]{:S(2)}) collective-permute-start(bf16[8,4096]{1,0:T(8,128)(2,1)S(1)} %get-tuple-element.26.refs_3_), channel_id=1, source_target_pairs={{0,1},{1,0},{2,3},{3,2},{4,5},{5,4},{6,7},{7,6},{8,9},{9,8},{10,11... | collective-permute-start | bytes 196616 | tf_op jit(solution)/shard_map/ppermute | solution.py:382
  10.8 4.4 %fetch.1.refs_4_ = bf16[22,2048,128]{2,1,0:T(8,128)(2,1)S(1)} custom-call(bf16[28,2048,128]{2,1,0:T(8,128)(2,1)} %refs_5_.1), custom_call_target="tpu_custom_call" | custom-call | bytes 5767168 | tf_op jit(solution)/shard_map/fetch/pallas_call | solution.py:168
  15.2 0.0 collective-permute-done.refs_0_
  15.2 0.1 collective-permute-done.1.refs_1_
  15.2 0.0 collective-permute-done.2.refs_2_
  15.3 0.1 assemble.1
  15.3 0.0 collective-permute-done.5.refs_2_
  15.3 0.0 collective-permute-done.7.refs_1_
  15.4 0.1 pack.1.refs_0_
  15.4 0.1 collective-permute-start.8
  15.5 0.6 %collective-permute-start.3 = (bf16[16,6144]{1,0:T(8,128)(2,1)S(1)}, bf16[16,6144]{1,0:T(8,128)(2,1)S(1)}, u32[]{:S(2)}, u32[]{:S(2)}) collective-permute-start(bf16[16,6144]{1,0:T(8,128)(2,1)S(1)} %get-tuple-element.27.refs_1_), channel_id=1, source_target_pairs={{0,8},{4,20},{8,0},{12,28},{16,24},{20,4},{24,16},{28,12},{1,9},{5... | collective-permute-start | bytes 589832 | tf_op jit(solution)/shard_map/ppermute | solution.py:388
  16.1 0.1 collective-permute-start.9
  16.2 1.5 %collective-permute-start.11 = (bf16[16,6144]{1,0:T(8,128)(2,1)S(1)}, bf16[16,6144]{1,0:T(8,128)(2,1)S(1)}, u32[]{:S(2)}, u32[]{:S(2)}) collective-permute-start(bf16[16,6144]{1,0:T(8,128)(2,1)S(1)} %get-tuple-element.27.refs_1_), channel_id=1, source_target_pairs={{0,16},{4,12},{8,24},{12,4},{16,0},{20,28},{24,8},{28,20},{1,17},{... | collective-permute-start | bytes 589832 | tf_op jit(solution)/shard_map/ppermute | solution.py:388
  17.8 0.5 %collective-permute-start.6 = (bf16[16,9216]{1,0:T(8,128)(2,1)S(1)}, bf16[16,9216]{1,0:T(8,128)(2,1)S(1)}, u32[]{:S(2)}, u32[]{:S(2)}) collective-permute-start(bf16[16,9216]{1,0:T(8,128)(2,1)S(1)} %collective-permute-done.5.refs_2_), channel_id=1, source_target_pairs={{0,8},{4,20},{8,0},{12,28},{16,24},{20,4},{24,16},{28,12},{1,9},{5... | collective-permute-start | bytes 884744 | tf_op jit(solution)/shard_map/ppermute | solution.py:390
  18.3 3.0 %hidden_grads.2 = (bf16[32,1792]{1,0:T(8,128)(2,1)S(1)}, bf16[32,1792]{1,0:T(8,128)(2,1)S(1)}, bf16[6,2048,128]{2,1,0:T(8,128)(2,1)S(1)}) custom-call(s32[16,28]{1,0:T(8,128)S(4)} %get-tuple-element.25.refs_0_.index_ref, bf16[32,4096]{1,0:T(8,128)(2,1)S(1)} %get-tuple-element.28.refs_1_.refs_3_, bf16[32,3584]{1,0:T(8,128)(2,1)S(1)} %get-tuple-element.29.refs_2_, ...), custom_call_target="tpu_custom_call" | custom-call | flops 234881024 | bytes 7340032 | tf_op jit(solution)/shard_map/hidden_grads/pallas_call | solution.py:218
  21.3 1.9 %collective-permute-done.3.refs_4_ = bf16[16,6144]{1,0:T(8,128)(2,1)S(1)} collective-permute-done((bf16[16,6144]{1,0:T(8,128)(2,1)S(1)}, bf16[16,6144]{1,0:T(8,128)(2,1)S(1)}, u32[]{:S(2)}, u32[]{:S(2)}) %collective-permute-start.3) | collective-permute-done | bytes 196640 | tf_op jit(solution)/shard_map/ppermute | solution.py:388
  23.3 0.0 collective-permute-start.10
  23.3 0.0 collective-permute-done.9.refs_3_
  23.3 0.0 collective-permute-start.4
  23.3 0.7 %collective-permute-done.11.refs_4_ = bf16[16,6144]{1,0:T(8,128)(2,1)S(1)} collective-permute-done((bf16[16,6144]{1,0:T(8,128)(2,1)S(1)}, bf16[16,6144]{1,0:T(8,128)(2,1)S(1)}, u32[]{:S(2)}, u32[]{:S(2)}) %collective-permute-start.11) | collective-permute-done | bytes 196640 | tf_op jit(solution)/shard_map/ppermute | solution.py:388
  24.0 0.0 collective-permute-start.12
  24.0 2.0 %hidden_grads.3 = (bf16[32,3584]{1,0:T(8,128)(2,1)}, bf16[32,3584]{1,0:T(8,128)(2,1)}) custom-call(s32[16,28]{1,0:T(8,128)S(4)} %get-tuple-element.25.refs_0_.index_ref, bf16[32,4096]{1,0:T(8,128)(2,1)S(1)} %get-tuple-element.28.refs_1_.refs_3_, bf16[32,3584]{1,0:T(8,128)(2,1)S(1)} %get-tuple-element.29.refs_2_, ...), custom_call_target="tpu_custom_call" | custom-call | flops 234881024 | bytes 7340032 | tf_op jit(solution)/shard_map/hidden_grads/pallas_call | solution.py:218
  26.1 0.0 collective-permute-done.10.refs_5_
  26.1 0.0 collective-permute-done.8.refs_2_.refs_1_
  26.1 0.3 turn.1.turned
  26.4 2.5 %collective-permute-done.4.refs_6_ = bf16[16,6144]{1,0:T(8,128)(2,1)S(1)} collective-permute-done((bf16[16,6144]{1,0:T(8,128)(2,1)S(1)}, bf16[16,6144]{1,0:T(8,128)(2,1)S(1)}, u32[]{:S(2)}, u32[]{:S(2)}) %collective-permute-start.4) | collective-permute-done | bytes 196640 | tf_op jit(solution)/shard_map/ppermute | solution.py:394
  29.0 0.0 collective-permute-done.12.refs_5_
  29.0 0.0 collective-permute-done.6.refs_2_
  29.0 0.0 collective-permute-start.13
  29.0 0.5 %collective-permute-start.14 = (bf16[16,6144]{1,0:T(8,128)(2,1)S(1)}, bf16[16,6144]{1,0:T(8,128)(2,1)S(1)}, u32[]{:S(2)}, u32[]{:S(2)}) collective-permute-start(bf16[16,6144]{1,0:T(8,128)(2,1)S(1)} %collective-permute-done.4.refs_6_), channel_id=1, source_target_pairs={{0,4},{4,0},{8,12},{12,8},{16,20},{20,16},{24,28},{28,24},{1,5},{5... | collective-permute-start | bytes 589832 | tf_op jit(solution)/shard_map/ppermute | solution.py:402
  29.5 1.4 %collective-permute-done.14.refs_7_ = bf16[16,6144]{1,0:T(8,128)(2,1)S(1)} collective-permute-done((bf16[16,6144]{1,0:T(8,128)(2,1)S(1)}, bf16[16,6144]{1,0:T(8,128)(2,1)S(1)}, u32[]{:S(2)}, u32[]{:S(2)}) %collective-permute-start.14) | collective-permute-done | bytes 196640 | tf_op jit(solution)/shard_map/ppermute | solution.py:402
  30.8 0.0 collective-permute-done.13.refs_3_
  30.8 2.3 %down_grads.1 = f32[28,256,128]{2,1,0:T(8,128)} custom-call(s32[16,28]{1,0:T(8,128)S(4)} %get-tuple-element.25.refs_0_.index_ref, bf16[32,128,128]{2,1,0:T(8,128)(2,1)S(1)} %turn.1.turned, bf16[48,9216]{1,0:T(8,128)(2,1)S(1)} %pack.1.refs_0_, bf16[48,9216]{1,0:T(8,128)(2,1)S(1)} %collective-permute-done.8.refs_2_.refs_1_, ...), custom_call_target="tpu_custom_call" | custom-call | flops 469762048 | bytes 3670016 | tf_op jit(solution)/shard_map/down_grads/pallas_call | solution.py:347
Async XLA Ops:
  1.9 13.5 %collective-permute-start.5 = (bf16[16,9216]{1,0:T(8,128)(2,1)S(1)}, bf16[16,9216]{1,0:T(8,128)(2,1)S(1)}, u32[]{:S(2)}, u32[]{:S(2)}) collective-permute-start(bf16[16,9216]{1,0:T(8,128)(2,1)S(1)} %get-tuple-element.34.refs_0_), channel_id=1, source_target_pairs={{0,16},{4,12},{8,24},{12,4},{16,0},{20,28},{24,8},{28,20},{1,17},{... | collective-permute-start | bytes 884744 | tf_op jit(solution)/shard_map/ppermute | solution.py:381
  4.9 10.5 %collective-permute-start.7 = (bf16[16,9216]{1,0:T(8,128)(2,1)S(1)}, bf16[16,9216]{1,0:T(8,128)(2,1)S(1)}, u32[]{:S(2)}, u32[]{:S(2)}) collective-permute-start(bf16[16,9216]{1,0:T(8,128)(2,1)S(1)} %get-tuple-element.34.refs_0_), channel_id=1, source_target_pairs={{0,8},{4,20},{8,0},{12,28},{16,24},{20,4},{24,16},{28,12},{1,9},{5... | collective-permute-start | bytes 884744 | tf_op jit(solution)/shard_map/ppermute | solution.py:381
  6.4 8.8 %collective-permute-start = (bf16[8,4096]{1,0:T(8,128)(2,1)S(1)}, bf16[8,4096]{1,0:T(8,128)(2,1)S(1)}, u32[]{:S(2)}, u32[]{:S(2)}) collective-permute-start(bf16[8,4096]{1,0:T(8,128)(2,1)S(1)} %get-tuple-element.26.refs_3_), channel_id=1, source_target_pairs={{0,3},{1,2},{2,1},{3,0},{4,7},{5,6},{6,5},{7,4},{8,11},{9,10},{10,... | collective-permute-start | bytes 196616 | tf_op jit(solution)/shard_map/ppermute | solution.py:382
  10.0 5.2 %collective-permute-start.1 = (bf16[8,4096]{1,0:T(8,128)(2,1)S(1)}, bf16[8,4096]{1,0:T(8,128)(2,1)S(1)}, u32[]{:S(2)}, u32[]{:S(2)}) collective-permute-start(bf16[8,4096]{1,0:T(8,128)(2,1)S(1)} %get-tuple-element.26.refs_3_), channel_id=1, source_target_pairs={{0,2},{1,3},{2,0},{3,1},{4,6},{5,7},{6,4},{7,5},{8,10},{9,11},{10,... | collective-permute-start | bytes 196616 | tf_op jit(solution)/shard_map/ppermute | solution.py:382
  10.0 5.2 %collective-permute-start.2 = (bf16[8,4096]{1,0:T(8,128)(2,1)S(1)}, bf16[8,4096]{1,0:T(8,128)(2,1)S(1)}, u32[]{:S(2)}, u32[]{:S(2)}) collective-permute-start(bf16[8,4096]{1,0:T(8,128)(2,1)S(1)} %get-tuple-element.26.refs_3_), channel_id=1, source_target_pairs={{0,1},{1,0},{2,3},{3,2},{4,5},{5,4},{6,7},{7,6},{8,9},{9,8},{10,11... | collective-permute-start | bytes 196616 | tf_op jit(solution)/shard_map/ppermute | solution.py:382
  15.4 10.7 %collective-permute-start.8 = (bf16[48,9216]{1,0:T(8,128)(2,1)S(1)}, bf16[48,9216]{1,0:T(8,128)(2,1)S(1)}, u32[]{:S(2)}, u32[]{:S(2)}) collective-permute-start(bf16[48,9216]{1,0:T(8,128)(2,1)S(1)} %pack.1.refs_0_), channel_id=1, source_target_pairs={{0,4},{4,0},{8,12},{12,8},{16,20},{20,16},{24,28},{28,24},{1,5},{5... | collective-permute-start | bytes 2654216 | tf_op jit(solution)/shard_map/ppermute | solution.py:391
  15.5 7.8 %collective-permute-start.3 = (bf16[16,6144]{1,0:T(8,128)(2,1)S(1)}, bf16[16,6144]{1,0:T(8,128)(2,1)S(1)}, u32[]{:S(2)}, u32[]{:S(2)}) collective-permute-start(bf16[16,6144]{1,0:T(8,128)(2,1)S(1)} %get-tuple-element.27.refs_1_), channel_id=1, source_target_pairs={{0,8},{4,20},{8,0},{12,28},{16,24},{20,4},{24,16},{28,12},{1,9},{5... | collective-permute-start | bytes 589832 | tf_op jit(solution)/shard_map/ppermute | solution.py:388
  16.1 7.2 %collective-permute-start.9 = (bf16[16,6144]{1,0:T(8,128)(2,1)S(1)}, bf16[16,6144]{1,0:T(8,128)(2,1)S(1)}, u32[]{:S(2)}, u32[]{:S(2)}) collective-permute-start(bf16[16,6144]{1,0:T(8,128)(2,1)S(1)} %get-tuple-element.27.refs_1_), channel_id=1, source_target_pairs={{0,4},{4,0},{8,12},{12,8},{16,20},{20,16},{24,28},{28,24},{1,5},{5... | collective-permute-start | bytes 589832 | tf_op jit(solution)/shard_map/ppermute | solution.py:391
  16.2 7.8 %collective-permute-start.11 = (bf16[16,6144]{1,0:T(8,128)(2,1)S(1)}, bf16[16,6144]{1,0:T(8,128)(2,1)S(1)}, u32[]{:S(2)}, u32[]{:S(2)}) collective-permute-start(bf16[16,6144]{1,0:T(8,128)(2,1)S(1)} %get-tuple-element.27.refs_1_), channel_id=1, source_target_pairs={{0,16},{4,12},{8,24},{12,4},{16,0},{20,28},{24,8},{28,20},{1,17},{... | collective-permute-start | bytes 589832 | tf_op jit(solution)/shard_map/ppermute | solution.py:388
  17.8 11.2 %collective-permute-start.6 = (bf16[16,9216]{1,0:T(8,128)(2,1)S(1)}, bf16[16,9216]{1,0:T(8,128)(2,1)S(1)}, u32[]{:S(2)}, u32[]{:S(2)}) collective-permute-start(bf16[16,9216]{1,0:T(8,128)(2,1)S(1)} %collective-permute-done.5.refs_2_), channel_id=1, source_target_pairs={{0,8},{4,20},{8,0},{12,28},{16,24},{20,4},{24,16},{28,12},{1,9},{5... | collective-permute-start | bytes 884744 | tf_op jit(solution)/shard_map/ppermute | solution.py:390
  23.3 2.8 %collective-permute-start.10 = (bf16[16,6144]{1,0:T(8,128)(2,1)S(1)}, bf16[16,6144]{1,0:T(8,128)(2,1)S(1)}, u32[]{:S(2)}, u32[]{:S(2)}) collective-permute-start(bf16[16,6144]{1,0:T(8,128)(2,1)S(1)} %collective-permute-done.3.refs_4_), channel_id=1, source_target_pairs={{0,4},{4,0},{8,12},{12,8},{16,20},{20,16},{24,28},{28,24},{1,5},{5... | collective-permute-start | bytes 589832 | tf_op jit(solution)/shard_map/ppermute | solution.py:395
  23.3 5.7 %collective-permute-start.4 = (bf16[16,6144]{1,0:T(8,128)(2,1)S(1)}, bf16[16,6144]{1,0:T(8,128)(2,1)S(1)}, u32[]{:S(2)}, u32[]{:S(2)}) collective-permute-start(bf16[16,6144]{1,0:T(8,128)(2,1)S(1)} %collective-permute-done.3.refs_4_), channel_id=1, source_target_pairs={{0,16},{4,12},{8,24},{12,4},{16,0},{20,28},{24,8},{28,20},{1,17},{... | collective-permute-start | bytes 589832 | tf_op jit(solution)/shard_map/ppermute | solution.py:394
  24.0 4.9 %collective-permute-start.12 = (bf16[16,6144]{1,0:T(8,128)(2,1)S(1)}, bf16[16,6144]{1,0:T(8,128)(2,1)S(1)}, u32[]{:S(2)}, u32[]{:S(2)}) collective-permute-start(bf16[16,6144]{1,0:T(8,128)(2,1)S(1)} %collective-permute-done.11.refs_4_), channel_id=1, source_target_pairs={{0,4},{4,0},{8,12},{12,8},{16,20},{20,16},{24,28},{28,24},{1,5},{5... | collective-permute-start | bytes 589832 | tf_op jit(solution)/shard_map/ppermute | solution.py:395
  29.0 1.9 %collective-permute-start.13 = (bf16[16,9216]{1,0:T(8,128)(2,1)S(1)}, bf16[16,9216]{1,0:T(8,128)(2,1)S(1)}, u32[]{:S(2)}, u32[]{:S(2)}) collective-permute-start(bf16[16,9216]{1,0:T(8,128)(2,1)S(1)} %collective-permute-done.6.refs_2_), channel_id=1, source_target_pairs={{0,4},{4,0},{8,12},{12,8},{16,20},{20,16},{24,28},{28,24},{1,5},{5... | collective-permute-start | bytes 884744 | tf_op jit(solution)/shard_map/ppermute | solution.py:402
  29.0 1.9 %collective-permute-start.14 = (bf16[16,6144]{1,0:T(8,128)(2,1)S(1)}, bf16[16,6144]{1,0:T(8,128)(2,1)S(1)}, u32[]{:S(2)}, u32[]{:S(2)}) collective-permute-start(bf16[16,6144]{1,0:T(8,128)(2,1)S(1)} %collective-permute-done.4.refs_6_), channel_id=1, source_target_pairs={{0,4},{4,0},{8,12},{12,8},{16,20},{20,16},{24,28},{28,24},{1,5},{5... | collective-permute-start | bytes 589832 | tf_op jit(solution)/shard_map/ppermute | solution.py:402

commit v7 on v6

--- a/solution.py
+++ b/solution.py
@@ -74,7 +74,7 @@
 
 
 def assemble_kernel(*refs, parts):
-    pieces, (out_ref, sent_ref) = refs[:parts][::-1], refs[-2:]
+    pieces, (out_ref, sent_ref, far_ref) = refs[:parts][::-1], refs[-3:]
     here = lax.axis_index("tensor")
     for place in range(parts):
 
@@ -83,7 +83,8 @@
             out_ref[...] = jnp.concatenate([pieces[place ^ q][...] for q in range(parts)], axis=0)
 
     width = out_ref.shape[1]
-    sent_ref[:, :width] = jnp.concatenate([piece[...] for piece in pieces[2:]], axis=0)
+    far_ref[...] = jnp.concatenate([piece[...] for piece in pieces[2:]], axis=0)
+    sent_ref[:, :width] = far_ref[...]
     sent_ref[:, width:] = stacked(pieces[1][...])
 
 
@@ -99,8 +100,10 @@
     return pl.pallas_call(
         functools.partial(assemble_kernel, parts=parts),
         in_specs=[IN_VMEM] * (parts + len(after)),
-        out_specs=[IN_VMEM] * 2,
-        out_shape=[pltpu.VMEM((parts * rows, width), dtype), pltpu.VMEM((2 * rows, width * 3 // 2), dtype)],
+        out_specs=[IN_VMEM] * 3,
+        out_shape=[
+            pltpu.VMEM(shape, dtype) for shape in ((parts * rows, width), (2 * rows, width * 3 // 2), (2 * rows, width))
+        ],
         compiler_params=pltpu.CompilerParams(vmem_limit_bytes=4 * 2**20),
         cost_estimate=pl.CostEstimate(flops=0, bytes_accessed=LONG, transcendentals=0),
         name="assemble",
@@ -237,24 +240,51 @@
     )
 
 
-def pack_kernel(*refs, count):
-    pieces, out_ref = refs[:count], refs[-1]
+def pack_kernel(*refs, count, ends):
+    pieces, extra, (out_ref, end_ref) = refs[:count], refs[count], refs[-2:]
     rows = pieces[0].shape[0]
-    for i, piece in enumerate(pieces):
-        out_ref[i * rows : (i + 1) * rows, :] = piece[...]
-
-
-def pack(pieces, after):
+    for i, ref in enumerate(pieces):
+        out_ref[i * rows : (i + 1) * rows, :] = ref[...]
+    width = extra.shape[1]
+    out_ref[count * rows :, :width] = extra[...]
+    out_ref[count * rows :, width:] = jnp.zeros_like(out_ref[count * rows :, width:])
+    for i, piece in enumerate(ends):
+        end_ref[i * rows : (i + 1) * rows, :] = pieces[piece][:, -end_ref.shape[1] :]
+
+
+def pack(pieces, extra, ends, columns):
     rows, width = pieces[0].shape
-    return pl.pallas_call(
-        functools.partial(pack_kernel, count=len(pieces)),
-        in_specs=[IN_VMEM] * (len(pieces) + len(after)),
-        out_specs=IN_VMEM,
-        out_shape=pltpu.VMEM((len(pieces) * rows, width), pieces[0].dtype),
+    dtype = pieces[0].dtype
+    return pl.pallas_call(
+        functools.partial(pack_kernel, count=len(pieces), ends=ends),
+        in_specs=[IN_VMEM] * (len(pieces) + 1),
+        out_specs=[IN_VMEM] * 2,
+        out_shape=[pltpu.VMEM((len(pieces) * rows + rows, width), dtype), pltpu.VMEM((len(ends) * rows, columns), dtype)],
         compiler_params=pltpu.CompilerParams(vmem_limit_bytes=4 * 2**20),
         cost_estimate=pl.CostEstimate(flops=0, bytes_accessed=LONG, transcendentals=0),
         name="pack",
-    )(*map(resident, pieces), *map(resident, after))
+    )(*map(resident, pieces), resident(extra))
+
+
+def join_kernel(*refs, count):
+    ends_ref, firsts, outs = refs[0], refs[1 : 1 + count], refs[1 + count :]
+    for i, (first, out) in enumerate(zip(firsts, outs)):
+        rows, width = first.shape
+        out[:, :width] = first[...]
+        out[:, width:] = ends_ref[i * rows : (i + 1) * rows, :]
+
+
+def join(ends, firsts):
+    rows, width = firsts[0].shape
+    out = pltpu.VMEM((rows, width + ends.shape[1]), firsts[0].dtype)
+    return pl.pallas_call(
+        functools.partial(join_kernel, count=len(firsts)),
+        in_specs=[IN_VMEM] * (1 + len(firsts)),
+        out_specs=[IN_VMEM] * len(firsts),
+        out_shape=[out] * len(firsts),
+        compiler_params=pltpu.CompilerParams(vmem_limit_bytes=4 * 2**20),
+        name="join",
+    )(*map(resident, (ends, *firsts)))
 
 
 def turn_kernel(*refs, places, rows):
@@ -384,18 +414,22 @@
     half = blocks // 2
     ahead = blocks * 3 // 14
     held = [fetch(down_blocks, 0, blocks - ahead)]
-    cot, sent = assemble([near] + slices, held)
-    c1, c2 = first(sent), second(sent)
-    packed = pack([message, m1, m2], [cot])
+    cot, sent, far = assemble([near] + slices, held)
+    c1, c2 = first(far), second(far)
+    packed, nears = pack([message, m1, m2], sent, (1, 2), near.shape[1] // 2)
+    nexts = lax.ppermute(nears, "tensor", [(i, i ^ 1) for i in range(parts)])
     m3 = first(m2)
-    packed_x, c0x = other(packed), other(sent)
+    packed_x = other(packed)
     *grads, rest = hidden_grads(index, cot, gate, up, held, 0, half, weights=down_blocks, ahead=ahead)
-    c1, grads = lax.optimization_barrier((c1, grads))
+    c1, c2, nexts, grads = lax.optimization_barrier((c1, c2, nexts, grads))
+    raw = [nexts, c1, c2]
+    c1, c2 = join(nexts, [c1, c2])
     c3 = second(c1)
-    c1x, c2x = other(c1), other(c2)
+    nexts_x, *raw_x = [other(array) for array in raw]
+    c1x, c2x = join(nexts_x, raw_x)
     grads = hidden_grads(index, cot, gate, up, held + [rest], half, blocks, grads)
     messages = [(array, i * rows) for i in range(3) for array in (packed, packed_x)]
-    early = turn(list(zip(messages[:4], [(sent, 0), (c0x, 0), (c1, 0), (c1x, 0)])), rows // 2)
+    early = turn(list(zip(messages[:4], [(sent, 0), (packed_x, 3 * rows), (c1, 0), (c1x, 0)])), rows // 2)
     c3, m3, early, c2x, packed_x, (gate_out, up_out) = lax.optimization_barrier(
         (c3, m3, early, c2x, packed_x, grads)
     )

time: 33.3 us -> 32.7 us (0.982)
  waiting for transfers between devices: 6.66 us -> 2.76 us
  starting transfers between devices: 12.3 us -> 15.4 us
    ppermute x6 -> x7, waiting for transfers between devices: 2.7 us -> 0.12 us  [the longest x2 0.11 us: gathered(): c1, c2 = (first(far), second(far))]
    ppermute x1, starting transfers between devices: 0.01 us -> 1.57 us  [gathered(): c3 = second(c1)]
    ppermute x1, waiting for transfers between devices: 2.53 us -> 1.21 us  [gathered(): c3 = second(c1)]
    ppermute x1, starting transfers between devices: 0.53 us -> 1.49 us  [gathered(): m3 = first(m2)]
    ppermute x6 -> x7, starting transfers between devices: 2.32 us -> 2.91 us  [the longest x1 1.22 us: gathered(): nexts = lax.ppermute(nears, 'tensor', [(i, i ^ 1) for i in range(parts)])]
  transfers between devices with their start and end apart: 15 -> 16, of which waited for: 5 -> 4; matrix products, arithmetic and copies ran while one was open for 0% -> 0% of each run, Pallas kernels for 30% -> 31%
where the time goes in v7:
time: 32.7 us; the launch traced here: 32.5 us
  starting transfers between devices  15.4 us (47%)
  Pallas kernels  13.6 us (42%)
  waiting for transfers between devices  2.76 us (8%)
  between operations  0.76 us (2%)
    pallas_call x2, Pallas kernels, hidden_grads(): pl.pallas_call(functools.partial(hidden_grad_kernel, start=start, fetched...  5.07 us
    ppermute x2, starting transfers between devices, gathered(): m1, m2 = (first(message), second(message))  4.52 us
    pallas_call x1, Pallas kernels, fetch(): pl.pallas_call(functools.partial(fetch_kernel, start=start, chunk=chunk),...  4.39 us
    ppermute x3, starting transfers between devices, gathered(): lax.ppermute(near, 'tensor', [(i, i ^ s) for i in range(parts)])  4.39 us
    pallas_call x1, Pallas kernels, down_grads(): pl.pallas_call(functools.partial(down_grad_kernel, places=places, pieces=...  2.31 us
    ppermute x1, starting transfers between devices, gathered(): c3 = second(c1)  1.57 us
    ppermute x1, starting transfers between devices, gathered(): m3 = first(m2)  1.49 us
    ppermute x2, waiting for transfers between devices, gathered(): m3x, c3x = (other(m3), other(c3))  1.36 us
  transfers between devices with their start and end apart: 16, of which 4 were waited for; matrix products, arithmetic and copies ran while one was open for 0% of the time, Pallas kernels for 31%

profile of v7, /device:TPU:0, one launch (start us, length us, event | category | flops | bytes accessed | tf_op | source)
XLA Modules:
  0.0 32.5 jit_solution(4706732935013959901)
XLA Ops:
  0.6 1.2 %hidden_units.1 = (bf16[16,9216]{1,0:T(8,128)(2,1)S(1)}, bf16[32,3584]{1,0:T(8,128)(2,1)S(1)}, bf16[32,3584]{1,0:T(8,128)(2,1)S(1)}, s32[16,28]{1,0:T(8,128)S(4)}, bf16[8,4096]{1,0:T(8,128)(2,1)S(1)}) custom-call(bf16[32,3584]{1,0:T(8,128)(2,1)} %refs_0_.1, bf16[32,3584]{1,0:T(8,128)(2,1)} %refs_1_.1, s32[16,28]{1,0:T(8,128)} %bitcast.3, bf16[8,4096]{1,0:T(8,128)(2,1)} %refs_3_.1), custom_call_target="tpu_custom_call" | custom-call | tf_op jit(solution)/shard_map/hidden_units/pallas_call | solution.py:146
  1.9 3.0 %collective-permute-start.6 = (bf16[16,9216]{1,0:T(8,128)(2,1)S(1)}, bf16[16,9216]{1,0:T(8,128)(2,1)S(1)}, u32[]{:S(2)}, u32[]{:S(2)}) collective-permute-start(bf16[16,9216]{1,0:T(8,128)(2,1)S(1)} %get-tuple-element.37.refs_0_), channel_id=1, source_target_pairs={{0,16},{4,12},{8,24},{12,4},{16,0},{20,28},{24,8},{28,20},{1,17},{... | collective-permute-start | bytes 884744 | tf_op jit(solution)/shard_map/ppermute | solution.py:411
  4.9 1.5 %collective-permute-start.5 = (bf16[16,9216]{1,0:T(8,128)(2,1)S(1)}, bf16[16,9216]{1,0:T(8,128)(2,1)S(1)}, u32[]{:S(2)}, u32[]{:S(2)}) collective-permute-start(bf16[16,9216]{1,0:T(8,128)(2,1)S(1)} %get-tuple-element.37.refs_0_), channel_id=1, source_target_pairs={{0,8},{4,20},{8,0},{12,28},{16,24},{20,4},{24,16},{28,12},{1,9},{5... | collective-permute-start | bytes 884744 | tf_op jit(solution)/shard_map/ppermute | solution.py:411
  6.4 3.6 %collective-permute-start = (bf16[8,4096]{1,0:T(8,128)(2,1)S(1)}, bf16[8,4096]{1,0:T(8,128)(2,1)S(1)}, u32[]{:S(2)}, u32[]{:S(2)}) collective-permute-start(bf16[8,4096]{1,0:T(8,128)(2,1)S(1)} %get-tuple-element.35.refs_3_), channel_id=1, source_target_pairs={{0,3},{1,2},{2,1},{3,0},{4,7},{5,6},{6,5},{7,4},{8,11},{9,10},{10,... | collective-permute-start | bytes 196616 | tf_op jit(solution)/shard_map/ppermute | solution.py:412
  10.0 0.0 collective-permute-start.1
  10.0 0.8 %collective-permute-start.2 = (bf16[8,4096]{1,0:T(8,128)(2,1)S(1)}, bf16[8,4096]{1,0:T(8,128)(2,1)S(1)}, u32[]{:S(2)}, u32[]{:S(2)}) collective-permute-start(bf16[8,4096]{1,0:T(8,128)(2,1)S(1)} %get-tuple-element.35.refs_3_), channel_id=1, source_target_pairs={{0,1},{1,0},{2,3},{3,2},{4,5},{5,4},{6,7},{7,6},{8,9},{9,8},{10,11... | collective-permute-start | bytes 196616 | tf_op jit(solution)/shard_map/ppermute | solution.py:412
  10.8 4.4 %fetch.1.refs_4_ = bf16[22,2048,128]{2,1,0:T(8,128)(2,1)S(1)} custom-call(bf16[28,2048,128]{2,1,0:T(8,128)(2,1)} %refs_5_.1), custom_call_target="tpu_custom_call" | custom-call | bytes 5767168 | tf_op jit(solution)/shard_map/fetch/pallas_call | solution.py:171
  15.2 0.0 collective-permute-done.refs_0_
  15.2 0.1 collective-permute-done.1.refs_1_
  15.2 0.0 collective-permute-done.2.refs_2_
  15.3 0.1 assemble.1
  15.3 0.0 collective-permute-done.6.refs_2_
  15.4 0.0 collective-permute-done.5.refs_1_
  15.4 0.1 pack.1
  15.5 0.1 collective-permute-start.10
  15.5 0.6 %collective-permute-start.3 = (bf16[16,4096]{1,0:T(8,128)(2,1)S(1)}, bf16[16,4096]{1,0:T(8,128)(2,1)S(1)}, u32[]{:S(2)}, u32[]{:S(2)}) collective-permute-start(bf16[16,4096]{1,0:T(8,128)(2,1)S(1)} %get-tuple-element.36), channel_id=1, source_target_pairs={{0,8},{4,20},{8,0},{12,28},{16,24},{20,4},{24,16},{28,12},{1,9},{5... | collective-permute-start | bytes 393224 | tf_op jit(solution)/shard_map/ppermute | solution.py:418
  16.1 0.5 %collective-permute-start.4 = (bf16[16,4096]{1,0:T(8,128)(2,1)S(1)}, bf16[16,4096]{1,0:T(8,128)(2,1)S(1)}, u32[]{:S(2)}, u32[]{:S(2)}) collective-permute-start(bf16[16,4096]{1,0:T(8,128)(2,1)S(1)} %get-tuple-element.36), channel_id=1, source_target_pairs={{0,16},{4,12},{8,24},{12,4},{16,0},{20,28},{24,8},{28,20},{1,17},{... | collective-permute-start | bytes 393224 | tf_op jit(solution)/shard_map/ppermute | solution.py:418
  16.6 1.2 %collective-permute-start.7 = (bf16[32,2048]{1,0:T(8,128)(2,1)S(1)}, bf16[32,2048]{1,0:T(8,128)(2,1)S(1)}, u32[]{:S(2)}, u32[]{:S(2)}) collective-permute-start(bf16[32,2048]{1,0:T(8,128)(2,1)S(1)} %get-tuple-element.39), channel_id=1, source_target_pairs={{0,1},{1,0},{2,3},{3,2},{4,5},{5,4},{6,7},{7,6},{8,9},{9,8},{10,11... | collective-permute-start | bytes 393224 | tf_op jit(solution)/shard_map/ppermute | solution.py:420
  17.9 1.5 %collective-permute-start.9 = (bf16[16,9216]{1,0:T(8,128)(2,1)S(1)}, bf16[16,9216]{1,0:T(8,128)(2,1)S(1)}, u32[]{:S(2)}, u32[]{:S(2)}) collective-permute-start(bf16[16,9216]{1,0:T(8,128)(2,1)S(1)} %collective-permute-done.6.refs_2_), channel_id=1, source_target_pairs={{0,8},{4,20},{8,0},{12,28},{16,24},{20,4},{24,16},{28,12},{1,9},{5... | collective-permute-start | bytes 884744 | tf_op jit(solution)/shard_map/ppermute | solution.py:421
  19.4 3.0 %hidden_grads.2 = (bf16[32,1792]{1,0:T(8,128)(2,1)S(1)}, bf16[32,1792]{1,0:T(8,128)(2,1)S(1)}, bf16[6,2048,128]{2,1,0:T(8,128)(2,1)S(1)}) custom-call(s32[16,28]{1,0:T(8,128)S(4)} %get-tuple-element.34.refs_0_.index_ref, bf16[32,4096]{1,0:T(8,128)(2,1)S(1)} %get-tuple-element.40.refs_1_, bf16[32,3584]{1,0:T(8,128)(2,1)S(1)} %get-tuple-element.41.refs_2_, ...), custom_call_target="tpu_custom_call" | custom-call | flops 234881024 | bytes 7340032 | tf_op jit(solution)/shard_map/hidden_grads/pallas_call | solution.py:221
  22.4 0.0 collective-permute-done.3.refs_1_
  22.4 0.1 collective-permute-done.4.refs_2_
  22.5 0.0 collective-permute-done.7.refs_0_
  22.5 0.0 collective-permute-start.11
  22.6 1.6 %collective-permute-start.8 = (bf16[16,6144]{1,0:T(8,128)(2,1)S(1)}, bf16[16,6144]{1,0:T(8,128)(2,1)S(1)}, u32[]{:S(2)}, u32[]{:S(2)}) collective-permute-start(bf16[16,6144]{1,0:T(8,128)(2,1)S(1)} %get-tuple-element.48.refs_4_), channel_id=1, source_target_pairs={{0,16},{4,12},{8,24},{12,4},{16,0},{20,28},{24,8},{28,20},{1,17},{... | collective-permute-start | bytes 589832 | tf_op jit(solution)/shard_map/ppermute | solution.py:427
  24.1 0.0 collective-permute-start.12
  24.1 0.0 collective-permute-done.11.refs_0_
  24.1 0.5 %collective-permute-start.13 = (bf16[16,4096]{1,0:T(8,128)(2,1)S(1)}, bf16[16,4096]{1,0:T(8,128)(2,1)S(1)}, u32[]{:S(2)}, u32[]{:S(2)}) collective-permute-start(bf16[16,4096]{1,0:T(8,128)(2,1)S(1)} %collective-permute-done.4.refs_2_), channel_id=1, source_target_pairs={{0,4},{4,0},{8,12},{12,8},{16,20},{20,16},{24,28},{28,24},{1,5},{5... | collective-permute-start | bytes 393224 | tf_op jit(solution)/shard_map/ppermute | solution.py:428
  24.6 2.0 %hidden_grads.3 = (bf16[32,3584]{1,0:T(8,128)(2,1)}, bf16[32,3584]{1,0:T(8,128)(2,1)}) custom-call(s32[16,28]{1,0:T(8,128)S(4)} %get-tuple-element.34.refs_0_.index_ref, bf16[32,4096]{1,0:T(8,128)(2,1)S(1)} %get-tuple-element.40.refs_1_, bf16[32,3584]{1,0:T(8,128)(2,1)S(1)} %get-tuple-element.41.refs_2_, bf16[32,3584]{1,0:T(8,128)(2,1)S(1)} %get-tuple-element.42.refs_3_, ...), custom_call_target="tpu_custom_call" | custom-call | flops 234881024 | bytes 7340032 | tf_op jit(solution)/shard_map/hidden_grads/pallas_call | solution.py:221
  26.7 0.0 collective-permute-done.12.refs_1_
  26.7 0.0 collective-permute-done.13.refs_2_
  26.7 0.0 collective-permute-done.10.refs_2_.refs_3_.refs_1_
  26.7 0.3 turn.1.turned
  27.1 0.0 collective-permute-done.9.refs_2_
  27.1 1.2 %collective-permute-done.8.refs_6_ = bf16[16,6144]{1,0:T(8,128)(2,1)S(1)} collective-permute-done((bf16[16,6144]{1,0:T(8,128)(2,1)S(1)}, bf16[16,6144]{1,0:T(8,128)(2,1)S(1)}, u32[]{:S(2)}, u32[]{:S(2)}) %collective-permute-start.8) | collective-permute-done | bytes 196640 | tf_op jit(solution)/shard_map/ppermute | solution.py:427
  28.3 0.0 collective-permute-start.14
  28.3 0.5 %collective-permute-start.15 = (bf16[16,6144]{1,0:T(8,128)(2,1)S(1)}, bf16[16,6144]{1,0:T(8,128)(2,1)S(1)}, u32[]{:S(2)}, u32[]{:S(2)}) collective-permute-start(bf16[16,6144]{1,0:T(8,128)(2,1)S(1)} %collective-permute-done.8.refs_6_), channel_id=1, source_target_pairs={{0,4},{4,0},{8,12},{12,8},{16,20},{20,16},{24,28},{28,24},{1,5},{5... | collective-permute-start | bytes 589832 | tf_op jit(solution)/shard_map/ppermute | solution.py:436
  28.8 1.4 %collective-permute-done.15.refs_7_ = bf16[16,6144]{1,0:T(8,128)(2,1)S(1)} collective-permute-done((bf16[16,6144]{1,0:T(8,128)(2,1)S(1)}, bf16[16,6144]{1,0:T(8,128)(2,1)S(1)}, u32[]{:S(2)}, u32[]{:S(2)}) %collective-permute-start.15) | collective-permute-done | bytes 196640 | tf_op jit(solution)/shard_map/ppermute | solution.py:436
  30.2 0.0 collective-permute-done.14.refs_3_
  30.2 2.3 %down_grads.1 = f32[28,256,128]{2,1,0:T(8,128)} custom-call(s32[16,28]{1,0:T(8,128)S(4)} %get-tuple-element.34.refs_0_.index_ref, bf16[32,128,128]{2,1,0:T(8,128)(2,1)S(1)} %turn.1.turned, bf16[64,9216]{1,0:T(8,128)(2,1)S(1)} %get-tuple-element.49.refs_0_, bf16[64,9216]{1,0:T(8,128)(2,1)S(1)} %collective-permute-done.10.refs_2_.refs_3_.refs_1_, ...), custom_call_target="tpu_custom_call" | custom-call | flops 469762048 | bytes 3670016 | tf_op jit(solution)/shard_map/down_grads/pallas_call | solution.py:377
  (2 shorter events, 0.1 us)
Async XLA Ops:
  1.9 13.5 %collective-permute-start.6 = (bf16[16,9216]{1,0:T(8,128)(2,1)S(1)}, bf16[16,9216]{1,0:T(8,128)(2,1)S(1)}, u32[]{:S(2)}, u32[]{:S(2)}) collective-permute-start(bf16[16,9216]{1,0:T(8,128)(2,1)S(1)} %get-tuple-element.37.refs_0_), channel_id=1, source_target_pairs={{0,16},{4,12},{8,24},{12,4},{16,0},{20,28},{24,8},{28,20},{1,17},{... | collective-permute-start | bytes 884744 | tf_op jit(solution)/shard_map/ppermute | solution.py:411
  4.9 10.5 %collective-permute-start.5 = (bf16[16,9216]{1,0:T(8,128)(2,1)S(1)}, bf16[16,9216]{1,0:T(8,128)(2,1)S(1)}, u32[]{:S(2)}, u32[]{:S(2)}) collective-permute-start(bf16[16,9216]{1,0:T(8,128)(2,1)S(1)} %get-tuple-element.37.refs_0_), channel_id=1, source_target_pairs={{0,8},{4,20},{8,0},{12,28},{16,24},{20,4},{24,16},{28,12},{1,9},{5... | collective-permute-start | bytes 884744 | tf_op jit(solution)/shard_map/ppermute | solution.py:411
  6.4 8.8 %collective-permute-start = (bf16[8,4096]{1,0:T(8,128)(2,1)S(1)}, bf16[8,4096]{1,0:T(8,128)(2,1)S(1)}, u32[]{:S(2)}, u32[]{:S(2)}) collective-permute-start(bf16[8,4096]{1,0:T(8,128)(2,1)S(1)} %get-tuple-element.35.refs_3_), channel_id=1, source_target_pairs={{0,3},{1,2},{2,1},{3,0},{4,7},{5,6},{6,5},{7,4},{8,11},{9,10},{10,... | collective-permute-start | bytes 196616 | tf_op jit(solution)/shard_map/ppermute | solution.py:412
  10.0 5.2 %collective-permute-start.1 = (bf16[8,4096]{1,0:T(8,128)(2,1)S(1)}, bf16[8,4096]{1,0:T(8,128)(2,1)S(1)}, u32[]{:S(2)}, u32[]{:S(2)}) collective-permute-start(bf16[8,4096]{1,0:T(8,128)(2,1)S(1)} %get-tuple-element.35.refs_3_), channel_id=1, source_target_pairs={{0,2},{1,3},{2,0},{3,1},{4,6},{5,7},{6,4},{7,5},{8,10},{9,11},{10,... | collective-permute-start | bytes 196616 | tf_op jit(solution)/shard_map/ppermute | solution.py:412
  10.0 5.2 %collective-permute-start.2 = (bf16[8,4096]{1,0:T(8,128)(2,1)S(1)}, bf16[8,4096]{1,0:T(8,128)(2,1)S(1)}, u32[]{:S(2)}, u32[]{:S(2)}) collective-permute-start(bf16[8,4096]{1,0:T(8,128)(2,1)S(1)} %get-tuple-element.35.refs_3_), channel_id=1, source_target_pairs={{0,1},{1,0},{2,3},{3,2},{4,5},{5,4},{6,7},{7,6},{8,9},{9,8},{10,11... | collective-permute-start | bytes 196616 | tf_op jit(solution)/shard_map/ppermute | solution.py:412
  15.5 11.3 %collective-permute-start.10 = (bf16[64,9216]{1,0:T(8,128)(2,1)S(1)}, bf16[64,9216]{1,0:T(8,128)(2,1)S(1)}, u32[]{:S(2)}, u32[]{:S(2)}) collective-permute-start(bf16[64,9216]{1,0:T(8,128)(2,1)S(1)} %get-tuple-element.49.refs_0_), channel_id=1, source_target_pairs={{0,4},{4,0},{8,12},{12,8},{16,20},{20,16},{24,28},{28,24},{1,5},{5... | collective-permute-start | bytes 3538952 | tf_op jit(solution)/shard_map/ppermute | solution.py:422
  15.5 6.9 %collective-permute-start.3 = (bf16[16,4096]{1,0:T(8,128)(2,1)S(1)}, bf16[16,4096]{1,0:T(8,128)(2,1)S(1)}, u32[]{:S(2)}, u32[]{:S(2)}) collective-permute-start(bf16[16,4096]{1,0:T(8,128)(2,1)S(1)} %get-tuple-element.36), channel_id=1, source_target_pairs={{0,8},{4,20},{8,0},{12,28},{16,24},{20,4},{24,16},{28,12},{1,9},{5... | collective-permute-start | bytes 393224 | tf_op jit(solution)/shard_map/ppermute | solution.py:418
  16.1 6.4 %collective-permute-start.4 = (bf16[16,4096]{1,0:T(8,128)(2,1)S(1)}, bf16[16,4096]{1,0:T(8,128)(2,1)S(1)}, u32[]{:S(2)}, u32[]{:S(2)}) collective-permute-start(bf16[16,4096]{1,0:T(8,128)(2,1)S(1)} %get-tuple-element.36), channel_id=1, source_target_pairs={{0,16},{4,12},{8,24},{12,4},{16,0},{20,28},{24,8},{28,20},{1,17},{... | collective-permute-start | bytes 393224 | tf_op jit(solution)/shard_map/ppermute | solution.py:418
  16.6 5.9 %collective-permute-start.7 = (bf16[32,2048]{1,0:T(8,128)(2,1)S(1)}, bf16[32,2048]{1,0:T(8,128)(2,1)S(1)}, u32[]{:S(2)}, u32[]{:S(2)}) collective-permute-start(bf16[32,2048]{1,0:T(8,128)(2,1)S(1)} %get-tuple-element.39), channel_id=1, source_target_pairs={{0,1},{1,0},{2,3},{3,2},{4,5},{5,4},{6,7},{7,6},{8,9},{9,8},{10,11... | collective-permute-start | bytes 393224 | tf_op jit(solution)/shard_map/ppermute | solution.py:420
  17.9 9.2 %collective-permute-start.9 = (bf16[16,9216]{1,0:T(8,128)(2,1)S(1)}, bf16[16,9216]{1,0:T(8,128)(2,1)S(1)}, u32[]{:S(2)}, u32[]{:S(2)}) collective-permute-start(bf16[16,9216]{1,0:T(8,128)(2,1)S(1)} %collective-permute-done.6.refs_2_), channel_id=1, source_target_pairs={{0,8},{4,20},{8,0},{12,28},{16,24},{20,4},{24,16},{28,12},{1,9},{5... | collective-permute-start | bytes 884744 | tf_op jit(solution)/shard_map/ppermute | solution.py:421
  22.5 1.6 %collective-permute-start.11 = (bf16[32,2048]{1,0:T(8,128)(2,1)S(1)}, bf16[32,2048]{1,0:T(8,128)(2,1)S(1)}, u32[]{:S(2)}, u32[]{:S(2)}) collective-permute-start(bf16[32,2048]{1,0:T(8,128)(2,1)S(1)} %collective-permute-done.7.refs_0_), channel_id=1, source_target_pairs={{0,4},{4,0},{8,12},{12,8},{16,20},{20,16},{24,28},{28,24},{1,5},{5... | collective-permute-start | bytes 393224 | tf_op jit(solution)/shard_map/ppermute | solution.py:428
  22.6 5.7 %collective-permute-start.8 = (bf16[16,6144]{1,0:T(8,128)(2,1)S(1)}, bf16[16,6144]{1,0:T(8,128)(2,1)S(1)}, u32[]{:S(2)}, u32[]{:S(2)}) collective-permute-start(bf16[16,6144]{1,0:T(8,128)(2,1)S(1)} %get-tuple-element.48.refs_4_), channel_id=1, source_target_pairs={{0,16},{4,12},{8,24},{12,4},{16,0},{20,28},{24,8},{28,20},{1,17},{... | collective-permute-start | bytes 589832 | tf_op jit(solution)/shard_map/ppermute | solution.py:427
  24.1 2.6 %collective-permute-start.12 = (bf16[16,4096]{1,0:T(8,128)(2,1)S(1)}, bf16[16,4096]{1,0:T(8,128)(2,1)S(1)}, u32[]{:S(2)}, u32[]{:S(2)}) collective-permute-start(bf16[16,4096]{1,0:T(8,128)(2,1)S(1)} %collective-permute-done.3.refs_1_), channel_id=1, source_target_pairs={{0,4},{4,0},{8,12},{12,8},{16,20},{20,16},{24,28},{28,24},{1,5},{5... | collective-permute-start | bytes 393224 | tf_op jit(solution)/shard_map/ppermute | solution.py:428
  24.1 2.6 %collective-permute-start.13 = (bf16[16,4096]{1,0:T(8,128)(2,1)S(1)}, bf16[16,4096]{1,0:T(8,128)(2,1)S(1)}, u32[]{:S(2)}, u32[]{:S(2)}) collective-permute-start(bf16[16,4096]{1,0:T(8,128)(2,1)S(1)} %collective-permute-done.4.refs_2_), channel_id=1, source_target_pairs={{0,4},{4,0},{8,12},{12,8},{16,20},{20,16},{24,28},{28,24},{1,5},{5... | collective-permute-start | bytes 393224 | tf_op jit(solution)/shard_map/ppermute | solution.py:428
  28.3 1.9 %collective-permute-start.14 = (bf16[16,9216]{1,0:T(8,128)(2,1)S(1)}, bf16[16,9216]{1,0:T(8,128)(2,1)S(1)}, u32[]{:S(2)}, u32[]{:S(2)}) collective-permute-start(bf16[16,9216]{1,0:T(8,128)(2,1)S(1)} %collective-permute-done.9.refs_2_), channel_id=1, source_target_pairs={{0,4},{4,0},{8,12},{12,8},{16,20},{20,16},{24,28},{28,24},{1,5},{5... | collective-permute-start | bytes 884744 | tf_op jit(solution)/shard_map/ppermute | solution.py:436
  28.3 1.9 %collective-permute-start.15 = (bf16[16,6144]{1,0:T(8,128)(2,1)S(1)}, bf16[16,6144]{1,0:T(8,128)(2,1)S(1)}, u32[]{:S(2)}, u32[]{:S(2)}) collective-permute-start(bf16[16,6144]{1,0:T(8,128)(2,1)S(1)} %collective-permute-done.8.refs_6_), channel_id=1, source_target_pairs={{0,4},{4,0},{8,12},{12,8},{16,20},{20,16},{24,28},{28,24},{1,5},{5... | collective-permute-start | bytes 589832 | tf_op jit(solution)/shard_map/ppermute | solution.py:436

commit v8 on v7

--- a/solution.py
+++ b/solution.py
@@ -411,8 +411,8 @@
     m1, m2 = first(message), second(message)
     slices = [lax.ppermute(near, "tensor", [(i, i ^ s) for i in range(parts)]) for s in range(1, parts)]
     blocks = down_blocks.shape[0]
-    half = blocks // 2
-    ahead = blocks * 3 // 14
+    half = blocks // 7
+    ahead = blocks * 2 // 7
     held = [fetch(down_blocks, 0, blocks - ahead)]
     cot, sent, far = assemble([near] + slices, held)
     c1, c2 = first(far), second(far)

time: 32.7 us -> 32.7 us (level)
  starting transfers between devices: 15.4 us -> 14.7 us
  waiting for transfers between devices: 2.76 us -> 3.43 us
    ppermute x2, waiting for transfers between devices: 0.11 us -> 0.95 us  [gathered(): c1, c2 = (first(far), second(far))]
    ppermute x1, starting transfers between devices: 1.57 us -> 0.99 us  [gathered(): c3 = second(c1)]
    ppermute x1, waiting for transfers between devices: 1.21 us -> 0.73 us  [gathered(): c3 = second(c1)]
  transfers between devices with their start and end apart: 16 -> 16, of which waited for: 4 -> 5; matrix products, arithmetic and copies ran while one was open for 0% -> 0% of each run, Pallas kernels for 31% -> 31%
where the time goes in v8:
time: 32.7 us; the launch traced here: 32.5 us
  starting transfers between devices  14.7 us (45%)
  Pallas kernels  13.6 us (42%)
  waiting for transfers between devices  3.43 us (10%)
  between operations  0.75 us (2%)
    pallas_call x2, Pallas kernels, hidden_grads(): pl.pallas_call(functools.partial(hidden_grad_kernel, start=start, fetched...  5.37 us
    ppermute x2, starting transfers between devices, gathered(): m1, m2 = (first(message), second(message))  4.52 us
    ppermute x3, starting transfers between devices, gathered(): lax.ppermute(near, 'tensor', [(i, i ^ s) for i in range(parts)])  4.39 us
    pallas_call x1, Pallas kernels, fetch(): pl.pallas_call(functools.partial(fetch_kernel, start=start, chunk=chunk),...  4.09 us
    pallas_call x1, Pallas kernels, down_grads(): pl.pallas_call(functools.partial(down_grad_kernel, places=places, pieces=...  2.32 us
    ppermute x1, starting transfers between devices, gathered(): m3 = first(m2)  1.49 us
    ppermute x2, waiting for transfers between devices, gathered(): m3x, c3x = (other(m3), other(c3))  1.36 us
    pallas_call x1, Pallas kernels, hidden_units(): pl.pallas_call(functools.partial(hidden_kernel, kept=len(arrays)), in_spe...  1.23 us
  transfers between devices with their start and end apart: 16, of which 5 were waited for; matrix products, arithmetic and copies ran while one was open for 0% of the time, Pallas kernels for 31%

profile of v8, /device:TPU:0, one launch (start us, length us, event | category | flops | bytes accessed | tf_op | source)
XLA Modules:
  0.0 32.5 jit_solution(12494080711218570851)
XLA Ops:
  0.6 1.2 %hidden_units.1 = (bf16[16,9216]{1,0:T(8,128)(2,1)S(1)}, bf16[32,3584]{1,0:T(8,128)(2,1)S(1)}, bf16[32,3584]{1,0:T(8,128)(2,1)S(1)}, s32[16,28]{1,0:T(8,128)S(4)}, bf16[8,4096]{1,0:T(8,128)(2,1)S(1)}) custom-call(bf16[32,3584]{1,0:T(8,128)(2,1)} %refs_0_.1, bf16[32,3584]{1,0:T(8,128)(2,1)} %refs_1_.1, s32[16,28]{1,0:T(8,128)} %bitcast.3, bf16[8,4096]{1,0:T(8,128)(2,1)} %refs_3_.1), custom_call_target="tpu_custom_call" | custom-call | tf_op jit(solution)/shard_map/hidden_units/pallas_call | solution.py:146
  1.9 3.0 %collective-permute-start.6 = (bf16[16,9216]{1,0:T(8,128)(2,1)S(1)}, bf16[16,9216]{1,0:T(8,128)(2,1)S(1)}, u32[]{:S(2)}, u32[]{:S(2)}) collective-permute-start(bf16[16,9216]{1,0:T(8,128)(2,1)S(1)} %get-tuple-element.37.refs_0_), channel_id=1, source_target_pairs={{0,16},{4,12},{8,24},{12,4},{16,0},{20,28},{24,8},{28,20},{1,17},{... | collective-permute-start | bytes 884744 | tf_op jit(solution)/shard_map/ppermute | solution.py:411
  4.9 1.5 %collective-permute-start.5 = (bf16[16,9216]{1,0:T(8,128)(2,1)S(1)}, bf16[16,9216]{1,0:T(8,128)(2,1)S(1)}, u32[]{:S(2)}, u32[]{:S(2)}) collective-permute-start(bf16[16,9216]{1,0:T(8,128)(2,1)S(1)} %get-tuple-element.37.refs_0_), channel_id=1, source_target_pairs={{0,8},{4,20},{8,0},{12,28},{16,24},{20,4},{24,16},{28,12},{1,9},{5... | collective-permute-start | bytes 884744 | tf_op jit(solution)/shard_map/ppermute | solution.py:411
  6.4 3.6 %collective-permute-start = (bf16[8,4096]{1,0:T(8,128)(2,1)S(1)}, bf16[8,4096]{1,0:T(8,128)(2,1)S(1)}, u32[]{:S(2)}, u32[]{:S(2)}) collective-permute-start(bf16[8,4096]{1,0:T(8,128)(2,1)S(1)} %get-tuple-element.35.refs_3_), channel_id=1, source_target_pairs={{0,3},{1,2},{2,1},{3,0},{4,7},{5,6},{6,5},{7,4},{8,11},{9,10},{10,... | collective-permute-start | bytes 196616 | tf_op jit(solution)/shard_map/ppermute | solution.py:412
  10.0 0.0 collective-permute-start.1
  10.0 0.8 %collective-permute-start.2 = (bf16[8,4096]{1,0:T(8,128)(2,1)S(1)}, bf16[8,4096]{1,0:T(8,128)(2,1)S(1)}, u32[]{:S(2)}, u32[]{:S(2)}) collective-permute-start(bf16[8,4096]{1,0:T(8,128)(2,1)S(1)} %get-tuple-element.35.refs_3_), channel_id=1, source_target_pairs={{0,1},{1,0},{2,3},{3,2},{4,5},{5,4},{6,7},{7,6},{8,9},{9,8},{10,11... | collective-permute-start | bytes 196616 | tf_op jit(solution)/shard_map/ppermute | solution.py:412
  10.8 4.1 %fetch.1.refs_4_ = bf16[20,2048,128]{2,1,0:T(8,128)(2,1)S(1)} custom-call(bf16[28,2048,128]{2,1,0:T(8,128)(2,1)} %refs_5_.1), custom_call_target="tpu_custom_call" | custom-call | bytes 5242880 | tf_op jit(solution)/shard_map/fetch/pallas_call | solution.py:171
  14.9 0.0 collective-permute-done.refs_0_
  14.9 0.4 %collective-permute-done.1.refs_1_ = bf16[8,4096]{1,0:T(8,128)(2,1)S(1)} collective-permute-done((bf16[8,4096]{1,0:T(8,128)(2,1)S(1)}, bf16[8,4096]{1,0:T(8,128)(2,1)S(1)}, u32[]{:S(2)}, u32[]{:S(2)}) %collective-permute-start.1) | collective-permute-done | bytes 65568 | tf_op jit(solution)/shard_map/ppermute | solution.py:412
  15.2 0.0 collective-permute-done.2.refs_2_
  15.3 0.1 assemble.1
  15.3 0.0 collective-permute-done.6.refs_2_
  15.4 0.0 collective-permute-done.5.refs_1_
  15.4 0.1 pack.1
  15.5 0.1 collective-permute-start.10
  15.5 0.6 %collective-permute-start.3 = (bf16[16,4096]{1,0:T(8,128)(2,1)S(1)}, bf16[16,4096]{1,0:T(8,128)(2,1)S(1)}, u32[]{:S(2)}, u32[]{:S(2)}) collective-permute-start(bf16[16,4096]{1,0:T(8,128)(2,1)S(1)} %get-tuple-element.36), channel_id=1, source_target_pairs={{0,8},{4,20},{8,0},{12,28},{16,24},{20,4},{24,16},{28,12},{1,9},{5... | collective-permute-start | bytes 393224 | tf_op jit(solution)/shard_map/ppermute | solution.py:418
  16.1 0.5 %collective-permute-start.4 = (bf16[16,4096]{1,0:T(8,128)(2,1)S(1)}, bf16[16,4096]{1,0:T(8,128)(2,1)S(1)}, u32[]{:S(2)}, u32[]{:S(2)}) collective-permute-start(bf16[16,4096]{1,0:T(8,128)(2,1)S(1)} %get-tuple-element.36), channel_id=1, source_target_pairs={{0,16},{4,12},{8,24},{12,4},{16,0},{20,28},{24,8},{28,20},{1,17},{... | collective-permute-start | bytes 393224 | tf_op jit(solution)/shard_map/ppermute | solution.py:418
  16.6 0.9 %collective-permute-start.7 = (bf16[32,2048]{1,0:T(8,128)(2,1)S(1)}, bf16[32,2048]{1,0:T(8,128)(2,1)S(1)}, u32[]{:S(2)}, u32[]{:S(2)}) collective-permute-start(bf16[32,2048]{1,0:T(8,128)(2,1)S(1)} %get-tuple-element.39), channel_id=1, source_target_pairs={{0,1},{1,0},{2,3},{3,2},{4,5},{5,4},{6,7},{7,6},{8,9},{9,8},{10,11... | collective-permute-start | bytes 393224 | tf_op jit(solution)/shard_map/ppermute | solution.py:420
  17.6 1.5 %collective-permute-start.9 = (bf16[16,9216]{1,0:T(8,128)(2,1)S(1)}, bf16[16,9216]{1,0:T(8,128)(2,1)S(1)}, u32[]{:S(2)}, u32[]{:S(2)}) collective-permute-start(bf16[16,9216]{1,0:T(8,128)(2,1)S(1)} %collective-permute-done.6.refs_2_), channel_id=1, source_target_pairs={{0,8},{4,20},{8,0},{12,28},{16,24},{20,4},{24,16},{28,12},{1,9},{5... | collective-permute-start | bytes 884744 | tf_op jit(solution)/shard_map/ppermute | solution.py:421
  19.1 2.5 %hidden_grads.2 = (bf16[32,512]{1,0:T(8,128)(2,1)S(1)}, bf16[32,512]{1,0:T(8,128)(2,1)S(1)}, bf16[8,2048,128]{2,1,0:T(8,128)(2,1)S(1)}) custom-call(s32[16,28]{1,0:T(8,128)S(4)} %get-tuple-element.34.refs_0_.index_ref, bf16[32,4096]{1,0:T(8,128)(2,1)S(1)} %get-tuple-element.40.refs_1_, bf16[32,3584]{1,0:T(8,128)(2,1)S(1)} %get-tuple-element.41.refs_2_, ...), custom_call_target="tpu_custom_call" | custom-call | flops 67108864 | bytes 2097152 | tf_op jit(solution)/shard_map/hidden_grads/pallas_call | solution.py:221
  21.6 0.1 collective-permute-done.3.refs_1_
  21.7 0.8 %collective-permute-done.4.refs_2_ = bf16[16,4096]{1,0:T(8,128)(2,1)S(1)} collective-permute-done((bf16[16,4096]{1,0:T(8,128)(2,1)S(1)}, bf16[16,4096]{1,0:T(8,128)(2,1)S(1)}, u32[]{:S(2)}, u32[]{:S(2)}) %collective-permute-start.4) | collective-permute-done | bytes 131104 | tf_op jit(solution)/shard_map/ppermute | solution.py:418
  22.5 0.0 collective-permute-done.7.refs_0_
  22.5 0.0 collective-permute-start.11
  22.6 1.0 %collective-permute-start.8 = (bf16[16,6144]{1,0:T(8,128)(2,1)S(1)}, bf16[16,6144]{1,0:T(8,128)(2,1)S(1)}, u32[]{:S(2)}, u32[]{:S(2)}) collective-permute-start(bf16[16,6144]{1,0:T(8,128)(2,1)S(1)} %get-tuple-element.48.refs_4_), channel_id=1, source_target_pairs={{0,16},{4,12},{8,24},{12,4},{16,0},{20,28},{24,8},{28,20},{1,17},{... | collective-permute-start | bytes 589832 | tf_op jit(solution)/shard_map/ppermute | solution.py:427
  23.5 0.8 %collective-permute-start.12 = (bf16[16,4096]{1,0:T(8,128)(2,1)S(1)}, bf16[16,4096]{1,0:T(8,128)(2,1)S(1)}, u32[]{:S(2)}, u32[]{:S(2)}) collective-permute-start(bf16[16,4096]{1,0:T(8,128)(2,1)S(1)} %collective-permute-done.3.refs_1_), channel_id=1, source_target_pairs={{0,4},{4,0},{8,12},{12,8},{16,20},{20,16},{24,28},{28,24},{1,5},{5... | collective-permute-start | bytes 393224 | tf_op jit(solution)/shard_map/ppermute | solution.py:428
  24.3 0.0 collective-permute-done.11.refs_0_
  24.3 0.0 collective-permute-start.13
  24.3 2.9 %hidden_grads.3 = (bf16[32,3584]{1,0:T(8,128)(2,1)}, bf16[32,3584]{1,0:T(8,128)(2,1)}) custom-call(s32[16,28]{1,0:T(8,128)S(4)} %get-tuple-element.34.refs_0_.index_ref, bf16[32,4096]{1,0:T(8,128)(2,1)S(1)} %get-tuple-element.40.refs_1_, bf16[32,3584]{1,0:T(8,128)(2,1)S(1)} %get-tuple-element.41.refs_2_, bf16[32,3584]{1,0:T(8,128)(2,1)S(1)} %get-tuple-element.42.refs_3_, ...), custom_call_target="tpu_custom_call" | custom-call | flops 402653184 | bytes 12582912 | tf_op jit(solution)/shard_map/hidden_grads/pallas_call | solution.py:221
  27.2 0.0 collective-permute-done.12.refs_1_
  27.2 0.0 collective-permute-done.13.refs_2_
  27.2 0.0 collective-permute-done.10.refs_2_.refs_3_.refs_1_
  27.2 0.3 turn.1.turned
  27.5 0.0 collective-permute-done.9.refs_2_
  27.6 0.7 %collective-permute-done.8.refs_6_ = bf16[16,6144]{1,0:T(8,128)(2,1)S(1)} collective-permute-done((bf16[16,6144]{1,0:T(8,128)(2,1)S(1)}, bf16[16,6144]{1,0:T(8,128)(2,1)S(1)}, u32[]{:S(2)}, u32[]{:S(2)}) %collective-permute-start.8) | collective-permute-done | bytes 196640 | tf_op jit(solution)/shard_map/ppermute | solution.py:427
  28.3 0.0 collective-permute-start.14
  28.3 0.5 %collective-permute-start.15 = (bf16[16,6144]{1,0:T(8,128)(2,1)S(1)}, bf16[16,6144]{1,0:T(8,128)(2,1)S(1)}, u32[]{:S(2)}, u32[]{:S(2)}) collective-permute-start(bf16[16,6144]{1,0:T(8,128)(2,1)S(1)} %collective-permute-done.8.refs_6_), channel_id=1, source_target_pairs={{0,4},{4,0},{8,12},{12,8},{16,20},{20,16},{24,28},{28,24},{1,5},{5... | collective-permute-start | bytes 589832 | tf_op jit(solution)/shard_map/ppermute | solution.py:436
  28.8 1.4 %collective-permute-done.15.refs_7_ = bf16[16,6144]{1,0:T(8,128)(2,1)S(1)} collective-permute-done((bf16[16,6144]{1,0:T(8,128)(2,1)S(1)}, bf16[16,6144]{1,0:T(8,128)(2,1)S(1)}, u32[]{:S(2)}, u32[]{:S(2)}) %collective-permute-start.15) | collective-permute-done | bytes 196640 | tf_op jit(solution)/shard_map/ppermute | solution.py:436
  30.2 0.0 collective-permute-done.14.refs_3_
  30.2 2.3 %down_grads.1 = f32[28,256,128]{2,1,0:T(8,128)} custom-call(s32[16,28]{1,0:T(8,128)S(4)} %get-tuple-element.34.refs_0_.index_ref, bf16[32,128,128]{2,1,0:T(8,128)(2,1)S(1)} %turn.1.turned, bf16[64,9216]{1,0:T(8,128)(2,1)S(1)} %get-tuple-element.49.refs_0_, bf16[64,9216]{1,0:T(8,128)(2,1)S(1)} %collective-permute-done.10.refs_2_.refs_3_.refs_1_, ...), custom_call_target="tpu_custom_call" | custom-call | flops 469762048 | bytes 3670016 | tf_op jit(solution)/shard_map/down_grads/pallas_call | solution.py:377
  (2 shorter events, 0.1 us)
Async XLA Ops:
  1.9 13.5 %collective-permute-start.6 = (bf16[16,9216]{1,0:T(8,128)(2,1)S(1)}, bf16[16,9216]{1,0:T(8,128)(2,1)S(1)}, u32[]{:S(2)}, u32[]{:S(2)}) collective-permute-start(bf16[16,9216]{1,0:T(8,128)(2,1)S(1)} %get-tuple-element.37.refs_0_), channel_id=1, source_target_pairs={{0,16},{4,12},{8,24},{12,4},{16,0},{20,28},{24,8},{28,20},{1,17},{... | collective-permute-start | bytes 884744 | tf_op jit(solution)/shard_map/ppermute | solution.py:411
  4.9 10.5 %collective-permute-start.5 = (bf16[16,9216]{1,0:T(8,128)(2,1)S(1)}, bf16[16,9216]{1,0:T(8,128)(2,1)S(1)}, u32[]{:S(2)}, u32[]{:S(2)}) collective-permute-start(bf16[16,9216]{1,0:T(8,128)(2,1)S(1)} %get-tuple-element.37.refs_0_), channel_id=1, source_target_pairs={{0,8},{4,20},{8,0},{12,28},{16,24},{20,4},{24,16},{28,12},{1,9},{5... | collective-permute-start | bytes 884744 | tf_op jit(solution)/shard_map/ppermute | solution.py:411
  6.4 8.5 %collective-permute-start = (bf16[8,4096]{1,0:T(8,128)(2,1)S(1)}, bf16[8,4096]{1,0:T(8,128)(2,1)S(1)}, u32[]{:S(2)}, u32[]{:S(2)}) collective-permute-start(bf16[8,4096]{1,0:T(8,128)(2,1)S(1)} %get-tuple-element.35.refs_3_), channel_id=1, source_target_pairs={{0,3},{1,2},{2,1},{3,0},{4,7},{5,6},{6,5},{7,4},{8,11},{9,10},{10,... | collective-permute-start | bytes 196616 | tf_op jit(solution)/shard_map/ppermute | solution.py:412
  10.0 5.2 %collective-permute-start.1 = (bf16[8,4096]{1,0:T(8,128)(2,1)S(1)}, bf16[8,4096]{1,0:T(8,128)(2,1)S(1)}, u32[]{:S(2)}, u32[]{:S(2)}) collective-permute-start(bf16[8,4096]{1,0:T(8,128)(2,1)S(1)} %get-tuple-element.35.refs_3_), channel_id=1, source_target_pairs={{0,2},{1,3},{2,0},{3,1},{4,6},{5,7},{6,4},{7,5},{8,10},{9,11},{10,... | collective-permute-start | bytes 196616 | tf_op jit(solution)/shard_map/ppermute | solution.py:412
  10.0 5.2 %collective-permute-start.2 = (bf16[8,4096]{1,0:T(8,128)(2,1)S(1)}, bf16[8,4096]{1,0:T(8,128)(2,1)S(1)}, u32[]{:S(2)}, u32[]{:S(2)}) collective-permute-start(bf16[8,4096]{1,0:T(8,128)(2,1)S(1)} %get-tuple-element.35.refs_3_), channel_id=1, source_target_pairs={{0,1},{1,0},{2,3},{3,2},{4,5},{5,4},{6,7},{7,6},{8,9},{9,8},{10,11... | collective-permute-start | bytes 196616 | tf_op jit(solution)/shard_map/ppermute | solution.py:412
  15.5 11.7 %collective-permute-start.10 = (bf16[64,9216]{1,0:T(8,128)(2,1)S(1)}, bf16[64,9216]{1,0:T(8,128)(2,1)S(1)}, u32[]{:S(2)}, u32[]{:S(2)}) collective-permute-start(bf16[64,9216]{1,0:T(8,128)(2,1)S(1)} %get-tuple-element.49.refs_0_), channel_id=1, source_target_pairs={{0,4},{4,0},{8,12},{12,8},{16,20},{20,16},{24,28},{28,24},{1,5},{5... | collective-permute-start | bytes 3538952 | tf_op jit(solution)/shard_map/ppermute | solution.py:422
  15.5 6.1 %collective-permute-start.3 = (bf16[16,4096]{1,0:T(8,128)(2,1)S(1)}, bf16[16,4096]{1,0:T(8,128)(2,1)S(1)}, u32[]{:S(2)}, u32[]{:S(2)}) collective-permute-start(bf16[16,4096]{1,0:T(8,128)(2,1)S(1)} %get-tuple-element.36), channel_id=1, source_target_pairs={{0,8},{4,20},{8,0},{12,28},{16,24},{20,4},{24,16},{28,12},{1,9},{5... | collective-permute-start | bytes 393224 | tf_op jit(solution)/shard_map/ppermute | solution.py:418
  16.1 6.4 %collective-permute-start.4 = (bf16[16,4096]{1,0:T(8,128)(2,1)S(1)}, bf16[16,4096]{1,0:T(8,128)(2,1)S(1)}, u32[]{:S(2)}, u32[]{:S(2)}) collective-permute-start(bf16[16,4096]{1,0:T(8,128)(2,1)S(1)} %get-tuple-element.36), channel_id=1, source_target_pairs={{0,16},{4,12},{8,24},{12,4},{16,0},{20,28},{24,8},{28,20},{1,17},{... | collective-permute-start | bytes 393224 | tf_op jit(solution)/shard_map/ppermute | solution.py:418
  16.6 5.9 %collective-permute-start.7 = (bf16[32,2048]{1,0:T(8,128)(2,1)S(1)}, bf16[32,2048]{1,0:T(8,128)(2,1)S(1)}, u32[]{:S(2)}, u32[]{:S(2)}) collective-permute-start(bf16[32,2048]{1,0:T(8,128)(2,1)S(1)} %get-tuple-element.39), channel_id=1, source_target_pairs={{0,1},{1,0},{2,3},{3,2},{4,5},{5,4},{6,7},{7,6},{8,9},{9,8},{10,11... | collective-permute-start | bytes 393224 | tf_op jit(solution)/shard_map/ppermute | solution.py:420
  17.6 10.0 %collective-permute-start.9 = (bf16[16,9216]{1,0:T(8,128)(2,1)S(1)}, bf16[16,9216]{1,0:T(8,128)(2,1)S(1)}, u32[]{:S(2)}, u32[]{:S(2)}) collective-permute-start(bf16[16,9216]{1,0:T(8,128)(2,1)S(1)} %collective-permute-done.6.refs_2_), channel_id=1, source_target_pairs={{0,8},{4,20},{8,0},{12,28},{16,24},{20,4},{24,16},{28,12},{1,9},{5... | collective-permute-start | bytes 884744 | tf_op jit(solution)/shard_map/ppermute | solution.py:421
  22.5 1.8 %collective-permute-start.11 = (bf16[32,2048]{1,0:T(8,128)(2,1)S(1)}, bf16[32,2048]{1,0:T(8,128)(2,1)S(1)}, u32[]{:S(2)}, u32[]{:S(2)}) collective-permute-start(bf16[32,2048]{1,0:T(8,128)(2,1)S(1)} %collective-permute-done.7.refs_0_), channel_id=1, source_target_pairs={{0,4},{4,0},{8,12},{12,8},{16,20},{20,16},{24,28},{28,24},{1,5},{5... | collective-permute-start | bytes 393224 | tf_op jit(solution)/shard_map/ppermute | solution.py:428
  22.6 5.7 %collective-permute-start.8 = (bf16[16,6144]{1,0:T(8,128)(2,1)S(1)}, bf16[16,6144]{1,0:T(8,128)(2,1)S(1)}, u32[]{:S(2)}, u32[]{:S(2)}) collective-permute-start(bf16[16,6144]{1,0:T(8,128)(2,1)S(1)} %get-tuple-element.48.refs_4_), channel_id=1, source_target_pairs={{0,16},{4,12},{8,24},{12,4},{16,0},{20,28},{24,8},{28,20},{1,17},{... | collective-permute-start | bytes 589832 | tf_op jit(solution)/shard_map/ppermute | solution.py:427
  23.5 3.6 %collective-permute-start.12 = (bf16[16,4096]{1,0:T(8,128)(2,1)S(1)}, bf16[16,4096]{1,0:T(8,128)(2,1)S(1)}, u32[]{:S(2)}, u32[]{:S(2)}) collective-permute-start(bf16[16,4096]{1,0:T(8,128)(2,1)S(1)} %collective-permute-done.3.refs_1_), channel_id=1, source_target_pairs={{0,4},{4,0},{8,12},{12,8},{16,20},{20,16},{24,28},{28,24},{1,5},{5... | collective-permute-start | bytes 393224 | tf_op jit(solution)/shard_map/ppermute | solution.py:428
  24.3 2.9 %collective-permute-start.13 = (bf16[16,4096]{1,0:T(8,128)(2,1)S(1)}, bf16[16,4096]{1,0:T(8,128)(2,1)S(1)}, u32[]{:S(2)}, u32[]{:S(2)}) collective-permute-start(bf16[16,4096]{1,0:T(8,128)(2,1)S(1)} %collective-permute-done.4.refs_2_), channel_id=1, source_target_pairs={{0,4},{4,0},{8,12},{12,8},{16,20},{20,16},{24,28},{28,24},{1,5},{5... | collective-permute-start | bytes 393224 | tf_op jit(solution)/shard_map/ppermute | solution.py:428
  28.3 1.9 %collective-permute-start.14 = (bf16[16,9216]{1,0:T(8,128)(2,1)S(1)}, bf16[16,9216]{1,0:T(8,128)(2,1)S(1)}, u32[]{:S(2)}, u32[]{:S(2)}) collective-permute-start(bf16[16,9216]{1,0:T(8,128)(2,1)S(1)} %collective-permute-done.9.refs_2_), channel_id=1, source_target_pairs={{0,4},{4,0},{8,12},{12,8},{16,20},{20,16},{24,28},{28,24},{1,5},{5... | collective-permute-start | bytes 884744 | tf_op jit(solution)/shard_map/ppermute | solution.py:436
  28.3 1.9 %collective-permute-start.15 = (bf16[16,6144]{1,0:T(8,128)(2,1)S(1)}, bf16[16,6144]{1,0:T(8,128)(2,1)S(1)}, u32[]{:S(2)}, u32[]{:S(2)}) collective-permute-start(bf16[16,6144]{1,0:T(8,128)(2,1)S(1)} %collective-permute-done.8.refs_6_), channel_id=1, source_target_pairs={{0,4},{4,0},{8,12},{12,8},{16,20},{20,16},{24,28},{28,24},{1,5},{5... | collective-permute-start | bytes 589832 | tf_op jit(solution)/shard_map/ppermute | solution.py:436
